TPU v7x, 32 devices: a whole 2x2x4 slice. The times are simulated.
32 devices in a mesh: dp: 8 (over z, core), seq: 4 (over y, x).
Axes of the slice: x: 2, y: 2, z: 4, core: 2. Of those that a mesh axis runs over, the one named last changes fastest.
Arguments:
- inputs: bfloat16 [8, 1024, 1024], P('dp', 'seq'), may hold values from -6 to 6
- cotangent: bfloat16 [8, 1024, 1024], P('dp', 'seq'), may hold values from -6 to 6
- first_gain: float32 [1024], P('dp'), may hold values from 0.25 to 1.75
- w_qkv: bfloat16 [1024, 2048], P('dp'), may hold values from -0.1875 to 0.1875
- qk_gain: float32 [128], P('dp'), may hold values from 0.5 to 1.5, as said below
- w_out: bfloat16 [1024, 1024], P('dp'), may hold values from -1.5 to 1.5
- second_gain: float32 [1024], P('dp'), may hold values from 0.25 to 1.75
- w_gate: bfloat16 [1024, 4608], P('dp'), may hold values from -0.1875 to 0.1875
- w_up: bfloat16 [1024, 4608], P('dp'), may hold values from -0.1875 to 0.1875
- w_down: bfloat16 [4608, 1024], P('dp'), may hold values from -0.09375 to 0.09375
Outputs:
- outputs: bfloat16 [8, 1024, 1024], P('dp', 'seq')
- grad_inputs: float32 [8, 1024, 1024], P('dp', 'seq')
- grad_first_gain: float32 [1024], P('dp')
- grad_qkv: float32 [1024, 2048], P('dp')
- grad_qk_gain: float32 [128], P('dp')
- grad_out: float32 [1024, 1024], P('dp')
- grad_second_gain: float32 [1024], P('dp')
- grad_gate: float32 [1024, 4608], P('dp')
- grad_up: float32 [1024, 4608], P('dp')
- grad_down: float32 [4608, 1024], P('dp')
Inputs may be any that keep to these rules, and one draw needn't show every extreme that they name: `qk_gain`: 64 query norm gains, then 64 key norm gains.
All inputs are finite; a program needn't handle non-finite values.
Results may differ from a plain program's by a relative error of at most 0.039.
Values may be sent and summed in bfloat16 or wider, within the bound.
A program may use at most 256 MiB of HBM per device.

v0:
```python
import jax
import jax.numpy as jnp
from jax import lax
from jax.sharding import PartitionSpec as P

H = 16
KV = 8
HD = 64


EPSILON = 1e-06
THETA_BASE = 1000000.0
NEG_FILL = -1e30


def norm_scale(vector):
    return lax.rsqrt(jnp.mean(vector * vector, axis=-1, keepdims=True) + EPSILON)


def norm_back(vector, scale, weighted):
    return scale * weighted - vector * scale**3 * jnp.mean(
        weighted * vector, axis=-1, keepdims=True
    )


def rotate(vector):
    middle = vector.shape[-1] // 2
    return jnp.concatenate([-vector[..., middle:], vector[..., :middle]], axis=-1)


def rotate_back(vector):
    middle = vector.shape[-1] // 2
    return jnp.concatenate([vector[..., middle:], -vector[..., :middle]], axis=-1)


def rope_tables(positions):
    inverse = THETA_BASE ** (-jnp.arange(0, HD, 2).astype(jnp.float32) / HD)
    angles = positions.astype(jnp.float32)[:, None] * inverse[None, :]
    angles = jnp.concatenate([angles, angles], axis=-1)
    return (jnp.cos(angles), jnp.sin(angles))


def masked_scores(query_block, key_heads, start_row):
    block_rows = query_block.shape[0]
    length = key_heads.shape[0]
    scores = jnp.einsum(
        "rkgd,lkd->kgrl", query_block, key_heads, preferred_element_type=jnp.float32
    ) * HD ** (-0.5)
    allowed = (start_row + jnp.arange(block_rows))[:, None] >= jnp.arange(length)[None, :]
    return jnp.where(allowed, scores, NEG_FILL)


def split_heads(queries, key_value):
    length = queries.shape[0]
    key_count = key_value.shape[1] // (2 * HD)
    per_group = queries.shape[1] // HD // key_count
    block_rows = min(512, length)
    blocks = length // block_rows
    key_heads = key_value[:, : key_count * HD].reshape(length, key_count, HD)
    value_heads = key_value[:, key_count * HD :].reshape(length, key_count, HD)
    query_blocks = queries.reshape(blocks, block_rows, key_count, per_group, HD)
    starts = jnp.arange(blocks) * block_rows
    return (key_heads, value_heads, query_blocks, starts)


def attend_forward(queries, key_value):
    key_heads, value_heads, query_blocks, starts = split_heads(queries, key_value)

    def one_block(block_item):
        query_block, start_row = block_item
        scores = masked_scores(query_block, key_heads, start_row)
        row_top = jnp.max(scores, axis=-1, keepdims=True)
        log_total = row_top + jnp.log(jnp.sum(jnp.exp(scores - row_top), axis=-1, keepdims=True))
        weights = jnp.exp(scores - log_total).astype(jnp.bfloat16)
        mixture = jnp.einsum(
            "kgrl,lkd->rkgd", weights, value_heads, preferred_element_type=jnp.float32
        )
        return (mixture.astype(jnp.bfloat16), log_total[..., 0])

    mixture, log_total = lax.map(one_block, (query_blocks, starts))
    return (mixture.reshape(queries.shape), log_total)


def attend_backward(queries, key_value, grad_mixed, log_total):
    key_heads, value_heads, query_blocks, starts = split_heads(queries, key_value)
    grad_blocks = grad_mixed.reshape(query_blocks.shape)

    def one_block(running, block_item):
        grad_keys, grad_values = running
        query_block, grad_block, total_block, start_row = block_item
        scores = masked_scores(query_block, key_heads, start_row)
        probability = jnp.exp(scores - total_block[..., None])
        weights = probability.astype(jnp.bfloat16)
        grad_values = grad_values + jnp.einsum(
            "kgrl,rkgd->lkd", weights, grad_block, preferred_element_type=jnp.float32
        )
        grad_probs = jnp.einsum(
            "rkgd,lkd->kgrl", grad_block, value_heads, preferred_element_type=jnp.float32
        )
        centre = jnp.sum(probability * grad_probs, axis=-1, keepdims=True)
        grad_scores = (probability * (grad_probs - centre) * HD ** (-0.5)).astype(jnp.bfloat16)
        grad_query = jnp.einsum(
            "kgrl,lkd->rkgd", grad_scores, key_heads, preferred_element_type=jnp.float32
        )
        grad_keys = grad_keys + jnp.einsum(
            "kgrl,rkgd->lkd", grad_scores, query_block, preferred_element_type=jnp.float32
        )
        return ((grad_keys, grad_values), grad_query.astype(jnp.bfloat16))

    zero_init = jnp.zeros(key_heads.shape, jnp.float32)
    (grad_keys, grad_values), grad_query = lax.scan(
        one_block, (zero_init, zero_init), (query_blocks, grad_blocks, log_total, starts)
    )
    length = queries.shape[0]
    grad_pair = jnp.concatenate(
        [grad_keys.reshape(length, -1), grad_values.reshape(length, -1)], axis=-1
    ).astype(jnp.bfloat16)
    return (grad_query.reshape(queries.shape), grad_pair)


def shards(inputs, cotangent, first_gain, w_qkv, qk_gain, w_out, second_gain, w_gate, w_up, w_down):
    seq_count, tok_count, model_width = inputs.shape
    groups = lax.axis_size("seq")
    row_total = seq_count * tok_count
    query_width = H * HD
    key_width = KV * HD
    gain_in, weight_qkv, gain_qk, weight_out = (
        lax.all_gather(first_gain.astype(jnp.bfloat16), "dp", axis=0, tiled=True).astype(
            first_gain.dtype
        ),
        lax.all_gather(w_qkv, "dp", axis=0, tiled=True),
        lax.all_gather(qk_gain.astype(jnp.bfloat16), "dp", axis=0, tiled=True).astype(
            qk_gain.dtype
        ),
        lax.all_gather(w_out, "dp", axis=0, tiled=True),
    )
    stream = inputs.reshape(row_total, model_width).astype(jnp.float32)
    scale_in = norm_scale(stream)
    normed_in = (stream * scale_in * gain_in).astype(jnp.bfloat16)
    projected = jnp.dot(normed_in, weight_qkv, preferred_element_type=jnp.float32)
    positions = lax.axis_index("seq") * tok_count + jnp.arange(row_total) % tok_count
    cosine_table, sine_table = rope_tables(positions)
    queries = projected[:, :query_width].reshape(row_total, H, HD)
    key_raw = projected[:, query_width : query_width + key_width].reshape(row_total, KV, HD)
    scale_query = norm_scale(queries)
    scale_key = norm_scale(key_raw)
    query_normed = queries * scale_query * gain_qk[:HD]
    key_normed = key_raw * scale_key * gain_qk[HD:]
    query_rot = (
        query_normed * cosine_table[:, None, :] + rotate(query_normed) * sine_table[:, None, :]
    ).astype(jnp.bfloat16)
    key_rot = (
        key_normed * cosine_table[:, None, :] + rotate(key_normed) * sine_table[:, None, :]
    ).astype(jnp.bfloat16)
    value_rows = projected[:, query_width + key_width :].astype(jnp.bfloat16)
    query_cube = query_rot.reshape(seq_count, tok_count, groups, query_width // groups)
    pair_cube = jnp.concatenate(
        [
            key_rot.reshape(seq_count, tok_count, groups, key_width // groups),
            value_rows.reshape(seq_count, tok_count, groups, key_width // groups),
        ],
        axis=-1,
    )
    query_items = lax.all_to_all(query_cube, "seq", split_axis=2, concat_axis=1, tiled=True)
    pair_items = lax.all_to_all(pair_cube, "seq", split_axis=2, concat_axis=1, tiled=True)

    def one_sequence(item_pair):
        query_seq, pair_seq = item_pair
        mixture, log_total = attend_forward(query_seq[:, 0, :], pair_seq[:, 0, :])
        return (mixture[:, None, :], log_total)

    mixture, log_total = lax.map(one_sequence, (query_items, pair_items))
    mixed_rows = lax.all_to_all(mixture, "seq", split_axis=1, concat_axis=2, tiled=True).reshape(
        row_total, query_width
    )
    residual = stream + jnp.dot(mixed_rows, weight_out, preferred_element_type=jnp.float32)
    gain_mid, weight_gate, weight_up, weight_down = (
        lax.all_gather(second_gain.astype(jnp.bfloat16), "dp", axis=0, tiled=True).astype(
            second_gain.dtype
        ),
        lax.all_gather(w_gate, "dp", axis=0, tiled=True),
        lax.all_gather(w_up, "dp", axis=0, tiled=True),
        lax.all_gather(w_down, "dp", axis=0, tiled=True),
    )
    scale_mid = norm_scale(residual)
    normed_mid = (residual * scale_mid * gain_mid).astype(jnp.bfloat16)
    gate_pre = jnp.dot(normed_mid, weight_gate, preferred_element_type=jnp.float32)
    up_pre = jnp.dot(normed_mid, weight_up, preferred_element_type=jnp.float32)
    gate_sig = jax.nn.sigmoid(gate_pre)
    hidden_act = (gate_pre * gate_sig * up_pre).astype(jnp.bfloat16)
    outputs = (
        residual + jnp.dot(hidden_act, weight_down, preferred_element_type=jnp.float32)
    ).astype(jnp.bfloat16)
    upstream = cotangent.reshape(row_total, model_width)
    grad_down_full = jnp.einsum(
        "ri,rj->ij", hidden_act, upstream, preferred_element_type=jnp.float32
    )
    grad_hidden = jnp.dot(upstream, weight_down.T, preferred_element_type=jnp.float32)
    grad_gate_pre = (grad_hidden * up_pre * gate_sig * (1.0 + gate_pre * (1.0 - gate_sig))).astype(
        jnp.bfloat16
    )
    grad_up_pre = (grad_hidden * gate_pre * gate_sig).astype(jnp.bfloat16)
    grad_gate_full = jnp.einsum(
        "ri,rj->ij", normed_mid, grad_gate_pre, preferred_element_type=jnp.float32
    )
    grad_up_full = jnp.einsum(
        "ri,rj->ij", normed_mid, grad_up_pre, preferred_element_type=jnp.float32
    )
    grad_normed_mid = jnp.dot(
        grad_gate_pre, weight_gate.T, preferred_element_type=jnp.float32
    ) + jnp.dot(grad_up_pre, weight_up.T, preferred_element_type=jnp.float32)
    grad_second = jnp.sum(grad_normed_mid * residual * scale_mid, axis=0)
    grad_residual = upstream.astype(jnp.float32) + norm_back(
        residual, scale_mid, grad_normed_mid * gain_mid
    )
    ffn_shards = (
        lax.psum_scatter(
            grad_second.astype(jnp.bfloat16), "dp", scatter_dimension=0, tiled=True
        ).astype(jnp.float32),
        lax.psum_scatter(
            grad_gate_full.astype(jnp.bfloat16), "dp", scatter_dimension=0, tiled=True
        ).astype(jnp.float32),
        lax.psum_scatter(
            grad_up_full.astype(jnp.bfloat16), "dp", scatter_dimension=0, tiled=True
        ).astype(jnp.float32),
        lax.psum_scatter(
            grad_down_full.astype(jnp.bfloat16), "dp", scatter_dimension=0, tiled=True
        ).astype(jnp.float32),
    )
    residual_back = grad_residual.astype(jnp.bfloat16)
    grad_out_full = jnp.einsum(
        "ri,rj->ij", mixed_rows, residual_back, preferred_element_type=jnp.float32
    )
    grad_mixed = jnp.dot(residual_back, weight_out.T, preferred_element_type=jnp.float32).astype(
        jnp.bfloat16
    )
    grad_cube = grad_mixed.reshape(seq_count, tok_count, groups, query_width // groups)
    grad_heads = lax.all_to_all(grad_cube, "seq", split_axis=2, concat_axis=1, tiled=True)

    def back_sequence(item_set):
        query_seq, pair_seq, grad_seq, total_seq = item_set
        grad_query, grad_pair = attend_backward(
            query_seq[:, 0, :], pair_seq[:, 0, :], grad_seq[:, 0, :], total_seq
        )
        return (grad_query[:, None, :], grad_pair[:, None, :])

    grad_query_heads, grad_pair_heads = lax.map(
        back_sequence, (query_items, pair_items, grad_heads, log_total)
    )
    grad_query_cube, grad_pair_cube = (
        lax.all_to_all(grad_query_heads, "seq", split_axis=1, concat_axis=2, tiled=True),
        lax.all_to_all(grad_pair_heads, "seq", split_axis=1, concat_axis=2, tiled=True),
    )
    half_pair = grad_pair_cube.shape[-1] // 2
    grad_query_rot = grad_query_cube.reshape(row_total, H, HD).astype(jnp.float32)
    grad_key_rot = grad_pair_cube[..., :half_pair].reshape(row_total, KV, HD).astype(jnp.float32)
    grad_value_rows = grad_pair_cube[..., half_pair:].reshape(row_total, key_width)
    grad_query_normed = grad_query_rot * cosine_table[:, None, :] + rotate_back(
        grad_query_rot * sine_table[:, None, :]
    )
    grad_key_normed = grad_key_rot * cosine_table[:, None, :] + rotate_back(
        grad_key_rot * sine_table[:, None, :]
    )
    grad_qk_full = jnp.concatenate(
        [
            jnp.sum(grad_query_normed * queries * scale_query, axis=(0, 1)),
            jnp.sum(grad_key_normed * key_raw * scale_key, axis=(0, 1)),
        ]
    )
    grad_query_lin = norm_back(queries, scale_query, grad_query_normed * gain_qk[:HD])
    grad_key_lin = norm_back(key_raw, scale_key, grad_key_normed * gain_qk[HD:])
    grad_projected = jnp.concatenate(
        [
            grad_query_lin.reshape(row_total, query_width).astype(jnp.bfloat16),
            grad_key_lin.reshape(row_total, key_width).astype(jnp.bfloat16),
            grad_value_rows,
        ],
        axis=-1,
    )
    grad_qkv_full = jnp.einsum(
        "ri,rj->ij", normed_in, grad_projected, preferred_element_type=jnp.float32
    )
    grad_normed_in = jnp.dot(grad_projected, weight_qkv.T, preferred_element_type=jnp.float32)
    grad_first = jnp.sum(grad_normed_in * stream * scale_in, axis=0)
    grad_stream = grad_residual + norm_back(stream, scale_in, grad_normed_in * gain_in)
    attn_shards = (
        lax.psum_scatter(
            grad_first.astype(jnp.bfloat16), "dp", scatter_dimension=0, tiled=True
        ).astype(jnp.float32),
        lax.psum_scatter(
            grad_qkv_full.astype(jnp.bfloat16), "dp", scatter_dimension=0, tiled=True
        ).astype(jnp.float32),
        lax.psum_scatter(
            grad_qk_full.astype(jnp.bfloat16), "dp", scatter_dimension=0, tiled=True
        ).astype(jnp.float32),
        lax.psum_scatter(
            grad_out_full.astype(jnp.bfloat16), "dp", scatter_dimension=0, tiled=True
        ).astype(jnp.float32),
    )
    finals = (
        lax.psum(attn_shards[0].astype(jnp.bfloat16), "seq").astype(jnp.float32),
        lax.psum(attn_shards[1].astype(jnp.bfloat16), "seq").astype(jnp.float32),
        lax.psum(attn_shards[2].astype(jnp.bfloat16), "seq").astype(jnp.float32),
        lax.psum(attn_shards[3].astype(jnp.bfloat16), "seq").astype(jnp.float32),
        lax.psum(ffn_shards[0].astype(jnp.bfloat16), "seq").astype(jnp.float32),
        lax.psum(ffn_shards[1].astype(jnp.bfloat16), "seq").astype(jnp.float32),
        lax.psum(ffn_shards[2].astype(jnp.bfloat16), "seq").astype(jnp.float32),
        lax.psum(ffn_shards[3].astype(jnp.bfloat16), "seq").astype(jnp.float32),
    )
    return (
        outputs.reshape(seq_count, tok_count, model_width),
        grad_stream.reshape(seq_count, tok_count, model_width),
        finals[0],
        finals[1],
        finals[2],
        finals[3],
        finals[4],
        finals[5],
        finals[6],
        finals[7],
    )


def solution(mesh):
    in_specs = (
        P("dp", "seq", None),
        P("dp", "seq", None),
        P("dp"),
        P("dp", None),
        P("dp"),
        P("dp", None),
        P("dp"),
        P("dp", None),
        P("dp", None),
        P("dp", None),
    )
    out_specs = (
        P("dp", "seq", None),
        P("dp", "seq", None),
        P("dp"),
        P("dp", None),
        P("dp"),
        P("dp", None),
        P("dp"),
        P("dp", None),
        P("dp", None),
        P("dp", None),
    )
    return jax.shard_map(shards, mesh=mesh, in_specs=in_specs, out_specs=out_specs, check_vma=False)
```

profile of v0, /device:TPU:30, one launch (start us, length us, event | category | flops | bytes accessed | tf_op | source)
XLA Modules:
  0.0 1080.0 jit_solution(14251357177326647332)
XLA Ops:
  11.2 7.7 all-gather
  21.9 13.8 %all-reduce = bf16[128]{0:T(256)(128)(2,1)S(1)} all-reduce(bf16[128]{0:T(256)(128)(2,1)S(1)} %dynamic-update-slice), channel_id=1, replica_groups=mesh['dp'=8,'seq'=4] {'dp'}, use_global_device_ids=true, to_apply=%add | all-reduce | flops 128 | bytes 512
  38.0 17.8 %all-gather.8.cloned.1.call-done = bf16[1024,2048]{1,0:T(8,128)(2,1)} async-done(((bf16[128,2048]{1,0:T(8,128)(2,1)}), bf16[1024,2048]{1,0:T(8,128)(2,1)}) %all-gather.8.cloned.1.call-update) | async-done | bytes 4194320 | tf_op jit(solution)/shard_map/all_gather | solution.py:131
  55.8 3.7 fusion.97
  64.0 4.2 all-to-all-start.1
  72.4 2.7 all-to-all-done.1
  75.1 5.2 all-to-all-start
  80.9 5.6 all-to-all-done
  87.4 16.0 %while.46 = (s32[]{:T(128)}, bf16[2,512,2,2,64]{1,4,3,2,0:T(8,128)(2,1)S(1)}, f32[2,2,2,512]{3,2,1,0:T(2,128)S(1)}, s32[2]{0:T(128)S(1)}, bf16[2,512,2,2,64]{1,4...) while((s32[]{:T(128)}, ...), condition=%wide.region_6.7_spmd, body=%wide.region_3.6_spmd.sunk | while | flops 560593408 | bytes 28381296 | solution.py:80
  105.4 4.2 reshape.505
  110.1 3.8 reduce.4
  114.8 4.9 all-to-all-start.2
  119.8 11.4 %all-gather.1 = bf16[8,1,128]{2,1,0:T(2,128)(2,1)S(1)} all-gather(bf16[1,1,128]{2,1,0:T(2,128)(2,1)S(1)} %convert_bitcast_fusion.1), channel_id=1, replica_groups=mesh['dp'=8,'seq'=4] {'dp'}, dimensions={0}, use_global_device_ids=true | all-gather | bytes 2304 | tf_op jit(solution)/shard_map/all_gather | solution.py:178
  133.9 2.6 multiply_reduce_fusion.4
  136.8 40.0 %all-gather.12.cloned.1.call-done = bf16[1024,4608]{1,0:T(8,128)(2,1)} async-done(((bf16[128,4608]{1,0:T(8,128)(2,1)}), bf16[1024,4608]{1,0:T(8,128)(2,1)}) %all-gather.12.cloned.1.call-update) | async-done | bytes 9437200 | tf_op jit(solution)/shard_map/all_gather | solution.py:181
  176.8 7.9 fusion.110
  184.7 82.8 %all-gather.14.cloned.1.call-done = bf16[1024,4608]{1,0:T(8,128)(2,1)} async-done(((bf16[128,4608]{1,0:T(8,128)(2,1)}), bf16[1024,4608]{1,0:T(8,128)(2,1)}) %all-gather.14.cloned.1.call-update) | async-done | bytes 9437200 | tf_op jit(solution)/shard_map/all_gather | solution.py:182
  267.5 7.9 fusion.111
  275.4 82.8 %all-gather.16.cloned.1.call-done = bf16[4608,1024]{1,0:T(8,128)(2,1)} async-done(((bf16[576,1024]{1,0:T(8,128)(2,1)}), bf16[4608,1024]{1,0:T(8,128)(2,1)}) %all-gather.16.cloned.1.call-update) | async-done | bytes 9437200 | tf_op jit(solution)/shard_map/all_gather | solution.py:183
  358.2 13.6 %multiply_convert_fusion = (bf16[256,4608]{1,0:T(8,128)(2,1)S(1)}, bf16[256,4608]{1,0:T(8,128)(2,1)S(1)}, bf16[256,4608]{1,0:T(8,128)(2,1)}) fusion(f32[256,4608]{1,0:T(8,128)} %fusion.110, f32[256,4608]{1,0:T(8,128)} %fusion.111, bf16[4608,1024]{1,0:T(8,128)(2,1)} %all-gather.16.cloned.1.call-done, bf16[1,256,1024]{2,1,0:T(8,128)(2,1)S(1)} %copy-done.25), kind=kOutput, calls=%fused_computation.77 | convolution fusion | flops 2434793472 | bytes 26476544 | tf_op jit(solution)/shard_map/dot_general | solution.py:198
  371.9 6.9 fusion.112
  380.0 3.3 multiply_reduce_fusion
  387.3 4.4 all-to-all-start.3
  391.7 3.1 convolution_convert_fusion.4
  394.8 4.2 all-to-all-done.3
  401.3 2.8 squeeze.52
  406.8 105.9 %while.47 = (s32[]{:T(128)}, f32[1024,2,64]{0,2,1:T(8,128)}, f32[1024,2,64]{0,2,1:T(8,128)}, bf16[2,512,2,2,64]{1,4,3,2,0:T(8,128)(2,1)}, bf16[2,512,2,2,64]{1,4...) while((s32[]{:T(128)}, f32[1024,2,64]{0,2,1:T(8,128)}, ...), condition=%wide.region_11.12_spmd.clone, body=%wide.region_9.11_spmd.clone.sunk | while | flops 1397889536 | bytes 103871704 | solution.py:111
  406.8 4.6 fusion.165
  411.4 4.5 fusion.164
  417.6 18.0 %fusion.168 = bf16[2,512,2,2,64]{1,4,3,2,0:T(8,128)(2,1)} fusion(bf16[2,512,2,2,64]{1,4,3,2,0:T(8,128)(2,1)} %get-tuple-element.489, s32[]{:T(128)} %get-tuple-element.486, f32[2,512,2,1024]{3,1,2,0:T(8,128)} %fusion.164, f32[2,512,2,1024]{3,1,2,0:T(8,128)} %fusion.165, f32[2,2,512]{2,1,0:T(2,128)S(1)} %dynamic-slice_bitcast_fusion.2, ...), kind=kOutput, calls=%fused_computation.46.clone.1 | convolution fusion | flops 291638272 | bytes 35144192 | tf_op jit(solution)/shard_map/while/body/eval_jaxpr/while/body/eval_jaxpr/kgrl,lkd->rkgd/dot_general | solution.py:102
  435.6 18.6 %fusion.166 = f32[1024,2,64]{0,2,1:T(8,128)} fusion(f32[2,512,2,1024]{3,1,2,0:T(8,128)} %fusion.164, f32[2,512,2,1024]{3,1,2,0:T(8,128)} %fusion.165, f32[2,2,512]{2,1,0:T(2,128)S(1)} %dynamic-slice_bitcast_fusion.2, pred[512,1024]{1,0:T(8,128)(4,1)S(1)} %iota_compare_fusion.5, f32[1024,2,64]{0,2,1:T(8,128)} %get-tuple-element.487, ...), kind=kOutput, calls=%fused_computation.42.clone.1 | convolution fusion | flops 291769344 | bytes 35930624 | tf_op jit(solution)/shard_map/while/body/eval_jaxpr/while/body/eval_jaxpr/kgrl,rkgd->lkd/dot_general | solution.py:105
  454.2 5.6 fusion.167
  459.8 4.6 fusion.165
  464.3 4.5 fusion.164
  470.6 17.8 %fusion.168 = bf16[2,512,2,2,64]{1,4,3,2,0:T(8,128)(2,1)} fusion(bf16[2,512,2,2,64]{1,4,3,2,0:T(8,128)(2,1)} %get-tuple-element.489, s32[]{:T(128)} %get-tuple-element.486, f32[2,512,2,1024]{3,1,2,0:T(8,128)} %fusion.164, f32[2,512,2,1024]{3,1,2,0:T(8,128)} %fusion.165, f32[2,2,512]{2,1,0:T(2,128)S(1)} %dynamic-slice_bitcast_fusion.2, ...), kind=kOutput, calls=%fused_computation.46.clone.1 | convolution fusion | flops 291638272 | bytes 35144192 | tf_op jit(solution)/shard_map/while/body/eval_jaxpr/while/body/eval_jaxpr/kgrl,lkd->rkgd/dot_general | solution.py:102
  488.4 18.6 %fusion.166 = f32[1024,2,64]{0,2,1:T(8,128)} fusion(f32[2,512,2,1024]{3,1,2,0:T(8,128)} %fusion.164, f32[2,512,2,1024]{3,1,2,0:T(8,128)} %fusion.165, f32[2,2,512]{2,1,0:T(2,128)S(1)} %dynamic-slice_bitcast_fusion.2, pred[512,1024]{1,0:T(8,128)(4,1)S(1)} %iota_compare_fusion.5, f32[1024,2,64]{0,2,1:T(8,128)} %get-tuple-element.487, ...), kind=kOutput, calls=%fused_computation.42.clone.1 | convolution fusion | flops 291769344 | bytes 35930624 | tf_op jit(solution)/shard_map/while/body/eval_jaxpr/while/body/eval_jaxpr/kgrl,rkgd->lkd/dot_general | solution.py:105
  507.0 5.7 fusion.167
  512.7 3.6 copy.186
  516.4 5.4 reshape.506
  521.7 5.6 reduce.6
  529.3 5.6 all-to-all-start.4
  537.9 3.6 copy.164
  541.4 5.6 reduce.5
  548.9 4.2 all-to-all-start.5
  562.6 2.6 reshape.515
  568.9 2.9 copy.157
  571.9 3.5 reshape.513
  593.2 4.1 multiply_reduce_fusion.1
  598.0 3.4 convolution_convert_fusion.3
  601.5 6.7 convolution_convert_fusion.2
  608.3 7.2 convolution_convert_fusion.1
  615.6 6.8 convolution_convert_fusion
  622.7 26.9 %reduce-scatter.6.cloned.1.call-done = bf16[128,2048]{1,0:T(8,128)(2,1)} async-done(((bf16[1024,2048]{1,0:T(8,128)(2,1)}), bf16[128,2048]{1,0:T(8,128)(2,1)}) %reduce-scatter.6.cloned.1.call-update) | async-done | bytes 524304 | tf_op jit(solution)/shard_map/reduce_scatter | solution.py:290
  649.6 100.7 %reduce-scatter.10.cloned.1.call-done = bf16[128,4608]{1,0:T(8,128)(2,1)} async-done(((bf16[1024,4608]{1,0:T(8,128)(2,1)}), bf16[128,4608]{1,0:T(8,128)(2,1)}) %reduce-scatter.10.cloned.1.call-update) | async-done | bytes 1179664 | tf_op jit(solution)/shard_map/reduce_scatter | solution.py:220
  750.3 100.2 %reduce-scatter.12.cloned.1.call-done = bf16[128,4608]{1,0:T(8,128)(2,1)} async-done(((bf16[1024,4608]{1,0:T(8,128)(2,1)}), bf16[128,4608]{1,0:T(8,128)(2,1)}) %reduce-scatter.12.cloned.1.call-update) | async-done | bytes 1179664 | tf_op jit(solution)/shard_map/reduce_scatter | solution.py:223
  850.6 100.0 %reduce-scatter.14.cloned.1.call-done = bf16[576,1024]{1,0:T(8,128)(2,1)} async-done(((bf16[4608,1024]{1,0:T(8,128)(2,1)}), bf16[576,1024]{1,0:T(8,128)(2,1)}) %reduce-scatter.14.cloned.1.call-update) | async-done | bytes 1179664 | tf_op jit(solution)/shard_map/reduce_scatter | solution.py:226
  951.9 7.8 fusion.77
  960.1 4.6 fusion.87
  964.6 11.9 %all-reduce.4 = (bf16[1024]{0:T(1024)(128)(2,1)S(1)}, bf16[128]{0:T(256)(128)(2,1)S(1)}, bf16[1024]{0:T(1024)(128)(2,1)S(1)}) all-reduce(bf16[1024]{0:T(1024)(128)(2,1)S(1)} %get-tuple-element.246, bf16[128]{0:T(256)(128)(2,1)S(1)} %pad_maximum_fusion.7, bf16[1024]{0:T(1024)(128)(2,1)S(1)} %copy-done.48), channel_id=2, replica_groups=mesh['dp'=8,'seq'=4] {'dp'}, use_global_device_ids=true, to_apply=%region_16.17.clone | all-reduce | flops 2176 | bytes 8704
  976.8 8.2 all-reduce.5
  987.8 74.7 %all-reduce.9.cloned.1.call-done = (bf16[128,2048]{1,0:T(8,128)(2,1)}, bf16[128,1024]{1,0:T(8,128)(2,1)}, bf16[128,4608]{1,0:T(8,128)(2,1)}, bf16[128,4608]{1,0:T(8,128)(2,1)}, bf16[576,1024]{1,0:T(8,128)(2,1)}) async-done(((bf16[128,2048]{1,0:T(8,128)(2,1)}, bf16[128,1024]{1,0:T(8,128)(2,1)}, bf16[128,4608]{1,0:T(8,128)(2,1)}, bf16[128,4608]{1,0:T(8,128)(2,1)}, bf16[576,1024]{1,0:T(8,128)(2,1)}), ...) | async-done | bytes 4325392 | tf_op jit(solution)/shard_map/psum | solution.py:302
  1062.5 3.0 convert_element_type.261
  1065.5 2.9 convert_element_type.263
  1068.4 3.0 convert_element_type.265
  (279 shorter events, 98.4 us)
Async XLA Ops:
  7.2 48.6 %all-gather.8.cloned.1.call-start = ((), (), s32[]{:S(2)}) async-start(), calls=%async_computation.11 | async-start | bytes 4718592 | tf_op jit(solution)/shard_map/all_gather | solution.py:131
  7.9 126.0 %all-gather.10.cloned.1.call-start = ((), (), s32[]{:S(2)}) async-start(), calls=%async_computation.12 | async-start | bytes 2359296 | tf_op jit(solution)/shard_map/all_gather | solution.py:135
  8.7 168.1 %all-gather.12.cloned.1.call-start = ((), (), s32[]{:S(2)}) async-start(), calls=%async_computation.13 | async-start | bytes 10616832 | tf_op jit(solution)/shard_map/all_gather | solution.py:181
  9.4 258.1 %all-gather.14.cloned.1.call-start = ((), (), s32[]{:S(2)}) async-start(), calls=%async_computation.14 | async-start | bytes 10616832 | tf_op jit(solution)/shard_map/all_gather | solution.py:182
  10.0 348.2 %all-gather.16.cloned.1.call-start = ((), (), s32[]{:S(2)}) async-start(), calls=%async_computation.15 | async-start | bytes 10616832 | tf_op jit(solution)/shard_map/all_gather | solution.py:183
  19.0 40.6 %copy-start.39 = (f32[8,1,128]{2,1,0:T(1,128)}, f32[8,1,128]{2,1,0:T(1,128)S(1)}, u32[]{:S(2)}) copy-start(f32[8,1,128]{2,1,0:T(1,128)S(1)} %convert_element_type.275) | copy-start | bytes 12292
  35.7 26.2 %copy-start.43 = (f32[64]{0:T(128)}, f32[64]{0:T(128)S(1)}, u32[]{:S(2)}) copy-start(f32[64]{0:T(128)S(1)} %get-tuple-element.332) | copy-start | bytes 772
  35.7 33.7 %copy-start.41 = (f32[64]{0:T(128)}, f32[64]{0:T(128)S(1)}, u32[]{:S(2)}) copy-start(f32[64]{0:T(128)S(1)} %get-tuple-element.333) | copy-start | bytes 772
  36.1 33.6 %copy-start.30 = (f32[256,64]{0,1:T(8,128)}, f32[256,64]{0,1:T(8,128)S(1)}, u32[]{:S(2)}) copy-start(f32[256,64]{0,1:T(8,128)S(1)} %get-tuple-element.321) | copy-start | bytes 196612
  36.1 33.9 %copy-start.28 = (f32[256,64]{0,1:T(8,128)}, f32[256,64]{0,1:T(8,128)S(1)}, u32[]{:S(2)}) copy-start(f32[256,64]{0,1:T(8,128)S(1)} %get-tuple-element.320) | copy-start | bytes 196612
  38.0 23.9 %copy-start.46 = (f32[256]{0:T(256)}, f32[256]{0:T(256)S(1)}, u32[]{:S(2)}) copy-start(f32[256]{0:T(256)S(1)} %get-tuple-element.327) | copy-start | bytes 3076
  59.5 1.3 copy-start.16
  61.1 2.9 copy-start.6
  64.0 11.1 %all-to-all-start.1 = ((bf16[1,256,4,256]{1,3,0,2:T(8,128)(2,1)}), bf16[1,256,4,256]{1,3,0,2:T(8,128)(2,1)S(1)}, u32[]{:S(2)}, u32[]{:S(2)}) async-start(bf16[1,256,4,256]{1,3,0,2:T(8,128)(2,1)} %maximum_bitcast_fusion), calls=%async_computation.1 | async-start | bytes 1048576 | tf_op jit(solution)/shard_map/all_to_all | solution.py:165
  68.5 12.1 %copy-start = (f32[256,1024]{0,1:T(8,128)}, f32[256,1024]{0,1:T(8,128)S(1)}, u32[]{:S(2)}) copy-start(f32[256,1024]{0,1:T(8,128)S(1)} %copy.181) | copy-start | bytes 3145732
  75.1 11.4 %all-to-all-start = ((bf16[1,256,4,256]{1,3,0,2:T(8,128)(2,1)}), bf16[1,256,4,256]{1,3,0,2:T(8,128)(2,1)S(1)}, u32[]{:S(2)}, u32[]{:S(2)}) async-start(bf16[1,256,4,256]{1,3,0,2:T(8,128)(2,1)} %fusion.88), calls=%async_computation | async-start | bytes 1048576 | tf_op jit(solution)/shard_map/all_to_all | solution.py:164
  87.4 32.4 %copy-start.49 = (f32[128]{0:T(128)S(1)}, f32[128]{0:T(128)}, u32[]{:S(2)}) copy-start(f32[128]{0:T(128)} %param.20) | copy-start | bytes 1540
  103.4 30.5 %copy-start.20 = (bf16[1,256,1024]{2,1,0:T(8,128)(2,1)S(1)}, bf16[1,256,1024]{2,1,0:T(8,128)(2,1)}, u32[]{:S(2)}) copy-start(bf16[1,256,1024]{2,1,0:T(8,128)(2,1)} %param.14) | copy-start | bytes 1572868
  114.8 16.4 %all-to-all-start.2 = ((bf16[4,2,32768]{2,1,0:T(2,128)(2,1)}), bf16[4,2,32768]{2,1,0:T(2,128)(2,1)S(1)}, u32[]{:S(2)}, u32[]{:S(2)}) async-start(bf16[4,2,32768]{2,1,0:T(2,128)(2,1)} %reshape.510), calls=%async_computation.2 | async-start | bytes 1048576 | tf_op jit(solution)/shard_map/all_to_all | solution.py:173
  133.9 2.7 copy-start.17
  136.8 138.6 %copy-start.4 = (bf16[256,1024]{1,0:T(8,128)(2,1)}, bf16[256,1024]{1,0:T(8,128)(2,1)S(1)}, u32[]{:S(2)}) copy-start(bf16[256,1024]{1,0:T(8,128)(2,1)S(1)} %multiply_convert_fusion.3) | copy-start | bytes 1572868
  184.7 173.5 %copy-start.25 = (bf16[1,256,1024]{2,1,0:T(8,128)(2,1)S(1)}, bf16[1,256,1024]{2,1,0:T(8,128)(2,1)}, u32[]{:S(2)}) copy-start(bf16[1,256,1024]{2,1,0:T(8,128)(2,1)} %param.15) | copy-start | bytes 1572868
  371.8 7.0 copy-start.23
  371.8 7.0 copy-start.22
  371.8 8.1 copy-start.12
  380.0 3.4 copy-start.26
  380.0 3.7 copy-start.13
  383.7 23.1 %copy-start.2 = (f32[256,1024]{1,0:T(8,128)}, f32[256,1024]{1,0:T(8,128)S(1)}, u32[]{:S(2)}) copy-start(f32[256,1024]{1,0:T(8,128)S(1)} %subtract_add_fusion) | copy-start | bytes 3145732
  387.3 11.7 %all-to-all-start.3 = ((bf16[1,256,4,256]{1,3,0,2:T(8,128)(2,1)}), bf16[1,256,4,256]{1,3,0,2:T(8,128)(2,1)}, u32[]{:S(2)}, u32[]{:S(2)}) async-start(bf16[1,256,4,256]{1,3,0,2:T(8,128)(2,1)} %bitcast.416), calls=%async_computation.3 | async-start | bytes 1048576 | tf_op jit(solution)/shard_map/all_to_all | solution.py:238
  391.7 230.9 %reduce-scatter.8.cloned.1.call-start = ((), (), s32[]{:S(2)}) async-start(), calls=%async_computation.17 | async-start | bytes 2359296 | tf_op jit(solution)/shard_map/reduce_scatter | solution.py:296
  406.8 4.6 copy-start.14
  435.6 18.6 %copy-start.15 = (bf16[2,512,2,2,64]{1,4,3,2,0:T(8,128)(2,1)S(1)}, bf16[2,512,2,2,64]{1,4,3,2,0:T(8,128)(2,1)}, u32[]{:S(2)}) copy-start(bf16[2,512,2,2,64]{1,4,3,2,0:T(8,128)(2,1)} %get-tuple-element.506) | copy-start | bytes 1572868 | tf_op jit(solution)/shard_map/while/body/eval_jaxpr/while
  459.8 4.6 copy-start.14
  488.4 18.6 %copy-start.15 = (bf16[2,512,2,2,64]{1,4,3,2,0:T(8,128)(2,1)S(1)}, bf16[2,512,2,2,64]{1,4,3,2,0:T(8,128)(2,1)}, u32[]{:S(2)}) copy-start(bf16[2,512,2,2,64]{1,4,3,2,0:T(8,128)(2,1)} %get-tuple-element.506) | copy-start | bytes 1572868 | tf_op jit(solution)/shard_map/while/body/eval_jaxpr/while
  512.7 40.4 %copy-start.11 = (f32[256,16,64]{0,2,1:T(8,128)S(1)}, f32[256,16,64]{0,2,1:T(8,128)}, u32[]{:S(2)}) copy-start(f32[256,16,64]{0,2,1:T(8,128)} %copy-done.10) | copy-start | bytes 3145732
  512.7 41.7 %copy-start.42 = (f32[64]{0:T(128)S(1)}, f32[64]{0:T(128)}, u32[]{:S(2)}) copy-start(f32[64]{0:T(128)} %copy-done.41) | copy-start | bytes 772
  516.4 40.3 %copy-start.44 = (f32[64]{0:T(128)S(1)}, f32[64]{0:T(128)}, u32[]{:S(2)}) copy-start(f32[64]{0:T(128)} %copy-done.43) | copy-start | bytes 772
  516.4 40.4 %copy-start.9 = (f32[256,16,64]{0,2,1:T(8,128)S(1)}, f32[256,16,64]{0,2,1:T(8,128)}, u32[]{:S(2)}) copy-start(f32[256,16,64]{0,2,1:T(8,128)} %copy-done.8) | copy-start | bytes 3145732
  521.7 36.4 %copy-start.37 = (f32[256,16]{0,1:T(8,128)S(1)}, f32[256,16]{0,1:T(8,128)}, u32[]{:S(2)}) copy-start(f32[256,16]{0,1:T(8,128)} %get-tuple-element.322) | copy-start | bytes 49156
  529.3 19.7 %all-to-all-start.4 = ((bf16[4,2,32768]{2,1,0:T(2,128)(2,1)}), bf16[4,2,32768]{2,1,0:T(2,128)(2,1)}, u32[]{:S(2)}, u32[]{:S(2)}) async-start(bf16[4,2,32768]{2,1,0:T(2,128)(2,1)} %reshape.514), calls=%async_computation.4 | async-start | bytes 1048576 | tf_op jit(solution)/shard_map/all_to_all | solution.py:251
  535.9 25.6 %copy-start.38 = (f32[256,8]{0,1:T(8,128)S(1)}, f32[256,8]{0,1:T(8,128)}, u32[]{:S(2)}) copy-start(f32[256,8]{0,1:T(8,128)} %get-tuple-element.324) | copy-start | bytes 24580
  548.9 22.9 %all-to-all-start.5 = ((bf16[4,2,32768]{2,1,0:T(2,128)(2,1)}), bf16[4,2,32768]{2,1,0:T(2,128)(2,1)}, u32[]{:S(2)}, u32[]{:S(2)}) async-start(bf16[4,2,32768]{2,1,0:T(2,128)(2,1)} %reshape.512), calls=%async_computation.5 | async-start | bytes 1048576 | tf_op jit(solution)/shard_map/all_to_all | solution.py:252
  553.1 96.5 %reduce-scatter.6.cloned.1.call-start = ((), (), s32[]{:S(2)}) async-start(), calls=%async_computation.16 | async-start | bytes 4718592 | tf_op jit(solution)/shard_map/reduce_scatter | solution.py:290
  561.6 16.5 %copy-start.31 = (f32[256,64]{0,1:T(8,128)S(1)}, f32[256,64]{0,1:T(8,128)}, u32[]{:S(2)}) copy-start(f32[256,64]{0,1:T(8,128)} %copy-done.30) | copy-start | bytes 196612
  565.3 14.2 %copy-start.1 = (f32[256,1024]{0,1:T(8,128)S(1)}, f32[256,1024]{0,1:T(8,128)}, u32[]{:S(2)}) copy-start(f32[256,1024]{0,1:T(8,128)} %copy-done) | copy-start | bytes 3145732
  565.3 14.2 %copy-start.29 = (f32[256,64]{0,1:T(8,128)S(1)}, f32[256,64]{0,1:T(8,128)}, u32[]{:S(2)}) copy-start(f32[256,64]{0,1:T(8,128)} %copy-done.28) | copy-start | bytes 196612
  579.4 9.2 copy-start.7
  583.5 7.8 copy-start.24
  588.6 9.5 copy-start.21
  588.6 9.5 copy-start.40
  589.5 8.6 copy-start.47
  591.2 6.0 copy-start.36
  593.2 8.4 copy-start.5
  601.5 148.9 %reduce-scatter.10.cloned.1.call-start = ((), (), s32[]{:S(2)}) async-start(), calls=%async_computation.18 | async-start | bytes 10616832 | tf_op jit(solution)/shard_map/reduce_scatter | solution.py:220
  608.2 7.3 copy-start.27
  608.2 242.3 %reduce-scatter.12.cloned.1.call-start = ((), (), s32[]{:S(2)}) async-start(), calls=%async_computation.19 | async-start | bytes 10616832 | tf_op jit(solution)/shard_map/reduce_scatter | solution.py:223
  615.5 335.1 %reduce-scatter.14.cloned.1.call-start = ((), (), s32[]{:S(2)}) async-start(), calls=%async_computation.20 | async-start | bytes 10616832 | tf_op jit(solution)/shard_map/reduce_scatter | solution.py:226
  622.4 440.1 %all-reduce.9.cloned.1.call-start = ((), (), s32[]{:S(2)}) async-start(), calls=%async_computation.21 | async-start | bytes 8650752 | tf_op jit(solution)/shard_map/psum | solution.py:302
  951.9 8.1 copy-start.33
  959.8 4.8 copy-start.48
  959.8 26.7 %copy-start.3 = (f32[256,1024]{1,0:T(8,128)S(1)}, f32[256,1024]{1,0:T(8,128)}, u32[]{:S(2)}) copy-start(f32[256,1024]{1,0:T(8,128)} %copy-done.2) | copy-start | bytes 3145732
  959.8 26.7 %copy-start.45 = (f32[256]{0:T(256)S(1)}, f32[256]{0:T(256)}, u32[]{:S(2)}) copy-start(f32[256]{0:T(256)} %get-tuple-element.326) | copy-start | bytes 3076
  1062.5 8.9 copy-start.34
  1062.5 9.9 copy-start.35
  (5 other events, 4.8 us)
Sparse Core Ops, SparseCore 0:
  9.6 46.1 all-gather.7
  57.4 28.5 all-gather.9
  87.6 89.1 all-gather.11
  178.3 89.1 all-gather.13
  269.0 89.1 all-gather.15
  395.0 33.2 reduce-scatter.7
  601.6 47.9 reduce-scatter.5
  651.9 98.3 reduce-scatter.9
  752.7 97.8 reduce-scatter.11
  852.7 97.8 reduce-scatter.13
  954.7 107.6 all-reduce.8
where the time goes:
time: 1090 us; the launch traced here: 1080 us
  waiting for transfers between devices  642 us (59%)
  matrix products  198 us (18%)
  local copies, waits for them, and re-layouts  80.8 us (7%)
  other arithmetic  60.7 us (6%)
  blocking collectives  53 us (5%)
  starting transfers between devices  29.1 us (3%)
  between operations  16.9 us (2%)
    reduce_scatter x1, waiting for transfers between devices, shards(): lax.psum_scatter(grad_gate_full.astype(jnp.bfloat16), 'dp', scatter_dimen...  101 us
    reduce_scatter x1, waiting for transfers between devices, shards(): lax.psum_scatter(grad_up_full.astype(jnp.bfloat16), 'dp', scatter_dimensi...  100 us
    reduce_scatter x1, waiting for transfers between devices, shards(): lax.psum_scatter(grad_down_full.astype(jnp.bfloat16), 'dp', scatter_dimen...  100 us
    all_gather x1, waiting for transfers between devices, shards(): lax.all_gather(w_down, 'dp', axis=0, tiled=True)  82.8 us
    all_gather x1, waiting for transfers between devices, shards(): lax.all_gather(w_up, 'dp', axis=0, tiled=True)  82.8 us
    psum x1, waiting for transfers between devices, shards(): lax.psum(attn_shards[1].astype(jnp.bfloat16), 'seq').astype(jnp.float32)  74.7 us
    all_gather x1, waiting for transfers between devices, shards(): lax.all_gather(w_gate, 'dp', axis=0, tiled=True)  40 us
    dot_general x2, matrix products, one_block(): jnp.einsum('kgrl,rkgd->lkd', grad_scores, query_block, preferred_element_...  37.2 us
  transfers between devices with their start and end apart: 17, of which 12 were waited for; matrix products, arithmetic and copies ran while one was open for 27% of the time, Pallas kernels for 0%

commit v1 on v0

v1 whole, which is shorter than its diff:
```python
import jax
import jax.numpy as jnp
from jax import lax
from jax.sharding import PartitionSpec as P

H = 16
KV = 8
HD = 64
EPSILON = 1e-06
THETA_BASE = 1000000.0
NEG_FILL = -1e30
F32 = jnp.float32
BF16 = jnp.bfloat16


def norm_scale(vector):
    return lax.rsqrt(jnp.mean(vector * vector, axis=-1, keepdims=True) + EPSILON)


def norm_back(vector, scale, weighted):
    return scale * weighted - vector * scale**3 * jnp.mean(weighted * vector, axis=-1, keepdims=True)


def rotate(vector):
    middle = vector.shape[-1] // 2
    return jnp.concatenate([-vector[..., middle:], vector[..., :middle]], axis=-1)


def rotate_back(vector):
    middle = vector.shape[-1] // 2
    return jnp.concatenate([vector[..., middle:], -vector[..., :middle]], axis=-1)


def rope_tables(positions):
    inverse = THETA_BASE ** (-jnp.arange(0, HD, 2).astype(F32) / HD)
    angles = positions.astype(F32)[:, None] * inverse[None, :]
    angles = jnp.concatenate([angles, angles], axis=-1)
    return (jnp.cos(angles), jnp.sin(angles))


def dot(a, b):
    return jnp.dot(a, b, preferred_element_type=F32)


def scores_of(q, k):
    length = q.shape[0]
    s = jnp.einsum("rkgd,lkd->kgrl", q, k, preferred_element_type=F32) * HD**-0.5
    allowed = jnp.arange(length)[:, None] >= jnp.arange(length)[None, :]
    return jnp.where(allowed, s, NEG_FILL)


def attend_forward(q, k, v):
    s = scores_of(q, k)
    top = jnp.max(s, axis=-1, keepdims=True)
    total = top + jnp.log(jnp.sum(jnp.exp(s - top), axis=-1, keepdims=True))
    w = jnp.exp(s - total).astype(BF16)
    mix = jnp.einsum("kgrl,lkd->rkgd", w, v, preferred_element_type=F32).astype(BF16)
    return mix, total


def attend_backward(q, k, v, g, total):
    s = scores_of(q, k)
    p = jnp.exp(s - total)
    w = p.astype(BF16)
    gv = jnp.einsum("kgrl,rkgd->lkd", w, g, preferred_element_type=F32)
    gp = jnp.einsum("rkgd,lkd->kgrl", g, v, preferred_element_type=F32)
    centre = jnp.sum(p * gp, axis=-1, keepdims=True)
    gs = (p * (gp - centre) * HD**-0.5).astype(BF16)
    gq = jnp.einsum("kgrl,lkd->rkgd", gs, k, preferred_element_type=F32)
    gk = jnp.einsum("kgrl,rkgd->lkd", gs, q, preferred_element_type=F32)
    return gq.astype(BF16), gk.astype(BF16), gv.astype(BF16)


def shards(inputs, cotangent, first_gain, w_qkv, qk_gain, w_out, second_gain, w_gate, w_up, w_down):
    _, tok, width = inputs.shape
    ns, nd = lax.axis_size("seq"), lax.axis_size("dp")
    s, d = lax.axis_index("seq"), lax.axis_index("dp")
    length = ns * tok
    hq, hk = H // ns, KV // ns
    qw, kw = hq * HD, hk * HD
    rows_d = w_down.shape[0]
    ff = rows_d * nd
    piece = rows_d // ns

    mine_qkv = jnp.concatenate(
        [
            lax.dynamic_slice_in_dim(w_qkv, s * qw, qw, 1),
            lax.dynamic_slice_in_dim(w_qkv, H * HD + s * kw, kw, 1),
            lax.dynamic_slice_in_dim(w_qkv, (H + KV) * HD + s * kw, kw, 1),
        ],
        axis=1,
    )
    gains = jnp.zeros((3, width), F32)
    gains = lax.dynamic_update_slice(gains, first_gain[None], (0, d * first_gain.shape[0]))
    gains = lax.dynamic_update_slice(gains, second_gain[None], (1, d * second_gain.shape[0]))
    gains = lax.dynamic_update_slice(gains, qk_gain[None], (2, d * qk_gain.shape[0]))
    gains = lax.psum(gains, "dp")
    gain_in, gain_mid, gain_qk = gains[0], gains[1], gains[2, : 2 * HD]
    weight_qkv = lax.all_gather(mine_qkv, "dp", axis=0, tiled=True)
    stream_all = lax.all_gather(inputs[0], "seq", axis=0, tiled=True)
    weight_out = lax.all_gather(w_out, "dp", axis=0, tiled=True)
    cot_all = lax.all_gather(cotangent[0], "seq", axis=0, tiled=True)

    def slice_ff(w):
        return w.reshape(w.shape[0], nd, ns, piece)[:, :, s, :].reshape(w.shape[0], nd * piece)

    ffn = jnp.concatenate([slice_ff(w_gate), slice_ff(w_up)], axis=1)
    ffn = lax.all_gather(ffn, "dp", axis=0, tiled=True)
    down = lax.all_gather(lax.dynamic_slice_in_dim(w_down, s * piece, piece, 0), "dp", axis=0, tiled=True)

    stream32 = stream_all.astype(F32)
    scale_in = norm_scale(stream32)
    normed_in = (stream32 * scale_in * gain_in).astype(BF16)
    projected = dot(normed_in, weight_qkv)
    cosine, sine = rope_tables(jnp.arange(length))
    cosine, sine = cosine[:, None, :], sine[:, None, :]
    queries = projected[:, :qw].reshape(length, hq, HD)
    key_raw = projected[:, qw : qw + kw].reshape(length, hk, HD)
    scale_query, scale_key = norm_scale(queries), norm_scale(key_raw)
    query_normed = queries * scale_query * gain_qk[:HD]
    key_normed = key_raw * scale_key * gain_qk[HD:]
    q = (query_normed * cosine + rotate(query_normed) * sine).astype(BF16).reshape(length, hk, hq // hk, HD)
    k = (key_normed * cosine + rotate(key_normed) * sine).astype(BF16)
    v = projected[:, qw + kw :].astype(BF16).reshape(length, hk, HD)
    mix, total = attend_forward(q, k, v)
    mix = mix.reshape(length, qw)
    mixed_rows = lax.all_to_all(mix, "seq", split_axis=0, concat_axis=1, tiled=True)
    stream = inputs[0].astype(F32)
    residual = stream + dot(mixed_rows, weight_out)

    scale_mid = norm_scale(residual)
    normed_own = (residual * scale_mid * gain_mid).astype(BF16)
    normed_mid = lax.all_gather(normed_own, "seq", axis=0, tiled=True)
    n = nd * piece
    both = dot(normed_mid, ffn)
    gate_pre, up_pre = both[:, :n], both[:, n:]
    gate_sig = jax.nn.sigmoid(gate_pre)
    hidden = (gate_pre * gate_sig * up_pre).astype(BF16)
    grad_hidden = jnp.einsum("ri,ji->rj", cot_all, down, preferred_element_type=F32)
    ggp = (grad_hidden * up_pre * gate_sig * (1.0 + gate_pre * (1.0 - gate_sig))).astype(BF16)
    gup = (grad_hidden * gate_pre * gate_sig).astype(BF16)
    gboth = jnp.concatenate([ggp, gup], axis=1)
    gnm = lax.psum_scatter(
        jnp.einsum("ri,ji->rj", gboth, ffn, preferred_element_type=F32).astype(BF16),
        "seq", scatter_dimension=0, tiled=True,
    ).astype(F32)
    out_part = lax.psum_scatter(dot(hidden, down).astype(BF16), "seq", scatter_dimension=0, tiled=True)
    outputs = (residual + out_part.astype(F32)).astype(BF16)
    upstream = cotangent[0]
    grad_second = jnp.sum(gnm * residual * scale_mid, axis=0)
    grad_residual = upstream.astype(F32) + norm_back(residual, scale_mid, gnm * gain_mid)
    residual_back = grad_residual.astype(BF16)
    grad_mixed = jnp.einsum("ri,ji->rj", residual_back, weight_out, preferred_element_type=F32).astype(BF16)
    g = lax.all_to_all(grad_mixed, "seq", split_axis=1, concat_axis=0, tiled=True)

    gg = jnp.einsum("ri,rj->ij", normed_mid, gboth, preferred_element_type=F32).astype(BF16)
    gd = jnp.einsum("ri,rj->ij", hidden, cot_all, preferred_element_type=F32).astype(BF16)
    gg = lax.psum_scatter(gg, "dp", scatter_dimension=0, tiled=True)
    gd = lax.psum_scatter(gd, "dp", scatter_dimension=0, tiled=True)
    gout = jnp.einsum("ri,rj->ij", mixed_rows, residual_back, preferred_element_type=F32).astype(BF16)
    gout = lax.psum_scatter(gout, "dp", scatter_dimension=0, tiled=True)
    gout = lax.psum_scatter(gout, "seq", scatter_dimension=1, tiled=True)

    gq, gk, gv = attend_backward(q, k, v, g.reshape(q.shape), total)
    gq = gq.reshape(length, hq, HD).astype(F32)
    gk = gk.astype(F32)
    gqn = gq * cosine + rotate_back(gq * sine)
    gkn = gk * cosine + rotate_back(gk * sine)
    grad_qk = jnp.concatenate(
        [jnp.sum(gqn * queries * scale_query, axis=(0, 1)), jnp.sum(gkn * key_raw * scale_key, axis=(0, 1))]
    )
    gql = norm_back(queries, scale_query, gqn * gain_qk[:HD]).reshape(length, qw).astype(BF16)
    gkl = norm_back(key_raw, scale_key, gkn * gain_qk[HD:]).reshape(length, kw).astype(BF16)
    gproj = jnp.concatenate([gql, gkl, gv.reshape(length, kw)], axis=1)
    gqkv = jnp.einsum("ri,rj->ij", normed_in, gproj, preferred_element_type=F32).astype(BF16)
    gqkv = lax.psum_scatter(gqkv, "dp", scatter_dimension=0, tiled=True)
    gni = jnp.einsum("ri,ji->rj", gproj, weight_qkv, preferred_element_type=F32).astype(BF16)
    gni = lax.psum_scatter(gni, "seq", scatter_dimension=0, tiled=True).astype(F32)
    scale_own = norm_scale(stream)
    grad_first = jnp.sum(gni * stream * scale_own, axis=0)
    grad_stream = grad_residual + norm_back(stream, scale_own, gni * gain_in)
    small = jnp.stack([grad_first, grad_second, jnp.pad(grad_qk, (0, width - 2 * HD))])
    small = lax.psum(small, ("dp", "seq"))

    gl = first_gain.shape[0]
    ql = qk_gain.shape[0]
    g_first = lax.dynamic_slice(small, (0, d * gl), (1, gl))[0]
    g_second = lax.dynamic_slice(small, (1, d * gl), (1, gl))[0]
    g_qk = lax.dynamic_slice(small, (2, d * ql), (1, ql))[0]

    flat = jnp.concatenate(
        [gg.reshape(-1, 128), gd.reshape(-1, 128), gout.reshape(-1, 128), gqkv.reshape(-1, 128)], axis=0
    )
    flat = lax.all_gather(flat, "seq", axis=0)
    rows = w_gate.shape[0]
    a = gg.size // 128
    b = a + gd.size // 128
    c = b + gout.size // 128
    gg = flat[:, :a].reshape(ns, rows, 2, nd, piece).astype(F32)
    gg = gg.transpose(2, 1, 3, 0, 4).reshape(2, rows, ff)
    gd = flat[:, a:b].reshape(rows_d, width).astype(F32)
    gout = flat[:, b:c].reshape(ns, rows, width // ns).astype(F32).transpose(1, 0, 2).reshape(rows, width)
    gqkv = flat[:, c:].reshape(ns, rows, qw + 2 * kw).astype(F32).transpose(1, 0, 2)
    gqkv = jnp.concatenate(
        [
            gqkv[:, :, :qw].reshape(rows, -1),
            gqkv[:, :, qw : qw + kw].reshape(rows, -1),
            gqkv[:, :, qw + kw :].reshape(rows, -1),
        ],
        axis=1,
    )
    return (outputs[None], grad_stream[None], g_first, gqkv, g_qk, gout, g_second, gg[0], gg[1], gd)


def solution(mesh):
    act = P("dp", "seq", None)
    vec, mat = P("dp"), P("dp", None)
    in_specs = (act, act, vec, mat, vec, mat, vec, mat, mat, mat)
    out_specs = (act, act, vec, mat, vec, mat, vec, mat, mat, mat)
    return jax.shard_map(shards, mesh=mesh, in_specs=in_specs, out_specs=out_specs, check_vma=False)
```

time: 1090 us -> 741 us (0.68)
  waiting for transfers between devices: 642 us -> 375 us
  matrix products: 198 us -> 143 us
  starting transfers between devices: 29.1 us -> 6.15 us
  blocking collectives: 53 us -> 75.4 us
  other arithmetic: 60.7 us -> 43.1 us
  local copies, waits for them, and re-layouts: 80.8 us -> 69.4 us
    reduce_scatter x5 -> x8, waiting for transfers between devices: 328 us -> 196 us  [the longest x1 54.7 us: shards(): gg = lax.psum_scatter(gg, 'dp', scatter_dimension=0, tiled=True)]
    psum x1 -> x0, waiting for transfers between devices: 74.7 us -> none  [shards(): lax.psum(attn_shards[1].astype(jnp.bfloat16), 'seq').astype(jnp.float32)]
    psum x1 -> x2, blocking collectives: 8.19 us -> 64.4 us  [the longest x1 40.8 us: shards(): small = lax.psum(small, ('dp', 'seq'))]
    dot_general x28 -> x17, matrix products: 194 us -> 141 us  [the longest x1 27 us: attend_backward(): gk = jnp.einsum('kgrl,rkgd->lkd', gs, q, preferred_element_type=F32)]
    all_gather x5 -> x8, waiting for transfers between devices: 223 us -> 176 us  [the longest x1 52.3 us: shards(): ffn = lax.all_gather(ffn, 'dp', axis=0, tiled=True)]
    unnamed x2 -> x0, blocking collectives: 25.7 us -> none
    all_to_all x6 -> x1, starting transfers between devices: 28.6 us -> 4.92 us  [shards(): lax.all_to_all(grad_mixed, 'seq', split_axis=1, concat_axis=0, tiled=True)]
    all_gather x2 -> x0, blocking collectives: 19.2 us -> none  [the longest x1 11.4 us: shards(): lax.all_gather(second_gain.astype(jnp.bfloat16), 'dp', axis=0, tiled=True)]
  transfers between devices with their start and end apart: 17 -> 17, of which waited for: 12 -> 14; matrix products, arithmetic and copies ran while one was open for 27% -> 24% of each run, Pallas kernels for 0% -> 0%
where the time goes in v1:
time: 741 us; the launch traced here: 727 us
  waiting for transfers between devices  375 us (51%)
  matrix products  143 us (19%)
  blocking collectives  75.4 us (10%)
  local copies, waits for them, and re-layouts  69.4 us (9%)
  other arithmetic  43.1 us (6%)
  between operations  15.2 us (2%)
    reduce_scatter x1, waiting for transfers between devices, shards(): gg = lax.psum_scatter(gg, 'dp', scatter_dimension=0, tiled=True)  54.7 us
    all_gather x1, waiting for transfers between devices, shards(): ffn = lax.all_gather(ffn, 'dp', axis=0, tiled=True)  52.3 us
    psum x1, blocking collectives, shards(): small = lax.psum(small, ('dp', 'seq'))  40.8 us
    reduce_scatter x1, waiting for transfers between devices, shards(): lax.psum_scatter(dot(hidden, down).astype(BF16), 'seq', scatter_dimension...  36.5 us
    reduce_scatter x1, waiting for transfers between devices, shards(): lax.psum_scatter(gni, 'seq', scatter_dimension=0, tiled=True).astype(F32)  35.6 us
    all_gather x1, waiting for transfers between devices, shards(): lax.all_gather(lax.dynamic_slice_in_dim(w_down, s * piece, piece, 0), 'dp...  33 us
    reduce_scatter x1, waiting for transfers between devices, shards(): lax.psum_scatter(jnp.einsum('ri,ji->rj', gboth, ffn, preferred_element_ty...  28.2 us
    all_gather x1, waiting for transfers between devices, shards(): normed_mid = lax.all_gather(normed_own, 'seq', axis=0, tiled=True)  27.2 us
  transfers between devices with their start and end apart: 17, of which 14 were waited for; matrix products, arithmetic and copies ran while one was open for 24% of the time, Pallas kernels for 0%

profile of v1, /device:TPU:30, one launch (start us, length us, event | category | flops | bytes accessed | tf_op | source)
XLA Modules:
  0.0 727.2 jit_solution(97462026462167627)
XLA Ops:
  13.6 23.6 %psum.14 = f32[3,1024]{1,0:T(4,128)S(1)} all-reduce(f32[3,1024]{1,0:T(4,128)S(1)} %dynamic_update_slice.11), channel_id=1, replica_groups=mesh['dp'=8,'seq'=4] {'dp'}, use_global_device_ids=true, to_apply=%region_1.0 | all-reduce | flops 3072 | bytes 24576 | tf_op jit(solution)/shard_map/psum | solution.py:97
  38.4 1.3 iota_compare_fusion
  39.8 1.6 fusion.64
  41.4 3.8 all-gather.22.cloned.1.call-done
  45.2 2.1 fusion.11
  47.3 21.6 %all-gather.12.cloned.1.call-done = bf16[1024,512]{1,0:T(8,128)(2,1)} async-done(((bf16[128,512]{1,0:T(8,128)(2,1)}), bf16[1024,512]{1,0:T(8,128)(2,1)}) %all-gather.12.cloned.1.call-update) | async-done | bytes 1048592 | tf_op jit(solution)/shard_map/all_gather | solution.py:99
  69.0 3.3 fusion.57
  72.4 1.2 slice.120
  78.8 3.1 fusion.5
  81.9 3.7 exponential_reduce_fusion
  85.6 2.1 copy-done.8
  87.7 5.5 fusion.27
  93.2 2.2 all_to_all.26
  96.5 11.0 %all_to_all.35 = bf16[4,256,256]{1,2,0:T(8,128)(2,1)} all-to-all(bf16[4,256,256]{1,2,0:T(8,128)(2,1)S(1)} %copy.61), channel_id=1, replica_groups=mesh['dp'=8,'seq'=4] {'seq'}, dimensions={0} | all-to-all | bytes 1048576 | tf_op jit(solution)/shard_map/all_to_all | solution.py:127
  107.5 2.7 multiply_reduce_fusion
  112.6 2.4 copy.62
  115.0 2.4 copy.63
  120.8 27.2 %all-gather.16.cloned.1.call-done = bf16[1024,1024]{1,0:T(8,128)(2,1)} async-done(((bf16[256,1024]{1,0:T(8,128)(2,1)}), bf16[1024,1024]{1,0:T(8,128)(2,1)}) %all-gather.16.cloned.1.call-update) | async-done | bytes 2097168 | tf_op jit(solution)/shard_map/all_gather | solution.py:133
  148.0 52.3 %all-gather.18.cloned.1.call-done = bf16[1024,2304]{0,1:T(8,128)(2,1)} async-done(((bf16[128,2304]{0,1:T(8,128)(2,1)}), bf16[1024,2304]{0,1:T(8,128)(2,1)}) %all-gather.18.cloned.1.call-update) | async-done | bytes 4718608 | tf_op jit(solution)/shard_map/all_gather | solution.py:108
  200.3 10.1 %fusion.89 = f32[1024,2304]{1,0:T(8,128)} fusion(bf16[1024,1024]{1,0:T(8,128)(2,1)} %all-gather.16.cloned.1.call-done, bf16[1024,2304]{0,1:T(8,128)(2,1)} %all-gather.18.cloned.1.call-done), kind=kOutput, calls=%fused_computation.183 | convolution fusion | flops 4831838208 | bytes 16252928 | tf_op jit(solution)/shard_map/dot_general | solution.py:42
  210.4 27.1 %all-gather.24.cloned.1.call-done = bf16[1,1024,1024]{2,1,0:T(8,128)(2,1)} async-done(((bf16[1,256,1024]{2,1,0:T(8,128)(2,1)}), bf16[1,1024,1024]{2,1,0:T(8,128)(2,1)}) %all-gather.24.cloned.1.call-update) | async-done | bytes 2097168 | tf_op jit(solution)/shard_map/all_gather | solution.py:102
  237.5 33.0 %all-gather.20.cloned.1.call-done = bf16[1152,1024]{1,0:T(8,128)(2,1)} async-done(((bf16[144,1024]{1,0:T(8,128)(2,1)}), bf16[1152,1024]{1,0:T(8,128)(2,1)}) %all-gather.20.cloned.1.call-update) | async-done | bytes 2359312 | tf_op jit(solution)/shard_map/all_gather | solution.py:109
  270.4 10.8 %fusion.8 = (bf16[1024,1152]{1,0:T(8,128)(2,1)S(1)}, bf16[1024,1152]{1,0:T(8,128)(2,1)S(1)}, bf16[1024,1152]{1,0:T(8,128)(2,1)}) fusion(f32[1024,2304]{1,0:T(8,128)} %fusion.89, bf16[1152,1024]{1,0:T(8,128)(2,1)} %all-gather.20.cloned.1.call-done, bf16[1,1024,1024]{2,1,0:T(8,128)(2,1)} %all-gather.24.cloned.1.call-done), kind=kOutput, calls=%fused_computation.19 | convolution fusion | flops 2434793472 | bytes 20971520 | tf_op jit(solution)/shard_map/ri,ji->rj/dot_general | solution.py:139
  281.3 1.5 copy-done.52
  283.5 6.2 fusion.21
  289.8 6.6 convolution_convert_fusion.2
  296.9 28.2 %reduce-scatter.11.cloned.1.call-done = bf16[256,1024]{1,0:T(8,128)(2,1)} async-done(((bf16[1024,1024]{1,0:T(8,128)(2,1)}), bf16[256,1024]{1,0:T(8,128)(2,1)}) %reduce-scatter.11.cloned.1.call-update) | async-done | bytes 524304 | tf_op jit(solution)/shard_map/reduce_scatter | solution.py:143
  325.1 2.0 fusion.40
  327.0 36.5 %reduce-scatter.9.cloned.1.call-done = bf16[256,1024]{1,0:T(8,128)(2,1)} async-done(((bf16[1024,1024]{1,0:T(8,128)(2,1)}), bf16[256,1024]{1,0:T(8,128)(2,1)}) %reduce-scatter.9.cloned.1.call-update) | async-done | bytes 524304 | tf_op jit(solution)/shard_map/reduce_scatter | solution.py:147
  363.5 2.9 fusion.37
  366.4 2.0 convolution_convert_fusion.3
  368.6 2.3 convolution_convert_fusion.7
  371.8 4.9 all-to-all-start.1
  376.7 6.4 convolution_convert_fusion.1
  385.0 9.1 %fusion.90 = f32[2,1024,1024,2]{2,1,3,0:T(8,128)} fusion(bf16[1024,2,64,1]{0,2,3,1:T(8,128)(2,1)} %bitcast.341, bf16[1024,2,2,64]{0,3,2,1:T(8,128)(2,1)S(1)} %reshape.292), kind=kOutput, calls=%fused_computation.184 | convolution fusion | flops 536870912 | bytes 17563648 | tf_op jit(solution)/shard_map/rkgd,lkd->kgrl/dot_general | solution.py:66
  394.1 24.6 %fusion.23 = f32[2,64,2,1024]{3,1,2,0:T(8,128)S(1)} fusion(bf16[1024,2,64,1]{0,2,3,1:T(8,128)(2,1)} %copy-done.21, f32[2,1024,1024,2]{2,1,3,0:T(8,128)} %fusion.90, f32[2,1024,1024,2]{2,1,3,0:T(8,128)} %copy-done.8, f32[2,2,1024]{2,1,0:T(2,128)S(1)} %copy-done.34, pred[1024,1024]{0,1:T(8,128)(4,1)} %iota_compare_fusion), kind=kOutput, calls=%fused_computation.53 | convolution fusion | flops 583537664 | bytes 35930112 | tf_op jit(solution)/shard_map/kgrl,lkd->rkgd/dot_general | solution.py:69
  420.4 1.8 fusion.43
  422.2 27.0 %broadcast_multiply_fusion = (f32[1024,2,64]{0,2,1:T(8,128)}, f32[1024,2,64]{0,2,1:T(8,128)}) fusion(f32[1024,64]{0,1:T(8,128)} %get-tuple-element.71, bf16[1024,2,2,64]{0,3,2,1:T(8,128)(2,1)} %copy-done.20, f32[2,1024,1024,2]{2,1,3,0:T(8,128)} %fusion.90, f32[2,1024,1024,2]{2,1,3,0:T(8,128)} %copy-done.8, f32[2,2,1024]{2,1,0:T(2,128)} %copy-done.33, ...), kind=kOutput, calls=%fused_computation.134 | convolution fusion | flops 583406592 | bytes 36454400 | tf_op jit(solution)/shard_map/kgrl,rkgd->lkd/dot_general | solution.py:70
  449.3 1.2 fusion.87
  450.5 1.9 multiply_reduce_fusion.2
  453.3 8.2 %fusion.29 = bf16[2,64,1024]{2,1,0:T(8,128)(2,1)S(1)} fusion(bf16[1024,2,2,64]{0,3,2,1:T(8,128)(2,1)S(1)} %copy-done.16, f32[2,1024,1024,2]{2,1,3,0:T(8,128)} %copy-done.8, f32[2,2,1024]{2,1,0:T(2,128)S(1)} %copy-done.35, pred[1024,1024]{0,1:T(8,128)(4,1)S(1)} %copy-done.12), kind=kOutput, calls=%fused_computation.62 | convolution fusion | flops 553779200 | bytes 18628608 | tf_op jit(solution)/shard_map/kgrl,rkgd->lkd/dot_general | solution.py:65
  462.3 2.6 convolution_convert_fusion.5
  465.7 9.5 %convolution_convert_fusion = bf16[1024,2304]{1,0:T(8,128)(2,1)} fusion(bf16[1024,1024]{1,0:T(8,128)(2,1)S(1)} %copy-done.48, bf16[1024,1152]{1,0:T(8,128)(2,1)} %copy-done.53, bf16[1024,1152]{1,0:T(8,128)(2,1)} %copy-done.52), kind=kOutput, calls=%fused_computation.11 | convolution fusion | flops 4843634688 | bytes 11534336 | tf_op jit(solution)/shard_map/ri,rj->ij/dot_general | solution.py:156
  475.3 1.2 copy-done.49
  476.4 2.6 convolution_convert_fusion.4
  479.2 1.2 reshape.295
  480.4 14.1 %reduce-scatter.23.cloned.1.call-done = bf16[128,512]{1,0:T(8,128)(2,1)} async-done(((bf16[1024,512]{1,0:T(8,128)(2,1)}), bf16[128,512]{1,0:T(8,128)(2,1)}) %reduce-scatter.23.cloned.1.call-update) | async-done | bytes 131088 | tf_op jit(solution)/shard_map/reduce_scatter | solution.py:176
  495.4 27.0 %reduce-scatter.21.cloned.1.call-done = bf16[128,256]{1,0:T(8,128)(2,1)} async-done(((bf16[128,1024]{1,0:T(8,128)(2,1)}), bf16[128,256]{1,0:T(8,128)(2,1)}) %reduce-scatter.21.cloned.1.call-update) | async-done | bytes 65552 | tf_op jit(solution)/shard_map/reduce_scatter | solution.py:162
  523.3 54.7 %reduce-scatter.15.cloned.1.call-done = bf16[128,2304]{1,0:T(8,128)(2,1)} async-done(((bf16[1024,2304]{1,0:T(8,128)(2,1)}), bf16[128,2304]{1,0:T(8,128)(2,1)}) %reduce-scatter.15.cloned.1.call-update) | async-done | bytes 589840 | tf_op jit(solution)/shard_map/reduce_scatter | solution.py:158
  578.0 1.8 reshape.294
  581.3 35.6 %reduce-scatter.13.cloned.1.call-done = bf16[256,1024]{1,0:T(8,128)(2,1)} async-done(((bf16[1024,1024]{1,0:T(8,128)(2,1)}), bf16[256,1024]{1,0:T(8,128)(2,1)}) %reduce-scatter.13.cloned.1.call-update) | async-done | bytes 524304 | tf_op jit(solution)/shard_map/reduce_scatter | solution.py:178
  616.9 1.4 fusion.48
  618.3 40.8 %psum.15 = f32[3,1024]{1,0:T(4,128)S(1)} all-reduce(f32[3,1024]{1,0:T(4,128)S(1)} %pad_maximum_fusion.14), channel_id=1, replica_groups=mesh['dp'=8,'seq'=4] {'dp','seq'}, use_global_device_ids=true, to_apply=%region_21.22 | all-reduce | flops 3072 | bytes 24576 | tf_op jit(solution)/shard_map/psum | solution.py:183
  660.3 2.3 fusion.35
  662.6 11.2 %all-gather.26.cloned.1.call-done = bf16[16896,128]{1,0:T(8,128)(2,1)} async-done(((bf16[4224,128]{1,0:T(8,128)(2,1)}), bf16[16896,128]{1,0:T(8,128)(2,1)}) %all-gather.26.cloned.1.call-update) | async-done | bytes 4325392 | tf_op jit(solution)/shard_map/all_gather | solution.py:194
  673.8 4.1 slice_convert_fusion
  680.8 2.8 slice_convert_fusion.1
  684.6 9.2 %reshape.310 = f32[4,128,2,8,144]{4,3,2,1,0:T(8,128)} reshape(f32[4,2304,128]{2,1,0:T(8,128)} %slice_convert_fusion) | data formatting | bytes 9437184 | tf_op jit(solution)/shard_map/transpose | solution.py:200
  693.9 7.3 %fusion.84 = (f32[1,128,8,4,144]{4,2,0,1,3:T(8,128)}, f32[1,128,8,4,144]{4,2,0,1,3:T(8,128)}) fusion(f32[2,128,8,4,144]{4,2,0,1,3:T(8,128)} %bitcast.318), kind=kLoop, calls=%fused_computation.178 | loop fusion | bytes 9437184 | tf_op jit(solution)/shard_map/slice | solution.py:212
  701.2 3.6 copy.72
  704.8 2.0 copy.74
  706.7 3.6 copy.73
  710.3 2.0 copy.75
  714.5 3.3 reshape.307
  (212 shorter events, 40.9 us)
Async XLA Ops:
  7.2 112.8 %copy-start = (bf16[576,1024]{1,0:T(8,128)(2,1)S(1)}, bf16[576,1024]{1,0:T(8,128)(2,1)}, u32[]{:S(2)}) copy-start(bf16[576,1024]{1,0:T(8,128)(2,1)} %param.19) | copy-start | bytes 3538948
  7.2 38.0 %all-gather.22.cloned.1.call-start = ((), (), s32[]{:S(2)}) async-start(), calls=%async_computation.23 | async-start | bytes 2621440 | tf_op jit(solution)/shard_map/all_gather | solution.py:100
  7.9 61.0 %all-gather.12.cloned.1.call-start = ((), (), s32[]{:S(2)}) async-start(), calls=%async_computation.10 | async-start | bytes 1179648 | tf_op jit(solution)/shard_map/all_gather | solution.py:99
  10.3 97.2 %all-gather.14.cloned.1.call-start = ((), (), s32[]{:S(2)}) async-start(), calls=%async_computation.11 | async-start | bytes 2359296 | tf_op jit(solution)/shard_map/all_gather | solution.py:101
  11.0 137.0 %all-gather.16.cloned.1.call-start = ((), (), s32[]{:S(2)}) async-start(), calls=%async_computation.12 | async-start | bytes 2621440 | tf_op jit(solution)/shard_map/all_gather | solution.py:133
  37.8 34.4 %copy-start.28 = (f32[1,1024]{1,0:T(1,128)}, f32[1,1024]{1,0:T(1,128)S(1)}, u32[]{:S(2)}) copy-start(f32[1,1024]{1,0:T(1,128)S(1)} %get-tuple-element.77) | copy-start | bytes 12292
  47.3 26.3 %copy-start.44 = (f32[1024]{0:T(1024)}, f32[1024]{0:T(1024)S(1)}, u32[]{:S(2)}) copy-start(f32[1024]{0:T(1024)S(1)} %add_rsqrt_fusion.2) | copy-start | bytes 12292
  72.2 348.1 %copy-start.2 = (f32[1024,512]{0,1:T(8,128)}, f32[1024,512]{0,1:T(8,128)S(1)}, u32[]{:S(2)}) copy-start(f32[1024,512]{0,1:T(8,128)S(1)} %fusion.57) | copy-start | bytes 6291460
  76.2 1.7 copy-start.40
  76.2 1.9 copy-start.14
  76.2 2.1 copy-start.13
  76.2 2.1 copy-start.27
  76.2 2.1 copy-start.38
  77.2 1.6 copy-start.11
  77.9 3.9 copy-start.22
  78.3 3.5 copy-start.21
  78.8 3.1 copy-start.20
  81.9 5.8 copy-start.8
  81.9 5.8 copy-start.18
  85.6 2.1 copy-start.33
  107.5 3.8 copy-start.24
  112.4 88.0 %all-gather.18.cloned.1.call-start = ((), (), s32[]{:S(2)}) async-start(), calls=%async_computation.13 | async-start | bytes 5308416 | tf_op jit(solution)/shard_map/all_gather | solution.py:108
  119.3 118.1 %all-gather.24.cloned.1.call-start = ((), (), s32[]{:S(2)}) async-start(), calls=%async_computation.24 | async-start | bytes 2621440 | tf_op jit(solution)/shard_map/all_gather | solution.py:102
  119.9 150.5 %all-gather.20.cloned.1.call-start = ((), (), s32[]{:S(2)}) async-start(), calls=%async_computation.14 | async-start | bytes 2654208 | tf_op jit(solution)/shard_map/all_gather | solution.py:109
  120.7 204.3 %reduce-scatter.11.cloned.1.call-start = ((), (), s32[]{:S(2)}) async-start(), calls=%async_computation.16 | async-start | bytes 2621440 | tf_op jit(solution)/shard_map/reduce_scatter | solution.py:143
  270.4 13.0 %copy-start.47 = (bf16[1024,2304]{0,1:T(8,128)(2,1)S(1)}, bf16[1024,2304]{0,1:T(8,128)(2,1)}, u32[]{:S(2)}) copy-start(bf16[1024,2304]{0,1:T(8,128)(2,1)} %all-gather.18.cloned.1.call-done) | copy-start | bytes 14155780
  281.3 2.2 copy-start.53
  289.7 73.8 %reduce-scatter.9.cloned.1.call-start = ((), (), s32[]{:S(2)}) async-start(), calls=%async_computation.15 | async-start | bytes 2621440 | tf_op jit(solution)/shard_map/reduce_scatter | solution.py:147
  289.8 35.3 %copy-start.7 = (f32[256,1024]{1,0:T(8,128)S(1)}, f32[256,1024]{1,0:T(8,128)}, u32[]{:S(2)}) copy-start(f32[256,1024]{1,0:T(8,128)} %copy-done.6) | copy-start | bytes 3145732
  289.8 35.3 %copy-start.25 = (f32[1,1024]{1,0:T(1,128)S(1)}, f32[1,1024]{1,0:T(1,128)}, u32[]{:S(2)}) copy-start(f32[1,1024]{1,0:T(1,128)} %get-tuple-element.76) | copy-start | bytes 12292
  289.8 35.3 %copy-start.37 = (f32[256]{0:T(256)S(1)}, f32[256]{0:T(256)}, u32[]{:S(2)}) copy-start(f32[256]{0:T(256)} %copy-done.36) | copy-start | bytes 3076
  289.8 73.8 %copy-start.43 = (f32[256]{0:T(256)S(1)}, f32[256]{0:T(256)}, u32[]{:S(2)}) copy-start(f32[256]{0:T(256)} %get-tuple-element.84) | copy-start | bytes 3076
  296.4 168.5 %reduce-scatter.19.cloned.1.call-start = ((), (), s32[]{:S(2)}) async-start(), calls=%async_computation.20 | async-start | bytes 2359296 | tf_op jit(solution)/shard_map/reduce_scatter | solution.py:161
  363.5 2.9 copy-start.10
  363.5 5.0 copy-start.39
  366.4 4.5 copy-start.4
  371.8 11.7 %all-to-all-start.1 = ((bf16[256,4,256]{2,0,1:T(8,128)(2,1)}), bf16[256,4,256]{2,0,1:T(8,128)(2,1)S(1)}, u32[]{:S(2)}, u32[]{:S(2)}) async-start(bf16[256,4,256]{2,0,1:T(8,128)(2,1)} %bitcast.314), calls=%async_computation.3 | async-start | bytes 1048576 | tf_op jit(solution)/shard_map/all_to_all | solution.py:154
  376.7 102.5 %reduce-scatter.17.cloned.1.call-start = ((), (), s32[]{:S(2)}) async-start(), calls=%async_computation.19 | async-start | bytes 2654208 | tf_op jit(solution)/shard_map/reduce_scatter | solution.py:159
  383.1 111.3 %reduce-scatter.23.cloned.1.call-start = ((), (), s32[]{:S(2)}) async-start(), calls=%async_computation.22 | async-start | bytes 1179648 | tf_op jit(solution)/shard_map/reduce_scatter | solution.py:176
  385.0 9.1 %copy-start.34 = (f32[2,2,1024]{2,1,0:T(2,128)S(1)}, f32[2,2,1024]{2,1,0:T(2,128)}, u32[]{:S(2)}) copy-start(f32[2,2,1024]{2,1,0:T(2,128)} %copy-done.33) | copy-start | bytes 49156
  418.6 1.7 copy-start.26
  422.2 28.2 %copy-start.3 = (f32[1024,512]{0,1:T(8,128)S(1)}, f32[1024,512]{0,1:T(8,128)}, u32[]{:S(2)}) copy-start(f32[1024,512]{0,1:T(8,128)} %copy-done.2) | copy-start | bytes 6291460
  422.2 28.3 %slice-start = ((f32[1024,512]{0,1:T(8,128)}), f32[1024,128]{0,1:T(8,128)S(1)}, s32[]{:S(2)}) async-start(f32[1024,512]{0,1:T(8,128)} %copy-done.2), calls=%async_computation.26 | async-start | bytes 1048576 | tf_op jit(solution)/shard_map/slice | solution.py:118
  422.2 28.3 %copy-start.23 = (f32[1024,2]{0,1:T(2,128)S(1)}, f32[1024,2]{0,1:T(2,128)}, u32[]{:S(2)}) copy-start(f32[1024,2]{0,1:T(2,128)} %copy-done.22) | copy-start | bytes 24580
  422.2 28.3 %copy-start.41 = (f32[64]{0:T(128)S(1)}, f32[64]{0:T(128)}, u32[]{:S(2)}) copy-start(f32[64]{0:T(128)} %get-tuple-element.79) | copy-start | bytes 772
  422.2 30.2 %copy-start.30 = (f32[1024,2]{0,1:T(2,128)S(1)}, f32[1024,2]{0,1:T(2,128)}, u32[]{:S(2)}) copy-start(f32[1024,2]{0,1:T(2,128)} %get-tuple-element.80) | copy-start | bytes 24580
  449.2 4.0 copy-start.12
  449.2 4.0 copy-start.16
  449.2 4.0 copy-start.35
  453.2 9.0 %copy-start.17 = (bf16[1,1024,1024]{2,1,0:T(8,128)(2,1)S(1)}, bf16[1,1024,1024]{2,1,0:T(8,128)(2,1)}, u32[]{:S(2)}) copy-start(bf16[1,1024,1024]{2,1,0:T(8,128)(2,1)} %all-gather.22.cloned.1.call-done) | copy-start | bytes 6291460
  453.3 9.0 %copy-start.19 = (bf16[1024,256]{0,1:T(8,128)(2,1)S(1)}, bf16[1024,256]{0,1:T(8,128)(2,1)}, u32[]{:S(2)}) copy-start(bf16[1024,256]{0,1:T(8,128)(2,1)} %get-tuple-element.53) | copy-start | bytes 1572868
  453.3 9.0 %copy-start.29 = (f32[1,1024]{1,0:T(1,128)S(1)}, f32[1,1024]{1,0:T(1,128)}, u32[]{:S(2)}) copy-start(f32[1,1024]{1,0:T(1,128)} %copy-done.28) | copy-start | bytes 12292
  453.3 9.0 %copy-start.45 = (f32[1024]{0:T(1024)S(1)}, f32[1024]{0:T(1024)}, u32[]{:S(2)}) copy-start(f32[1024]{0:T(1024)} %copy-done.44) | copy-start | bytes 12292
  462.2 3.4 copy-start.48
  464.9 57.6 %reduce-scatter.21.cloned.1.call-start = ((), (), s32[]{:S(2)}) async-start(), calls=%async_computation.21 | async-start | bytes 327680 | tf_op jit(solution)/shard_map/reduce_scatter | solution.py:162
  465.6 112.4 %reduce-scatter.15.cloned.1.call-start = ((), (), s32[]{:S(2)}) async-start(), calls=%async_computation.18 | async-start | bytes 5308416 | tf_op jit(solution)/shard_map/reduce_scatter | solution.py:158
  475.2 141.7 %reduce-scatter.13.cloned.1.call-start = ((), (), s32[]{:S(2)}) async-start(), calls=%async_computation.17 | async-start | bytes 2621440 | tf_op jit(solution)/shard_map/reduce_scatter | solution.py:178
  479.1 101.9 %copy-start.9 = (bf16[1,256,1024]{2,1,0:T(8,128)(2,1)S(1)}, bf16[1,256,1024]{2,1,0:T(8,128)(2,1)}, u32[]{:S(2)}) copy-start(bf16[1,256,1024]{2,1,0:T(8,128)(2,1)} %param.10) | copy-start | bytes 1572868
  479.1 102.1 %copy-start.42 = (f32[256]{0:T(256)S(1)}, f32[256]{0:T(256)}, u32[]{:S(2)}) copy-start(f32[256]{0:T(256)} %get-tuple-element.52) | copy-start | bytes 3076
  479.1 102.2 %copy-start.46 = (f32[64]{0:T(128)S(1)}, f32[64]{0:T(128)}, u32[]{:S(2)}) copy-start(f32[64]{0:T(128)} %get-tuple-element.44) | copy-start | bytes 772
  479.1 139.2 %copy-start.32 = (f32[1024]{0:T(1024)S(1)}, f32[1024]{0:T(1024)}, u32[]{:S(2)}) copy-start(f32[1024]{0:T(1024)} %get-tuple-element.40) | copy-start | bytes 12292
  479.1 181.2 %copy-start.5 = (f32[256,1024]{1,0:T(8,128)S(1)}, f32[256,1024]{1,0:T(8,128)}, u32[]{:S(2)}) copy-start(f32[256,1024]{1,0:T(8,128)} %copy-done.4) | copy-start | bytes 3145732
  479.1 194.7 %all-gather.26.cloned.1.call-start = ((), (), s32[]{:S(2)}) async-start(), calls=%async_computation.25 | async-start | bytes 5406720 | tf_op jit(solution)/shard_map/all_gather | solution.py:194
  713.4 6.8 copy-start.1
  (8 other events, 8.1 us)
Sparse Core Ops, SparseCore 0:
  9.9 35.2 all-gather.21
  47.4 21.5 all-gather.11
  70.6 28.7 all-gather.13
  112.5 35.5 all-gather.15
  150.0 50.2 all-gather.17
  202.0 35.4 all-gather.23
  239.7 30.7 all-gather.19
  289.8 35.2 reduce-scatter.10
  328.3 35.1 reduce-scatter.8
  368.6 32.7 reduce-scatter.18
  404.3 34.9 reduce-scatter.16
  465.0 29.4 reduce-scatter.22
  497.2 25.1 reduce-scatter.20
  524.7 53.3 reduce-scatter.14
  581.7 35.1 reduce-scatter.12
  619.2 54.5 all-gather.25

commit v2 on v1

--- a/solution.py
+++ b/solution.py
@@ -1,6 +1,11 @@
+import functools
+
 import jax
 import jax.numpy as jnp
+import numpy as np
 from jax import lax
+from jax.experimental import pallas as pl
+from jax.experimental.pallas import tpu as pltpu
 from jax.sharding import PartitionSpec as P
 
 H = 16
@@ -36,6 +41,225 @@
     angles = positions.astype(F32)[:, None] * inverse[None, :]
     angles = jnp.concatenate([angles, angles], axis=-1)
     return (jnp.cos(angles), jnp.sin(angles))
+
+
+def rope_columns(length):
+    inverse = np.float32(THETA_BASE) ** (-np.arange(0, HD, 2).astype(np.float32) / np.float32(HD))
+    angles = (np.arange(length, dtype=np.float32)[None, :] * inverse.astype(np.float32)[:, None]).astype(np.float32)
+    angles = angles.astype(np.float64)
+    return jnp.asarray(np.cos(angles), F32), jnp.asarray(np.sin(angles), F32)
+
+
+MESH = pl.DeviceIdType.MESH
+DMA = pltpu.SemaphoreType.DMA
+
+
+def mm(a, b):
+    return jnp.dot(a, b, preferred_element_type=F32)
+
+
+def mm_nt(a, b):
+    return lax.dot_general(a, b, (((1,), (1,)), ((), ())), preferred_element_type=F32)
+
+
+def remote(src, dst, send, recv, device):
+    return pltpu.make_async_remote_copy(
+        src_ref=src, dst_ref=dst, send_sem=send, recv_sem=recv, device_id=device, device_id_type=MESH
+    )
+
+
+def greet(ns, nd, s, d):
+    bar = pltpu.get_barrier_semaphore()
+    for j in range(1, nd):
+        pl.semaphore_signal(bar, inc=1, device_id=(lax.rem(d + j, nd), s), device_id_type=MESH)
+    for j in range(1, ns):
+        pl.semaphore_signal(bar, inc=1, device_id=(d, lax.rem(s + j, ns)), device_id_type=MESH)
+    pl.semaphore_wait(bar, nd + ns - 2)
+
+
+def front_kernel(
+    ns, nd, x, gains, wqkv_mine, wout_mine, cot, cos, sin,
+    normed, projT, qT, kT, vT, krows, vrows, inv, mixT, mrowsT, resid, wout, wqkv, gsum, cotall,
+    xall, gbuf, xs, xr, gs, gr, qs, qr, os_, or_, fs, fr, cs, cr, ms, mr,
+):
+    d, s = lax.axis_index("dp"), lax.axis_index("seq")
+    nz = nd // 2
+    zz, core = d // 2, lax.rem(d, 2)
+    sib = d + 1 - 2 * core
+    T = x.shape[0]
+    L = ns * T
+    R = wqkv_mine.shape[0]
+    hq, hk = H // ns, KV // ns
+    group = hq // hk
+    qw, kw = hq * HD, hk * HD
+    own = pl.ds(pl.multiple_of(s * T, T), T)
+    mine = pl.ds(pl.multiple_of(d * R, R), R)
+    greet(ns, nd, s, d)
+
+    def to(j):
+        return (d, lax.rem(s + j, ns))
+
+    x_copies = [remote(x, xall.at[own], xs.at[j], xr.at[j], to(j)) for j in range(1, ns)]
+    g_copies = [
+        remote(gains, gbuf.at[d], gs.at[j], gr.at[j], (lax.rem(d + j, nd), s)) for j in range(1, nd)
+    ]
+    q_copies = [
+        remote(wqkv_mine, wqkv.at[mine], qs.at[j], qr.at[j], (lax.rem(d + j, nd), s)) for j in range(1, nd)
+    ]
+    o_copies = [
+        remote(wout_mine, wout.at[mine], os_.at[j], or_.at[j], (2 * lax.rem(zz + j, nz) + core, s))
+        for j in range(1, nz)
+    ]
+    o_copies.append(remote(wout_mine, wout.at[mine], os_.at[0], or_.at[0], (sib, s)))
+    for c in x_copies + g_copies + q_copies + o_copies:
+        c.start()
+    xall[own, :] = x[...]
+    gbuf[d] = gains[...]
+    wqkv[mine, :] = wqkv_mine[...]
+    wout[mine, :] = wout_mine[...]
+    cotall[own, :] = cot[...]
+    for c in g_copies:
+        c.wait_recv()
+    total = gbuf[0]
+    for k in range(1, nd):
+        total = total + gbuf[k]
+    gsum[...] = total
+    gain_in = total[0:1, :]
+    columns = jnp.transpose(total[:, : 2 * HD])
+    gain_q, gain_k = columns[:HD, 2:3], columns[HD:, 2:3]
+
+    c_copies = [remote(cot, cotall.at[own], cs.at[j], cr.at[j], to(j)) for j in range(1, ns)]
+    for j in range(ns):
+        rows = pl.ds(pl.multiple_of(lax.rem(s + ns - j, ns) * T, T), T)
+        if j:
+            x_copies[j - 1].wait_recv()
+        xc = xall[rows, :].astype(F32)
+        scale = lax.rsqrt(jnp.mean(xc * xc, axis=-1, keepdims=True) + EPSILON)
+        normed[rows, :] = (xc * scale * gain_in).astype(BF16)
+    for c in c_copies:
+        c.start()
+    for c in q_copies:
+        c.wait_recv()
+    for j in range(ns):
+        rows = pl.ds(j * T, T)
+        proj = mm(normed[rows, :], wqkv[...])
+        projT[:, rows] = jnp.transpose(proj[:, : qw + kw])
+        val = proj[:, qw + kw :]
+        vT[:, rows] = jnp.transpose(val).astype(BF16)
+        for i in range(hk):
+            vrows[i, rows, :] = val[:, i * HD : (i + 1) * HD].astype(BF16)
+
+    half = HD // 2
+
+    def rope(row, gain, factor):
+        u = projT[row, :]
+        scale = lax.rsqrt(jnp.mean(u * u, axis=0, keepdims=True) + EPSILON)
+        u = u * scale * gain
+        a, b = u[:half], u[half:]
+        return jnp.concatenate([a * cos[...] - b * sin[...], b * cos[...] + a * sin[...]], axis=0) * factor
+
+    def rope_query(h, carry):
+        row = pl.ds(pl.multiple_of(h * HD, HD), HD)
+        qT[row, :] = rope(row, gain_q, HD**-0.5).astype(BF16)
+        return carry
+
+    lax.fori_loop(0, hq, rope_query, 0)
+    for i in range(hk):
+        r = rope(pl.ds(qw + i * HD, HD), gain_k, 1.0)
+        kT[i * HD : (i + 1) * HD, :] = r.astype(BF16)
+        krows[i, :, :] = jnp.transpose(r).astype(BF16)
+
+    for c in o_copies:
+        c.wait_recv()
+    f_copies = []
+    for j in range(1, nz):
+        piece = pl.ds(pl.multiple_of((2 * lax.rem(zz + nz - j, nz) + core) * R, R), R)
+        c = remote(wout.at[piece], wout.at[piece], fs.at[j], fr.at[j], (sib, s))
+        c.start()
+        f_copies.append(c)
+
+    keep = lax.broadcasted_iota(jnp.int32, (T, T), 0) <= lax.broadcasted_iota(jnp.int32, (T, T), 1)
+    for rb in range(ns):
+        cols = pl.ds(rb * T, T)
+        span = rb * T
+
+        def head(h, carry):
+            kv = h // group
+            row = pl.ds(pl.multiple_of(h * HD, HD), HD)
+            vrow = pl.ds(pl.multiple_of(kv * HD, HD), HD)
+            q = qT[row, cols]
+            p = jnp.where(keep, jnp.exp(mm(krows[kv, cols, :], q)), 0.0)
+            tot = jnp.sum(p, axis=0, keepdims=True)
+            m = mm(vT[vrow, cols], p.astype(BF16))
+            if span:
+                p = jnp.exp(mm(krows[kv, 0:span, :], q))
+                tot = tot + jnp.sum(p, axis=0, keepdims=True)
+                m = m + mm(vT[vrow, 0:span], p.astype(BF16))
+            one = 1.0 / tot
+            inv[h, :, cols] = one
+            mixT[rb, row, :] = (m * one).astype(BF16)
+            return carry
+
+        lax.fori_loop(0, hq, head, 0)
+        block = pl.ds(pl.multiple_of(s * qw, qw), qw)
+
+        @pl.when(s != rb)
+        def _():
+            remote(mixT.at[rb], mrowsT.at[block], ms.at[rb], mr.at[s], (d, rb)).start()
+
+    block = pl.ds(pl.multiple_of(s * qw, qw), qw)
+    mrowsT[block, :] = mixT[s]
+    for j in range(1, ns):
+        src = lax.rem(s + ns - j, ns)
+        part = pl.ds(pl.multiple_of(src * qw, qw), qw)
+        remote(mixT.at[0], mrowsT.at[part], ms.at[0], mr.at[src], (d, src)).wait_recv()
+    for c in f_copies:
+        c.wait_recv()
+    resid[...] = x[...].astype(F32) + mm(jnp.transpose(mrowsT[...]), wout[...])
+    for rb in range(ns):
+
+        @pl.when(s != rb)
+        def _():
+            remote(mixT.at[rb], mrowsT.at[block], ms.at[rb], mr.at[s], (d, rb)).wait_send()
+
+    for c in c_copies:
+        c.wait_recv()
+    for c in x_copies + g_copies + q_copies + o_copies + f_copies + c_copies:
+        c.wait_send()
+
+
+def vmem(n):
+    return [pl.BlockSpec(memory_space=pltpu.VMEM)] * n
+
+
+def front(ns, nd, x, gains, wqkv_mine, wout_mine, cot):
+    T, width = x.shape
+    L = ns * T
+    hq, hk = H // ns, KV // ns
+    qw, kw = hq * HD, hk * HD
+    cos, sin = rope_columns(L)
+    sh = jax.ShapeDtypeStruct
+    outs = (
+        sh((L, width), BF16), sh((qw + kw, L), F32), sh((qw, L), BF16), sh((kw, L), BF16), sh((kw, L), BF16),
+        sh((hk, L, HD), BF16), sh((hk, L, HD), BF16), sh((hq, 1, L), F32), sh((ns, qw, T), BF16),
+        sh((H * HD, T), BF16), sh((T, width), F32), sh((H * HD, width), BF16), sh((width, qw + 2 * kw), BF16),
+        sh((8, width), F32), sh((L, width), BF16),
+    )
+    return pl.pallas_call(
+        functools.partial(front_kernel, ns, nd),
+        out_shape=outs,
+        in_specs=vmem(7),
+        out_specs=vmem(len(outs)),
+        scratch_shapes=[
+            pltpu.VMEM((L, width), BF16), pltpu.VMEM((nd, 8, width), F32),
+            DMA((ns,)), DMA((ns,)), DMA((nd,)), DMA((nd,)), DMA((nd,)), DMA((nd,)), DMA((nd,)), DMA((nd,)),
+            DMA((nd,)), DMA((nd,)), DMA((ns,)), DMA((ns,)), DMA((ns,)), DMA((ns,)),
+        ],
+        compiler_params=pltpu.CompilerParams(
+            collective_id=0, has_side_effects=True, vmem_limit_bytes=56 << 20
+        ),
+        cost_estimate=pl.CostEstimate(flops=6_000_000_000, bytes_accessed=20_000_000, transcendentals=3_000_000),
+    )(x, gains, wqkv_mine, wout_mine, cot, cos, sin)
 
 
 def dot(a, b):
@@ -90,16 +314,13 @@
         ],
         axis=1,
     )
-    gains = jnp.zeros((3, width), F32)
+    gains = jnp.zeros((8, width), F32)
     gains = lax.dynamic_update_slice(gains, first_gain[None], (0, d * first_gain.shape[0]))
     gains = lax.dynamic_update_slice(gains, second_gain[None], (1, d * second_gain.shape[0]))
     gains = lax.dynamic_update_slice(gains, qk_gain[None], (2, d * qk_gain.shape[0]))
-    gains = lax.psum(gains, "dp")
+    (normed_in, projT, qT, kT, vT, krows, vrows, inv, mixT, mrowsT, residual, weight_out, weight_qkv, gains,
+     cot_all) = front(ns, nd, inputs[0], gains, mine_qkv, w_out, cotangent[0])
     gain_in, gain_mid, gain_qk = gains[0], gains[1], gains[2, : 2 * HD]
-    weight_qkv = lax.all_gather(mine_qkv, "dp", axis=0, tiled=True)
-    stream_all = lax.all_gather(inputs[0], "seq", axis=0, tiled=True)
-    weight_out = lax.all_gather(w_out, "dp", axis=0, tiled=True)
-    cot_all = lax.all_gather(cotangent[0], "seq", axis=0, tiled=True)
 
     def slice_ff(w):
         return w.reshape(w.shape[0], nd, ns, piece)[:, :, s, :].reshape(w.shape[0], nd * piece)
@@ -108,25 +329,17 @@
     ffn = lax.all_gather(ffn, "dp", axis=0, tiled=True)
     down = lax.all_gather(lax.dynamic_slice_in_dim(w_down, s * piece, piece, 0), "dp", axis=0, tiled=True)
 
-    stream32 = stream_all.astype(F32)
-    scale_in = norm_scale(stream32)
-    normed_in = (stream32 * scale_in * gain_in).astype(BF16)
-    projected = dot(normed_in, weight_qkv)
+    stream = inputs[0].astype(F32)
     cosine, sine = rope_tables(jnp.arange(length))
     cosine, sine = cosine[:, None, :], sine[:, None, :]
-    queries = projected[:, :qw].reshape(length, hq, HD)
-    key_raw = projected[:, qw : qw + kw].reshape(length, hk, HD)
+    queries = projT[:qw].T.reshape(length, hq, HD)
+    key_raw = projT[qw:].T.reshape(length, hk, HD)
     scale_query, scale_key = norm_scale(queries), norm_scale(key_raw)
-    query_normed = queries * scale_query * gain_qk[:HD]
-    key_normed = key_raw * scale_key * gain_qk[HD:]
-    q = (query_normed * cosine + rotate(query_normed) * sine).astype(BF16).reshape(length, hk, hq // hk, HD)
-    k = (key_normed * cosine + rotate(key_normed) * sine).astype(BF16)
-    v = projected[:, qw + kw :].astype(BF16).reshape(length, hk, HD)
-    mix, total = attend_forward(q, k, v)
-    mix = mix.reshape(length, qw)
-    mixed_rows = lax.all_to_all(mix, "seq", split_axis=0, concat_axis=1, tiled=True)
-    stream = inputs[0].astype(F32)
-    residual = stream + dot(mixed_rows, weight_out)
+    q = (qT.T * 8.0).astype(BF16).reshape(length, hk, hq // hk, HD)
+    k = krows.transpose(1, 0, 2)
+    v = vrows.transpose(1, 0, 2)
+    total = -jnp.log(inv.reshape(hk, hq // hk, length, 1))
+    mixed_rows = mrowsT.T
 
     scale_mid = norm_scale(residual)
     normed_own = (residual * scale_mid * gain_mid).astype(BF16)

time: 741 us -> 694 us (0.937)
  Pallas kernels: 0 us -> 75.6 us
  waiting for transfers between devices: 375 us -> 315 us
  blocking collectives: 75.4 us -> 40.8 us
  other arithmetic: 43.1 us -> 33.1 us
  matrix products: 143 us -> 135 us
    pallas_call x0 -> x1, Pallas kernels: none -> 75.6 us  [front(): pl.pallas_call(functools.partial(front_kernel, ns, nd), out_shape=outs, i...]
    all_gather x4 -> x0, waiting for transfers between devices: 52.5 us -> none  [the longest x1 27.1 us: shards(): cot_all = lax.all_gather(cotangent[0], 'seq', axis=0, tiled=True)]
    psum x1 -> x0, blocking collectives: 23.6 us -> none  [shards(): gains = lax.psum(gains, 'dp')]
    all_to_all x1 -> x0, blocking collectives: 11 us -> none  [shards(): lax.all_to_all(mix, 'seq', split_axis=0, concat_axis=1, tiled=True)]
    all_gather x1, waiting for transfers between devices: 33 us -> 22.9 us  [shards(): lax.all_gather(lax.dynamic_slice_in_dim(w_down, s * piece, piece, 0), 'dp...]
    dot_general x4 -> x2, matrix products: 22.6 us -> 16.9 us  [dot(): return jnp.dot(a, b, preferred_element_type=F32)]
    unnamed x116 -> x76, local copies, waits for them, and re-layouts: 19.3 us -> 17.4 us
  transfers between devices with their start and end apart: 17 -> 13, of which waited for: 14 -> 11; matrix products, arithmetic and copies ran while one was open for 24% -> 21% of each run, Pallas kernels for 0% -> 0%
where the time goes in v2:
time: 694 us; the launch traced here: 685 us
  waiting for transfers between devices  315 us (45%)
  matrix products  135 us (19%)
  Pallas kernels  75.6 us (11%)
  local copies, waits for them, and re-layouts  64.2 us (9%)
  blocking collectives  40.8 us (6%)
  other arithmetic  33.1 us (5%)
  between operations  15.3 us (2%)
    pallas_call x1, Pallas kernels, front(): pl.pallas_call(functools.partial(front_kernel, ns, nd), out_shape=outs, i...  75.6 us
    reduce_scatter x1, waiting for transfers between devices, shards(): gg = lax.psum_scatter(gg, 'dp', scatter_dimension=0, tiled=True)  54.7 us
    all_gather x1, waiting for transfers between devices, shards(): ffn = lax.all_gather(ffn, 'dp', axis=0, tiled=True)  52.4 us
    psum x1, blocking collectives, shards(): small = lax.psum(small, ('dp', 'seq'))  40.8 us
    reduce_scatter x1, waiting for transfers between devices, shards(): lax.psum_scatter(dot(hidden, down).astype(BF16), 'seq', scatter_dimension...  36.9 us
    reduce_scatter x1, waiting for transfers between devices, shards(): lax.psum_scatter(gni, 'seq', scatter_dimension=0, tiled=True).astype(F32)  35.7 us
    all_gather x1, waiting for transfers between devices, shards(): normed_mid = lax.all_gather(normed_own, 'seq', axis=0, tiled=True)  30.6 us
    reduce_scatter x1, waiting for transfers between devices, shards(): lax.psum_scatter(jnp.einsum('ri,ji->rj', gboth, ffn, preferred_element_ty...  28.4 us
  transfers between devices with their start and end apart: 13, of which 11 were waited for; matrix products, arithmetic and copies ran while one was open for 21% of the time, Pallas kernels for 0%

profile of v2, /device:TPU:30, one launch (start us, length us, event | category | flops | bytes accessed | tf_op | source)
XLA Modules:
  0.0 685.0 jit_solution(6548460465041722402)
XLA Ops:
  12.8 75.6 %shard_map.195 = (bf16[1024,1024]{1,0:T(8,128)(2,1)}, f32[384,1024]{1,0:T(8,128)}, bf16[256,1024]{1,0:T(8,128)(2,1)}, bf16[128,1024]{1,0:T(8,128)(2,1)}, bf16[12...) custom-call(bf16[256,1024]{1,0:T(8,128)(2,1)} %bitcast.291, ...), custom_call_target="tpu_custom_call" | custom-call | flops 6000000000 | bytes 20000000 | tf_op jit(solution)/shard_map/pallas_call | solution.py:248
  88.4 1.4 multiply_reduce_fusion.1
  91.2 2.2 multiply_convert_fusion.3
  94.2 1.7 copy.64
  98.2 30.6 %all-gather.6.cloned.1.call-done = bf16[1024,1024]{1,0:T(8,128)(2,1)} async-done(((bf16[256,1024]{1,0:T(8,128)(2,1)}), bf16[1024,1024]{1,0:T(8,128)(2,1)}) %all-gather.6.cloned.1.call-update) | async-done | bytes 2097168 | tf_op jit(solution)/shard_map/all_gather | solution.py:346
  128.8 52.4 %all-gather.8.cloned.1.call-done = bf16[1024,2304]{0,1:T(8,128)(2,1)} async-done(((bf16[128,2304]{0,1:T(8,128)(2,1)}), bf16[1024,2304]{0,1:T(8,128)(2,1)}) %all-gather.8.cloned.1.call-update) | async-done | bytes 4718608 | tf_op jit(solution)/shard_map/all_gather | solution.py:329
  181.3 10.2 %fusion.83 = f32[1024,2304]{1,0:T(8,128)} fusion(bf16[1024,1024]{1,0:T(8,128)(2,1)} %all-gather.6.cloned.1.call-done, bf16[1024,2304]{0,1:T(8,128)(2,1)} %all-gather.8.cloned.1.call-done), kind=kOutput, calls=%fused_computation.163 | convolution fusion | flops 4831838208 | bytes 16252928 | tf_op jit(solution)/shard_map/dot_general | solution.py:266
  191.5 22.9 %all-gather.10.cloned.1.call-done = bf16[1152,1024]{1,0:T(8,128)(2,1)} async-done(((bf16[144,1024]{1,0:T(8,128)(2,1)}), bf16[1152,1024]{1,0:T(8,128)(2,1)}) %all-gather.10.cloned.1.call-update) | async-done | bytes 2359312 | tf_op jit(solution)/shard_map/all_gather | solution.py:330
  214.3 10.8 %multiply_convert_fusion.1 = (bf16[1024,1152]{1,0:T(8,128)(2,1)S(1)}, bf16[1024,1152]{1,0:T(8,128)(2,1)S(1)}, bf16[1024,1152]{1,0:T(8,128)(2,1)}) fusion(f32[1024,2304]{1,0:T(8,128)} %fusion.83, bf16[1024,1024]{1,0:T(8,128)(2,1)} %get-tuple-element.24, bf16[1152,1024]{1,0:T(8,128)(2,1)} %all-gather.10.cloned.1.call-done), kind=kOutput, calls=%fused_computation.15 | convolution fusion | flops 2434793472 | bytes 20971520 | tf_op jit(solution)/shard_map/ri,ji->rj/dot_general | solution.py:352
  225.2 1.4 copy-done.30
  227.4 6.2 fusion.14
  233.7 6.7 convolution_convert_fusion.2
  240.7 28.4 %reduce-scatter.11.cloned.1.call-done = bf16[256,1024]{1,0:T(8,128)(2,1)} async-done(((bf16[1024,1024]{1,0:T(8,128)(2,1)}), bf16[256,1024]{1,0:T(8,128)(2,1)}) %reduce-scatter.11.cloned.1.call-update) | async-done | bytes 524304 | tf_op jit(solution)/shard_map/reduce_scatter | solution.py:356
  269.0 1.4 fusion.37
  270.4 36.9 %reduce-scatter.9.cloned.1.call-done = bf16[256,1024]{1,0:T(8,128)(2,1)} async-done(((bf16[1024,1024]{1,0:T(8,128)(2,1)}), bf16[256,1024]{1,0:T(8,128)(2,1)}) %reduce-scatter.9.cloned.1.call-update) | async-done | bytes 524304 | tf_op jit(solution)/shard_map/reduce_scatter | solution.py:360
  307.3 2.4 fusion.34
  309.7 2.1 convolution_convert_fusion.3
  311.8 1.3 slice_bitcast_fusion.1
  313.9 1.1 slice.77
  315.1 1.0 fusion.58
  316.1 1.3 iota_compare_fusion
  317.4 8.0 %fusion.54 = f32[2,1024,1024,2]{2,1,3,0:T(8,128)} fusion(bf16[1024,2,2,64]{0,3,2,1:T(8,128)(2,1)S(1)} %bitcast.299, bf16[2,1024,64]{2,1,0:T(8,128)(2,1)S(1)} %copy-done.16), kind=kOutput, calls=%fused_computation.96 | convolution fusion | flops 536870912 | bytes 17563648 | tf_op jit(solution)/shard_map/rkgd,lkd->kgrl/dot_general | solution.py:271
  327.1 5.0 all-to-all-start
  332.0 6.4 convolution_convert_fusion.1
  340.2 9.1 %fusion.52 = f32[2,1024,1024,2]{2,1,3,0:T(8,128)} fusion(bf16[1024,2,2,64]{0,3,2,1:T(8,128)(2,1)S(1)} %reshape.266, bf16[2,1024,64]{2,1,0:T(8,128)(2,1)} %get-tuple-element.29), kind=kOutput, calls=%fused_computation.94 | convolution fusion | flops 536870912 | bytes 17563648 | tf_op jit(solution)/shard_map/rkgd,lkd->kgrl/dot_general | solution.py:290
  349.4 24.9 %fusion.16 = f32[2,64,2,1024]{3,1,2,0:T(8,128)S(1)} fusion(f32[2,1024,1024,2]{2,1,3,0:T(8,128)} %fusion.52, f32[2,1024,1024,2]{2,1,3,0:T(8,128)} %fusion.54, f32[2,2,1024]{2,1,0:T(2,128)S(1)} %neg.31, pred[1024,1024]{0,1:T(8,128)(4,1)} %iota_compare_fusion, bf16[2,1024,64]{2,1,0:T(8,128)(2,1)} %get-tuple-element.26), kind=kOutput, calls=%fused_computation.40 | convolution fusion | flops 583537664 | bytes 35930112 | tf_op jit(solution)/shard_map/kgrl,lkd->rkgd/dot_general | solution.py:293
  374.6 1.1 copy-done.3
  376.3 1.3 fusion.40
  377.6 26.8 %broadcast_multiply_fusion = (f32[1024,2,64]{0,2,1:T(8,128)}, f32[1024,2,64]{0,2,1:T(8,128)}) fusion(f32[1024,64]{0,1:T(8,128)} %copy-done.13, bf16[1024,2,2,64]{0,3,2,1:T(8,128)(2,1)} %bitcast.300, f32[2,1024,1024,2]{2,1,3,0:T(8,128)} %fusion.52, f32[2,1024,1024,2]{2,1,3,0:T(8,128)} %fusion.54, f32[2,2,1024]{2,1,0:T(2,128)S(1)} %copy-done.23, ...), kind=kOutput, calls=%fused_computation.110 | convolution fusion | flops 583406592 | bytes 36454400 | tf_op jit(solution)/shard_map/kgrl,rkgd->lkd/dot_general | solution.py:294
  404.4 1.2 fusion.81
  405.6 1.3 multiply_reduce_fusion.4
  407.7 8.2 %fusion.24 = bf16[2,64,1024]{2,1,0:T(8,128)(2,1)S(1)} fusion(bf16[1024,2,2,64]{0,3,2,1:T(8,128)(2,1)S(1)} %copy-done.8, f32[2,1024,1024,2]{2,1,3,0:T(8,128)} %fusion.54, f32[2,2,1024]{2,1,0:T(2,128)S(1)} %copy-done.23, pred[1024,1024]{0,1:T(8,128)(4,1)S(1)} %copy-done.14), kind=kOutput, calls=%fused_computation.47 | convolution fusion | flops 553779200 | bytes 18628608 | tf_op jit(solution)/shard_map/kgrl,rkgd->lkd/dot_general | solution.py:289
  416.0 2.3 convolution_convert_fusion.5
  419.1 9.7 %convolution_convert_fusion = bf16[1024,2304]{1,0:T(8,128)(2,1)} fusion(bf16[1024,1024]{1,0:T(8,128)(2,1)} %all-gather.6.cloned.1.call-done, bf16[1024,1152]{1,0:T(8,128)(2,1)} %copy-done.31, bf16[1024,1152]{1,0:T(8,128)(2,1)} %copy-done.30), kind=kOutput, calls=%fused_computation.12 | convolution fusion | flops 4843634688 | bytes 11534336 | tf_op jit(solution)/shard_map/ri,rj->ij/dot_general | solution.py:369
  428.9 1.2 copy-done.29
  430.0 2.6 convolution_convert_fusion.4
  432.8 1.1 reshape.270
  433.9 14.1 %reduce-scatter.23.cloned.1.call-done = bf16[128,512]{1,0:T(8,128)(2,1)} async-done(((bf16[1024,512]{1,0:T(8,128)(2,1)}), bf16[128,512]{1,0:T(8,128)(2,1)}) %reduce-scatter.23.cloned.1.call-update) | async-done | bytes 131088 | tf_op jit(solution)/shard_map/reduce_scatter | solution.py:389
  448.0 1.0 reshape.272
  449.0 27.0 %reduce-scatter.21.cloned.1.call-done = bf16[128,256]{1,0:T(8,128)(2,1)} async-done(((bf16[128,1024]{1,0:T(8,128)(2,1)}), bf16[128,256]{1,0:T(8,128)(2,1)}) %reduce-scatter.21.cloned.1.call-update) | async-done | bytes 65552 | tf_op jit(solution)/shard_map/reduce_scatter | solution.py:375
  476.9 54.7 %reduce-scatter.15.cloned.1.call-done = bf16[128,2304]{1,0:T(8,128)(2,1)} async-done(((bf16[1024,2304]{1,0:T(8,128)(2,1)}), bf16[128,2304]{1,0:T(8,128)(2,1)}) %reduce-scatter.15.cloned.1.call-update) | async-done | bytes 589840 | tf_op jit(solution)/shard_map/reduce_scatter | solution.py:371
  531.6 1.8 reshape.269
  533.4 1.1 pad_maximum_fusion.5
  534.9 35.7 %reduce-scatter.13.cloned.1.call-done = bf16[256,1024]{1,0:T(8,128)(2,1)} async-done(((bf16[1024,1024]{1,0:T(8,128)(2,1)}), bf16[256,1024]{1,0:T(8,128)(2,1)}) %reduce-scatter.13.cloned.1.call-update) | async-done | bytes 524304 | tf_op jit(solution)/shard_map/reduce_scatter | solution.py:391
  570.6 1.4 fusion.45
  572.0 40.8 %psum.7 = f32[3,1024]{1,0:T(4,128)S(1)} all-reduce(f32[3,1024]{1,0:T(4,128)S(1)} %pad_maximum_fusion.14), channel_id=1, replica_groups=mesh['dp'=8,'seq'=4] {'dp','seq'}, use_global_device_ids=true, to_apply=%region_17.18 | all-reduce | flops 3072 | bytes 24576 | tf_op jit(solution)/shard_map/psum | solution.py:396
  614.0 2.3 fusion.32
  616.3 11.2 %all-gather.12.cloned.1.call-done = bf16[16896,128]{1,0:T(8,128)(2,1)} async-done(((bf16[4224,128]{1,0:T(8,128)(2,1)}), bf16[16896,128]{1,0:T(8,128)(2,1)}) %all-gather.12.cloned.1.call-update) | async-done | bytes 4325392 | tf_op jit(solution)/shard_map/all_gather | solution.py:407
  627.5 1.8 slice_convert_fusion.3
  629.3 1.1 slice_convert_fusion.2
  632.9 1.4 slice_convert_fusion.1
  634.4 4.3 slice_convert_fusion
  638.7 0.9 reshape.287
  639.6 1.4 copy.74
  641.9 1.7 copy.106
  643.6 1.7 copy.105
  646.1 1.6 reshape.282
  647.7 9.3 %reshape.285 = f32[4,128,2,8,144]{4,3,2,1,0:T(8,128)} reshape(f32[4,2304,128]{2,1,0:T(8,128)} %slice_convert_fusion) | data formatting | bytes 9437184 | tf_op jit(solution)/shard_map/transpose | solution.py:413
  657.0 7.2 %fusion.78 = (f32[1,128,8,4,144]{4,2,0,1,3:T(8,128)}, f32[1,128,8,4,144]{4,2,0,1,3:T(8,128)}) fusion(f32[2,128,8,4,144]{4,2,0,1,3:T(8,128)} %bitcast.288), kind=kLoop, calls=%fused_computation.158 | loop fusion | bytes 9437184 | tf_op jit(solution)/shard_map/slice | solution.py:425
  664.2 3.6 copy.76
  667.8 2.0 copy.78
  669.8 3.7 copy.75
  673.5 2.0 copy.77
  675.4 2.3 pad_maximum_fusion.8
  (143 shorter events, 24.7 us)
Async XLA Ops:
  7.2 89.7 %copy-start = (bf16[576,1024]{1,0:T(8,128)(2,1)S(1)}, bf16[576,1024]{1,0:T(8,128)(2,1)}, u32[]{:S(2)}) copy-start(bf16[576,1024]{1,0:T(8,128)(2,1)} %param.21) | copy-start | bytes 3538948
  7.2 121.6 %all-gather.6.cloned.1.call-start = ((), (), s32[]{:S(2)}) async-start(), calls=%async_computation.9 | async-start | bytes 2621440 | tf_op jit(solution)/shard_map/all_gather | solution.py:346
  12.2 0.6 copy-start.20
  12.8 80.6 %copy-start.12 = (bf16[128,4608]{1,0:T(8,128)(2,1)S(1)}, bf16[128,4608]{1,0:T(8,128)(2,1)}, u32[]{:S(2)}) copy-start(bf16[128,4608]{1,0:T(8,128)(2,1)} %param.19) | copy-start | bytes 3538948
  93.4 87.9 %all-gather.8.cloned.1.call-start = ((), (), s32[]{:S(2)}) async-start(), calls=%async_computation.10 | async-start | bytes 5308416 | tf_op jit(solution)/shard_map/all_gather | solution.py:329
  96.8 117.5 %all-gather.10.cloned.1.call-start = ((), (), s32[]{:S(2)}) async-start(), calls=%async_computation.11 | async-start | bytes 2654208 | tf_op jit(solution)/shard_map/all_gather | solution.py:330
  97.6 171.4 %reduce-scatter.11.cloned.1.call-start = ((), (), s32[]{:S(2)}) async-start(), calls=%async_computation.13 | async-start | bytes 2621440 | tf_op jit(solution)/shard_map/reduce_scatter | solution.py:356
  181.3 46.1 %slice-start = ((s8[4718592]{0:T(1024)(128)(4,1)}), s8[524288]{0:T(1024)(128)(4,1)S(1)}, s32[]{:S(2)}) async-start(s8[4718592]{0:T(1024)(128)(4,1)} %bitcast.329), calls=%async_computation.21 | async-start | bytes 1048576
  214.3 13.0 %slice-start.1 = ((s8[4718592]{0:T(1024)(128)(4,1)}), s8[4194304]{0:T(1024)(128)(4,1)S(1)}, s32[]{:S(2)}) async-start(s8[4718592]{0:T(1024)(128)(4,1)} %bitcast.329), calls=%async_computation.22 | async-start | bytes 8388608
  225.2 1.4 copy-start.30
  225.2 2.2 copy-start.31
  233.6 73.7 %reduce-scatter.9.cloned.1.call-start = ((), (), s32[]{:S(2)}) async-start(), calls=%async_computation.12 | async-start | bytes 2621440 | tf_op jit(solution)/shard_map/reduce_scatter | solution.py:360
  233.7 35.3 %copy-start.2 = (f32[256,1024]{1,0:T(8,128)S(1)}, f32[256,1024]{1,0:T(8,128)}, u32[]{:S(2)}) copy-start(f32[256,1024]{1,0:T(8,128)} %get-tuple-element.22) | copy-start | bytes 3145732
  233.7 73.6 %copy-start.15 = (bf16[1,256,1024]{2,1,0:T(8,128)(2,1)S(1)}, bf16[1,256,1024]{2,1,0:T(8,128)(2,1)}, u32[]{:S(2)}) copy-start(bf16[1,256,1024]{2,1,0:T(8,128)(2,1)} %param.13) | copy-start | bytes 1572868
  233.7 73.6 %copy-start.25 = (f32[256]{0:T(256)S(1)}, f32[256]{0:T(256)}, u32[]{:S(2)}) copy-start(f32[256]{0:T(256)} %get-tuple-element.107) | copy-start | bytes 3076
  240.4 69.3 %copy-start.17 = (bf16[1024,256]{1,0:T(8,128)(2,1)S(1)}, bf16[1024,256]{1,0:T(8,128)(2,1)}, u32[]{:S(2)}) copy-start(bf16[1024,256]{1,0:T(8,128)(2,1)} %get-tuple-element.32) | copy-start | bytes 1572868
  240.4 177.9 %reduce-scatter.19.cloned.1.call-start = ((), (), s32[]{:S(2)}) async-start(), calls=%async_computation.17 | async-start | bytes 2359296 | tf_op jit(solution)/shard_map/reduce_scatter | solution.py:374
  307.3 6.5 copy-start.21
  309.7 7.7 %copy-start.19 = (bf16[256,1024]{1,0:T(8,128)(2,1)S(1)}, bf16[256,1024]{1,0:T(8,128)(2,1)}, u32[]{:S(2)}) copy-start(bf16[256,1024]{1,0:T(8,128)(2,1)} %get-tuple-element.27) | copy-start | bytes 1572868
  309.7 7.7 %copy-start.16 = (bf16[2,1024,64]{2,1,0:T(8,128)(2,1)S(1)}, bf16[2,1024,64]{2,1,0:T(8,128)(2,1)}, u32[]{:S(2)}) copy-start(bf16[2,1024,64]{2,1,0:T(8,128)(2,1)} %get-tuple-element.26) | copy-start | bytes 786436
  313.9 35.5 %copy-start.22 = (f32[2,2,1024]{2,1,0:T(2,128)}, f32[2,2,1024]{2,1,0:T(2,128)S(1)}, u32[]{:S(2)}) copy-start(f32[2,2,1024]{2,1,0:T(2,128)S(1)} %neg.31) | copy-start | bytes 49156
  316.1 58.3 %copy-start.13 = (f32[1024,64]{0,1:T(8,128)}, f32[1024,64]{0,1:T(8,128)S(1)}, u32[]{:S(2)}) copy-start(f32[1024,64]{0,1:T(8,128)S(1)} %get-tuple-element.94) | copy-start | bytes 786436
  317.4 8.1 %copy-start.9 = (bf16[256,1024]{1,0:T(8,128)(2,1)}, bf16[256,1024]{1,0:T(8,128)(2,1)S(1)}, u32[]{:S(2)}) copy-start(bf16[256,1024]{1,0:T(8,128)(2,1)S(1)} %broadcast_multiply_fusion.1) | copy-start | bytes 1572868
  317.4 8.1 %copy-start.6 = (bf16[1024,1024]{1,0:T(8,128)(2,1)S(1)}, bf16[1024,1024]{1,0:T(8,128)(2,1)}, u32[]{:S(2)}) copy-start(bf16[1024,1024]{1,0:T(8,128)(2,1)} %get-tuple-element.30) | copy-start | bytes 6291460
  327.1 11.7 %all-to-all-start = ((bf16[256,4,256]{2,0,1:T(8,128)(2,1)}), bf16[256,4,256]{2,0,1:T(8,128)(2,1)S(1)}, u32[]{:S(2)}, u32[]{:S(2)}) async-start(bf16[256,4,256]{2,0,1:T(8,128)(2,1)} %bitcast.285), calls=%async_computation.2 | async-start | bytes 1048576 | tf_op jit(solution)/shard_map/all_to_all | solution.py:367
  332.0 100.7 %reduce-scatter.17.cloned.1.call-start = ((), (), s32[]{:S(2)}) async-start(), calls=%async_computation.16 | async-start | bytes 2654208 | tf_op jit(solution)/shard_map/reduce_scatter | solution.py:372
  338.4 109.6 %reduce-scatter.23.cloned.1.call-start = ((), (), s32[]{:S(2)}) async-start(), calls=%async_computation.19 | async-start | bytes 1179648 | tf_op jit(solution)/shard_map/reduce_scatter | solution.py:389
  339.5 0.8 copy-start.7
  374.3 1.4 copy-start.3
  374.3 2.0 copy-start.26
  374.6 3.0 copy-start.23
  377.6 28.0 %copy-start.4 = (f32[384,1024]{1,0:T(8,128)S(1)}, f32[384,1024]{1,0:T(8,128)}, u32[]{:S(2)}) copy-start(f32[384,1024]{1,0:T(8,128)} %get-tuple-element.25) | copy-start | bytes 4718596
  377.6 28.0 %copy-start.24 = (f32[64]{0:T(128)S(1)}, f32[64]{0:T(128)}, u32[]{:S(2)}) copy-start(f32[64]{0:T(128)} %get-tuple-element.98) | copy-start | bytes 772
  404.4 3.3 copy-start.8
  404.4 3.3 copy-start.14
  407.7 8.3 %copy-start.18 = (bf16[1024,256]{0,1:T(8,128)(2,1)S(1)}, bf16[1024,256]{0,1:T(8,128)(2,1)}, u32[]{:S(2)}) copy-start(bf16[1024,256]{0,1:T(8,128)(2,1)} %get-tuple-element.79) | copy-start | bytes 1572868
  407.7 8.3 %copy-start.28 = (bf16[1024,1024]{1,0:T(8,128)(2,1)S(1)}, bf16[1024,1024]{1,0:T(8,128)(2,1)}, u32[]{:S(2)}) copy-start(bf16[1024,1024]{1,0:T(8,128)(2,1)} %get-tuple-element.33) | copy-start | bytes 6291460
  418.3 57.7 %reduce-scatter.21.cloned.1.call-start = ((), (), s32[]{:S(2)}) async-start(), calls=%async_computation.18 | async-start | bytes 327680 | tf_op jit(solution)/shard_map/reduce_scatter | solution.py:375
  419.0 112.6 %reduce-scatter.15.cloned.1.call-start = ((), (), s32[]{:S(2)}) async-start(), calls=%async_computation.15 | async-start | bytes 5308416 | tf_op jit(solution)/shard_map/reduce_scatter | solution.py:371
  428.8 1.2 copy-start.29
  428.8 141.8 %reduce-scatter.13.cloned.1.call-start = ((), (), s32[]{:S(2)}) async-start(), calls=%async_computation.14 | async-start | bytes 2621440 | tf_op jit(solution)/shard_map/reduce_scatter | solution.py:391
  432.7 101.9 %copy-start.5 = (bf16[1,256,1024]{2,1,0:T(8,128)(2,1)S(1)}, bf16[1,256,1024]{2,1,0:T(8,128)(2,1)}, u32[]{:S(2)}) copy-start(bf16[1,256,1024]{2,1,0:T(8,128)(2,1)} %param.12) | copy-start | bytes 1572868
  432.7 102.2 %copy-start.27 = (f32[64]{0:T(128)S(1)}, f32[64]{0:T(128)}, u32[]{:S(2)}) copy-start(f32[64]{0:T(128)} %get-tuple-element.87) | copy-start | bytes 772
  432.7 194.8 %all-gather.12.cloned.1.call-start = ((), (), s32[]{:S(2)}) async-start(), calls=%async_computation.20 | async-start | bytes 5406720 | tf_op jit(solution)/shard_map/all_gather | solution.py:407
  634.4 4.3 copy-start.11
  634.4 10.8 %copy-start.10 = (f32[128,4,256]{2,1,0:T(4,128)S(1)}, f32[128,4,256]{2,1,0:T(4,128)}, u32[]{:S(2)}) copy-start(f32[128,4,256]{2,1,0:T(4,128)} %slice.98) | copy-start | bytes 1572868
  669.8 7.9 %copy-start.1 = (bf16[576,1024]{1,0:T(8,128)(2,1)S(1)}, bf16[576,1024]{1,0:T(8,128)(2,1)}, u32[]{:S(2)}) copy-start(bf16[576,1024]{1,0:T(8,128)(2,1)} %param.21) | copy-start | bytes 3538948
Sparse Core Ops, SparseCore 0:
  93.5 35.2 all-gather.5
  131.0 50.2 all-gather.7
  183.5 30.8 all-gather.9
  233.7 35.2 reduce-scatter.10
  272.1 35.1 reduce-scatter.8
  311.9 32.7 reduce-scatter.18
  347.7 34.8 reduce-scatter.16
  418.4 29.5 reduce-scatter.22
  450.8 25.1 reduce-scatter.20
  478.3 53.3 reduce-scatter.14
  535.4 35.1 reduce-scatter.12
  572.9 54.5 all-gather.11

commit v3 on v2

v3 whole, which is shorter than its diff:
```python
import functools

import jax
import jax.numpy as jnp
import numpy as np
from jax import lax
from jax.experimental import pallas as pl
from jax.experimental.pallas import tpu as pltpu
from jax.sharding import PartitionSpec as P

H = 16
KV = 8
HD = 64
EPSILON = 1e-06
THETA_BASE = 1000000.0
F32 = jnp.float32
BF16 = jnp.bfloat16


def rope_columns(length):
    inverse = np.float32(THETA_BASE) ** (-np.arange(0, HD, 2).astype(np.float32) / np.float32(HD))
    angles = (np.arange(length, dtype=np.float32)[None, :] * inverse.astype(np.float32)[:, None]).astype(np.float32)
    angles = angles.astype(np.float64)
    return jnp.asarray(np.cos(angles), F32), jnp.asarray(np.sin(angles), F32)


MESH = pl.DeviceIdType.MESH
DMA = pltpu.SemaphoreType.DMA


def mm(a, b):
    return jnp.dot(a, b, preferred_element_type=F32)


def mm_nt(a, b):
    return lax.dot_general(a, b, (((1,), (1,)), ((), ())), preferred_element_type=F32)


def remote(src, dst, send, recv, device):
    return pltpu.make_async_remote_copy(
        src_ref=src, dst_ref=dst, send_sem=send, recv_sem=recv, device_id=device, device_id_type=MESH
    )


def block_of(index, size):
    return pl.ds(pl.multiple_of(index * size, size), size)


class Place:
    def __init__(self, ns, nd):
        self.ns, self.nd, self.nz = ns, nd, nd // 2
        self.d, self.s = lax.axis_index("dp"), lax.axis_index("seq")
        self.zz, self.core = self.d // 2, lax.rem(self.d, 2)
        self.sib = (self.d + 1 - 2 * self.core, self.s)

    def seq_to(self, j):
        return (self.d, lax.rem(self.s + j, self.ns))

    def seq_from(self, j):
        return lax.rem(self.s + self.ns - j, self.ns)

    def dp_to(self, j):
        return (lax.rem(self.d + j, self.nd), self.s)

    def z_index(self, j):
        return lax.rem(self.zz + j, self.nz)

    def z_from(self, j):
        return lax.rem(self.zz + self.nz - j, self.nz)

    def z_device(self, z):
        return (2 * z + self.core, self.s)

    def greet(self):
        bar = pltpu.get_barrier_semaphore()
        for j in range(1, self.nd):
            pl.semaphore_signal(bar, inc=1, device_id=self.dp_to(j), device_id_type=MESH)
        for j in range(1, self.ns):
            pl.semaphore_signal(bar, inc=1, device_id=self.seq_to(j), device_id_type=MESH)
        pl.semaphore_wait(bar, self.nd + self.ns - 2)


class Gather:
    def __init__(self, at, src, dst, sems):
        self.at, self.src, self.dst = at, src, dst
        self.send, self.recv, self.fsend, self.frecv, self.rsend = sems
        self.rows = src.shape[0]

    def piece(self, z):
        return self.dst.at[block_of(2 * z + self.at.core, self.rows)]

    def direct(self, j):
        at = self.at
        return remote(self.src, self.piece(at.zz), self.send.at[j], self.recv.at[j], at.z_device(at.z_index(j)))

    def near(self, j):
        at = self.at
        away = at.z_index(j) - at.zz
        return (away < at.nz - 1) & (away > 1 - at.nz)

    def across(self, j):
        piece = self.src if j == 0 else self.piece(self.at.z_from(j))
        return remote(piece, self.piece(self.at.z_from(j)), self.fsend.at[j], self.frecv.at[j], self.at.sib)

    def relay(self, j):
        nz = self.at.nz
        legs = []
        if j == nz - 2:
            legs.append((nz - 2, 0, nz - 1, nz - 1, 0))
        if j == 2:
            legs.append((1, nz - 1, 0, 1, 1))
        out = []
        for here, origin, target, index, k in legs:
            piece = self.piece(origin)
            copy = remote(piece, piece, self.rsend.at[k], self.recv.at[index], self.at.z_device(target))
            out.append((self.at.zz == here, copy))
        return out

    def order(self):
        nz = self.at.nz
        return list(range(2, nz - 1)) + [1, nz - 1]

    def start(self):
        at = self.at
        for j in range(1, at.nz):

            @pl.when(self.near(j))
            def _():
                self.direct(j).start()

        self.across(0).start()
        self.dst[block_of(at.d, self.rows), :] = self.src[...]

    def arrive(self):
        for j in self.order():
            self.direct(j).wait_recv()
            for here, copy in self.relay(j):
                pl.when(here)(copy.start)
            self.across(j).start()

    def finish(self):
        for j in range(self.at.nz):
            self.across(j).wait_recv()

    def drain(self):
        for j in range(self.at.nz):
            self.across(j).wait_send()
            if j:
                pl.when(self.near(j))(self.direct(j).wait_send)
                for here, copy in self.relay(j):
                    pl.when(here)(copy.wait_send)


def gather_sems(nz):
    return [DMA((nz,)), DMA((nz,)), DMA((nz,)), DMA((nz,)), DMA((2,))]


def forward_kernel(
    ns, nd, x, gains, wqkv_mine, wout_mine, cot, gu_mine, dn_mine, cos, sin,
    normed, projT, qT, kT, krows, vrows, inv, mixT, mrowsT, wout, wqkv, gsum, gres, osend, oown, guown, dnown, gsecond,
    vT, resid, cotall, xall, gbuf, gu, dn, pre, hrow, hT, gb, gsend, grecv, gown, nmT, gus, gur, dns, dnr,
    xs, xr, gs, gr, cs, cr, ms, mr, ns_, nr, ps, pr, ss, sr, *gsems,
):
    at = Place(ns, nd)
    s, d, nz, core = at.s, at.d, at.nz, at.core
    T, width = x.shape
    L = ns * T
    R = wqkv_mine.shape[0]
    n = dn.shape[0]
    piece = dn_mine.shape[0]
    hq, hk = H // ns, KV // ns
    group = hq // hk
    qw, kw = hq * HD, hk * HD
    own = block_of(s, T)
    at.greet()

    x_copies = [remote(x, xall.at[own], xs.at[j], xr.at[j], at.seq_to(j)) for j in range(1, ns)]
    g_copies = [remote(gains, gbuf.at[d], gs.at[j], gr.at[j], at.dp_to(j)) for j in range(1, nd)]
    c_copies = [remote(cot, cotall.at[own], cs.at[j], cr.at[j], at.seq_to(j)) for j in range(1, ns)]
    take_qkv = Gather(at, wqkv_mine, wqkv, gsems[0:5])
    take_out = Gather(at, wout_mine, wout, gsems[5:10])
    take_gu = Gather(at, gu_mine, gu, gsems[10:15])
    take_dn = Gather(at, dn_mine, dn, gsems[15:20])
    for c in g_copies + x_copies:
        c.start()
    take_qkv.start()
    xall[own, :] = x[...]
    gbuf[d] = gains[...]
    cotall[own, :] = cot[...]
    for c in g_copies:
        c.wait_recv()
    total = gbuf[0]
    for k in range(1, nd):
        total = total + gbuf[k]
    gsum[...] = total
    gain_in, gain_mid = total[0:1, :], total[1:2, :]
    columns = jnp.transpose(total[:, : 2 * HD])
    gain_q, gain_k = columns[:HD, 2:3], columns[HD:, 2:3]
    take_qkv.arrive()
    take_out.start()
    take_gu.start()
    for j in range(ns):
        rows = block_of(at.seq_from(j), T)
        if j:
            x_copies[j - 1].wait_recv()
        xc = xall[rows, :].astype(F32)
        scale = lax.rsqrt(jnp.mean(xc * xc, axis=-1, keepdims=True) + EPSILON)
        normed[rows, :] = (xc * scale * gain_in).astype(BF16)
    for c in c_copies:
        c.start()
    take_qkv.finish()
    for j in range(ns):
        rows = pl.ds(j * T, T)
        proj = mm(normed[rows, :], wqkv[...])
        projT[:, rows] = jnp.transpose(proj[:, : qw + kw])
        val = proj[:, qw + kw :]
        vT[:, rows] = jnp.transpose(val).astype(BF16)
        for i in range(hk):
            vrows[i, rows, :] = val[:, i * HD : (i + 1) * HD].astype(BF16)

    half = HD // 2

    def rope(row, gain, factor):
        u = projT[row, :]
        scale = lax.rsqrt(jnp.mean(u * u, axis=0, keepdims=True) + EPSILON)
        u = u * scale * gain
        a, b = u[:half], u[half:]
        return jnp.concatenate([a * cos[...] - b * sin[...], b * cos[...] + a * sin[...]], axis=0) * factor

    def rope_query(h, carry):
        row = block_of(h, HD)
        qT[row, :] = rope(row, gain_q, HD**-0.5).astype(BF16)
        return carry

    lax.fori_loop(0, hq, rope_query, 0)
    for i in range(hk):
        r = rope(pl.ds(qw + i * HD, HD), gain_k, 1.0)
        kT[i * HD : (i + 1) * HD, :] = r.astype(BF16)
        krows[i, :, :] = jnp.transpose(r).astype(BF16)

    keep = lax.broadcasted_iota(jnp.int32, (T, T), 0) <= lax.broadcasted_iota(jnp.int32, (T, T), 1)
    block = block_of(s, qw)

    def mixed_out(rb):
        return remote(mixT.at[rb], mrowsT.at[block], ms.at[rb], mr.at[s], (d, rb))

    for rb in range(ns):
        cols = pl.ds(rb * T, T)
        span = rb * T

        def head(h, carry):
            kv = h // group
            row, vrow = block_of(h, HD), block_of(kv, HD)
            q = qT[row, cols]
            p = jnp.where(keep, jnp.exp(mm(krows[kv, cols, :], q)), 0.0)
            tot = jnp.sum(p, axis=0, keepdims=True)
            m = mm(vT[vrow, cols], p.astype(BF16))
            if span:
                p = jnp.exp(mm(krows[kv, 0:span, :], q))
                tot = tot + jnp.sum(p, axis=0, keepdims=True)
                m = m + mm(vT[vrow, 0:span], p.astype(BF16))
            one = 1.0 / tot
            inv[h, :, cols] = one
            mixT[rb, row, :] = (m * one).astype(BF16)
            return carry

        lax.fori_loop(0, hq, head, 0)
        pl.when(s != rb)(mixed_out(rb).start)

    take_out.arrive()
    mrowsT[block, :] = mixT[s]
    for j in range(1, ns):
        src = at.seq_from(j)
        remote(mixT.at[0], mrowsT.at[block_of(src, qw)], ms.at[0], mr.at[src], (d, src)).wait_recv()
    take_out.finish()
    residual = x[...].astype(F32) + mm(jnp.transpose(mrowsT[...]), wout[...])
    resid[...] = residual
    scale_mid = lax.rsqrt(jnp.mean(residual * residual, axis=-1, keepdims=True) + EPSILON)
    xall[own, :] = (residual * scale_mid * gain_mid).astype(BF16)
    n_copies = [
        remote(xall.at[own], xall.at[own], ns_.at[j], nr.at[j], at.seq_to(j)) for j in range(1, ns)
    ]
    for c in c_copies:
        c.wait_recv()
    for c in n_copies:
        c.start()
    take_gu.arrive()
    take_dn.start()
    take_gu.finish()

    ft = 384 if n % 384 == 0 else 128
    nt = n // ft
    p_copies = []
    for j in range(ns):
        rows = block_of(at.seq_from(j), T)
        if j:
            n_copies[j - 1].wait_recv()

        def pre_tile(i, carry):
            f = block_of(i, ft)
            pre[:, f] = mm(xall[rows, :], gu[:, f])
            return carry

        lax.fori_loop(0, 2 * nt, pre_tile, 0)
        if j == 0:
            take_dn.arrive()
            take_dn.finish()

        def hidden_tile(i, carry):
            f, f2 = block_of(i, ft), block_of(i + nt, ft)
            gate, up = pre[:, f], pre[:, f2]
            sig = 1.0 / (1.0 + jnp.exp(-gate))
            act = gate * sig
            back = mm_nt(cotall[rows, :], dn[f, :])
            hid = act * up
            hrow[:, f] = hid.astype(BF16)
            hT[f, rows] = jnp.transpose(hid).astype(BF16)
            gb[rows, f] = (back * up * sig * (1.0 + gate * (1.0 - sig))).astype(BF16)
            gb[rows, f2] = (back * act).astype(BF16)
            return carry

        lax.fori_loop(0, nt, hidden_tile, 0)
        wt = 256

        def back_tile(i, carry):
            w = block_of(i, wt)
            part = mm_nt(gb[rows, :], gu[w, :])
            if j:
                gsend[j - 1, :, w] = part.astype(BF16)
            else:
                gown[:, w] = part
            return carry

        lax.fori_loop(0, width // wt, back_tile, 0)
        if j:
            c = remote(gsend.at[j - 1], grecv.at[ns - j - 1], ps.at[j], pr.at[ns - j], at.seq_to(ns - j))
            c.start()
            p_copies.append(c)

        def out_tile(i, carry):
            w = block_of(i, wt)
            part = mm(hrow[...], dn[:, w])
            if j:
                osend[j - 1, :, w] = part.astype(BF16)
            else:
                oown[:, w] = part + resid[:, w]
            return carry

        lax.fori_loop(0, width // wt, out_tile, 0)

    for k in range(nd):
        nmT[k % 2, (k // 2) * R : (k // 2 + 1) * R, :] = jnp.transpose(xall[:, k * R : (k + 1) * R])

    def dn_rows(c, i):
        return hT[block_of(2 * i + c, piece), :]

    def dn_other(i, carry):
        dns[block_of(i, piece), :] = mm(dn_rows(1 - core, i), cotall[...]).astype(BF16)
        return carry

    lax.fori_loop(0, nz, dn_other, 0)
    dn_copy = remote(dns, dnr, ss.at[0], sr.at[0], at.sib)
    dn_copy.start()

    def gu_other(i, carry):
        f = block_of(i, 256)
        gus[:, f] = mm(nmT[1 - core], gb[:, f]).astype(BF16)
        return carry

    lax.fori_loop(0, 2 * n // 256, gu_other, 0)
    gu_copy = remote(gus, gur, ss.at[1], sr.at[1], at.sib)
    gu_copy.start()
    dn_copy.wait_recv()

    def dn_mine_sum(i, carry):
        r = block_of(i, piece)
        dnown[r, :] = (mm(dn_rows(core, i), cotall[...]) + dnr[r, :].astype(F32)).astype(BF16)
        return carry

    lax.fori_loop(0, nz, dn_mine_sum, 0)
    gu_copy.wait_recv()

    def gu_mine_sum(i, carry):
        f = block_of(i, 256)
        guown[:, f] = (mm(nmT[core], gb[:, f]) + gur[:, f].astype(F32)).astype(BF16)
        return carry

    lax.fori_loop(0, 2 * n // 256, gu_mine_sum, 0)

    for c in p_copies:
        c.wait_recv()
    gnm = gown[...]
    for j in range(1, ns):
        gnm = gnm + grecv[j - 1].astype(F32)
    residual = resid[...]
    scale_mid = lax.rsqrt(jnp.mean(residual * residual, axis=-1, keepdims=True) + EPSILON)
    gsecond[...] = jnp.broadcast_to(jnp.sum(gnm * residual * scale_mid, axis=0, keepdims=True), (8, width))
    weighted = gnm * gain_mid
    gres[...] = (
        cot[...].astype(F32)
        + scale_mid * weighted
        - residual * (scale_mid * scale_mid * scale_mid) * jnp.mean(weighted * residual, axis=-1, keepdims=True)
    )
    for rb in range(ns):
        pl.when(s != rb)(mixed_out(rb).wait_send)
    for c in x_copies + g_copies + c_copies + n_copies + p_copies + [dn_copy, gu_copy]:
        c.wait_send()
    for t in (take_qkv, take_out, take_gu, take_dn):
        t.drain()


def vmem(n):
    return [pl.BlockSpec(memory_space=pltpu.VMEM)] * n


def forward(ns, nd, x, gains, wqkv_mine, wout_mine, cot, gu_mine, dn_mine):
    T, width = x.shape
    L = ns * T
    R, n2 = gu_mine.shape
    n = n2 // 2
    piece = dn_mine.shape[0]
    nz = nd // 2
    hq, hk = H // ns, KV // ns
    qw, kw = hq * HD, hk * HD
    cos, sin = rope_columns(L)
    sh, vm = jax.ShapeDtypeStruct, pltpu.VMEM
    outs = (
        sh((L, width), BF16), sh((qw + kw, L), F32), sh((qw, L), BF16), sh((kw, L), BF16),
        sh((hk, L, HD), BF16), sh((hk, L, HD), BF16), sh((hq, 1, L), F32), sh((ns, qw, T), BF16),
        sh((H * HD, T), BF16), sh((H * HD, width), BF16), sh((width, qw + 2 * kw), BF16), sh((8, width), F32),
        sh((T, width), F32), sh((ns - 1, T, width), BF16), sh((T, width), F32),
        sh((nz * R, n2), BF16), sh((nz * piece, width), BF16), sh((8, width), F32),
    )
    scratch = [
        vm((kw, L), BF16), vm((T, width), F32), vm((L, width), BF16), vm((L, width), BF16), vm((nd, 8, width), F32),
        vm((nd * R, n2), BF16), vm((n, width), BF16), vm((T, n2), F32), vm((T, n), BF16), vm((n, L), BF16),
        vm((L, n2), BF16), vm((ns - 1, T, width), BF16), vm((ns - 1, T, width), BF16), vm((T, width), F32),
        vm((2, nz * R, L), BF16), vm((nz * R, n2), BF16), vm((nz * R, n2), BF16),
        vm((nz * piece, width), BF16), vm((nz * piece, width), BF16),
    ]
    sems = [DMA((ns,)), DMA((ns,)), DMA((nd,)), DMA((nd,))] + [DMA((ns,))] * 8 + [DMA((2,)), DMA((2,))]
    return pl.pallas_call(
        functools.partial(forward_kernel, ns, nd),
        out_shape=outs,
        in_specs=vmem(9),
        out_specs=vmem(len(outs)),
        scratch_shapes=scratch + sems + gather_sems(nz) * 4,
        compiler_params=pltpu.CompilerParams(
            collective_id=0, has_side_effects=True, vmem_limit_bytes=60 << 20
        ),
        cost_estimate=pl.CostEstimate(flops=28_000_000_000, bytes_accessed=30_000_000, transcendentals=6_000_000),
    )(x, gains, wqkv_mine, wout_mine, cot, gu_mine, dn_mine, cos, sin)


class Scatter:
    def __init__(self, at, pieces, inbox, final, out, sems):
        self.at, self.pieces, self.inbox, self.final, self.out = at, pieces, inbox, final, out
        self.send, self.recv, self.osend, self.orecv, self.local = sems
        self.rows = final.shape[0]

    def copy(self, j):
        at = self.at
        piece = self.pieces.at[block_of(at.z_index(j), self.rows)]
        return remote(piece, self.inbox.at[j - 1], self.send.at[j], self.recv.at[j], at.z_device(at.z_index(j)))

    def spread(self, j):
        at = self.at
        return remote(self.final, self.out.at[at.s], self.osend.at[j], self.orecv.at[j], at.seq_to(j))

    def keep(self):
        return pltpu.make_async_copy(self.final, self.out.at[self.at.s], self.local.at[0])

    def start(self):
        for j in range(1, self.at.nz):
            self.copy(j).start()

    def total(self):
        for j in range(1, self.at.nz):
            self.copy(j).wait_recv()
        acc = self.pieces[block_of(self.at.zz, self.rows), :].astype(F32)
        for j in range(1, self.at.nz):
            acc = acc + self.inbox[j - 1].astype(F32)
        self.final[...] = acc.astype(BF16)
        self.keep().start()
        for j in range(1, self.at.ns):
            self.spread(j).start()

    def drain(self):
        self.keep().wait()
        for j in range(1, self.at.ns):
            self.spread(j).wait()
        for j in range(1, self.at.nz):
            self.copy(j).wait_send()


def scatter_sems(ns, nz):
    return [DMA((nz,)), DMA((nz,)), DMA((ns,)), DMA((ns,)), DMA((1,))]


def backward_kernel(
    ns, nd, x, normed, projT, qT, kT, krows, vrows, inv, mixT, mrowsT, wout, wqkv, gsum, gres, osend, oown, guown,
    dnown, gsecond, cos, sin,
    outputs, gstream, guall, dnall, qkvall, outall, small,
    guz, guf, dnz, dnf, orecv, gmr, grows, gT, qrows, gk, gv, gqT, gprojT, gproj, nisend, nirecv, niown,
    qk2, qkr, qkown, qkz, qkf, go2, gor, gosend, gorecv, goown, goz, gof, sm0, sm1, sm2, sm3,
    os_, or_, ms, mr, nis, nir, ss, sr, gos, gorc, s1, r1, s2, r2, *sems,
):
    at = Place(ns, nd)
    s, d, nz, core = at.s, at.d, at.nz, at.core
    T, width = x.shape
    L = ns * T
    R = guf.shape[0]
    hq, hk = H // ns, KV // ns
    group = hq // hk
    qw, kw = hq * HD, hk * HD
    half = HD // 2
    own = block_of(s, T)
    at.greet()
    dn_sum = Scatter(at, dnown, dnz, dnf, dnall, sems[0:5])
    gu_sum = Scatter(at, guown, guz, guf, guall, sems[5:10])
    qkv_sum = Scatter(at, qkown, qkz, qkf, qkvall, sems[10:15])
    out_sum = Scatter(at, goown, goz, gof, outall, sems[15:20])
    dn_sum.start()
    gu_sum.start()

    rback = gres[...].astype(BF16)

    def mixed_back(p):
        return remote(gmr.at[p], grows.at[own], ms.at[p], mr.at[s], (d, p))

    for p in range(ns):
        gmr[p] = mm_nt(rback, wout[p * qw : (p + 1) * qw, :]).astype(BF16)
        pl.when(s != p)(mixed_back(p).start)
    grows[own, :] = gmr[s]

    for k in range(nd):
        go2[k % 2, (k // 2) * R : (k // 2 + 1) * R, :] = mm(mrowsT[k * R : (k + 1) * R, :], rback).astype(BF16)
    go_copy = remote(go2.at[1 - core], gor, ss.at[0], sr.at[0], at.sib)
    go_copy.start()
    for i in range(hk):
        qrows[i, :, :] = jnp.transpose(qT[i * group * HD : (i + 1) * group * HD, :])
    go_copy.wait_recv()
    cw = width // ns
    for p in range(ns):
        c = pl.ds(p * cw, cw)
        gosend[p] = (go2[core, :, c].astype(F32) + gor[:, c].astype(F32)).astype(BF16)

    for j in range(1, ns):
        src = at.seq_from(j)
        remote(gmr.at[0], grows.at[block_of(src, T)], ms.at[0], mr.at[src], (d, src)).wait_recv()
    for i in range(ns):
        rows = pl.ds(i * T, T)
        gT[:, rows] = jnp.transpose(grows[rows, :])

    def gout_copy(j):
        return remote(gosend.at[at.seq_to(j)[1]], gorecv.at[j - 1], gos.at[j], gorc.at[j], at.seq_to(j))

    def out_copy(j):
        return remote(osend.at[j - 1], orecv.at[ns - j - 1], os_.at[j], or_.at[ns - j], at.seq_to(ns - j))

    for j in range(1, ns):
        gout_copy(j).start()
    for j in range(1, ns):
        out_copy(j).start()

    causal = lax.broadcasted_iota(jnp.int32, (T, T), 0) <= lax.broadcasted_iota(jnp.int32, (T, T), 1)
    causal = jnp.concatenate([causal] * group, axis=1)
    gk[...] = jnp.zeros_like(gk)
    gv[...] = jnp.zeros_like(gv)

    def key_head(kv, carry):
        krow = block_of(kv, HD)
        lanes = block_of(kv, group * HD)
        for rb in range(ns):
            cols = pl.ds(rb * T, T)

            def side(ref):
                return jnp.concatenate(
                    [ref[block_of(kv * group + u, HD), cols] for u in range(group)], axis=1
                )

            q, g = side(qT), side(gT)
            one = jnp.concatenate([inv[kv * group + u, :, cols] for u in range(group)], axis=1)
            m = jnp.concatenate(
                [mixT[rb, block_of(kv * group + u, HD), :] for u in range(group)], axis=1
            )
            delta = jnp.sum(g.astype(F32) * m.astype(F32), axis=0, keepdims=True)
            gr, qr = grows[cols, lanes], qrows[kv, cols, :]
            gr = jnp.concatenate([gr[:, u * HD : (u + 1) * HD] for u in range(group)], axis=0)
            qr = jnp.concatenate([qr[:, u * HD : (u + 1) * HD] for u in range(group)], axis=0)
            gq = jnp.zeros((HD, group * T), F32)
            for part, masked in ((pl.ds(0, rb * T), False), (cols, True)):
                if rb == 0 and not masked:
                    continue
                p = jnp.exp(mm(krows[kv, part, :], q)) * one
                if masked:
                    p = jnp.where(causal, p, 0.0)
                gp = mm(vrows[kv, part, :], g)
                ds = (p * (gp - delta)).astype(BF16)
                gv[kv, part, :] += mm(p.astype(BF16), gr)
                gk[kv, part, :] += mm(ds, qr)
                gq = gq + mm(kT[krow, part], ds)
            gq = gq * HD**-0.5
            for u in range(group):
                gqT[block_of(kv * group + u, HD), cols] = gq[:, u * T : (u + 1) * T]
        return carry

    lax.fori_loop(0, hk, key_head, 0)

    columns = jnp.transpose(gsum[:, : 2 * HD])
    gain_q, gain_k = columns[:HD, 2:3], columns[HD:, 2:3]

    def norm_column(row, g, gain):
        a, b = g[:half], g[half:]
        g = jnp.concatenate([a * cos[...] + b * sin[...], b * cos[...] - a * sin[...]], axis=0)
        u = projT[row, :]
        scale = lax.rsqrt(jnp.mean(u * u, axis=0, keepdims=True) + EPSILON)
        us = u * scale
        weighted = g * gain
        inner = jnp.mean(weighted * us, axis=0, keepdims=True)
        gprojT[row, :] = (scale * (weighted - us * inner)).astype(BF16)
        return jnp.sum(g * us, axis=1, keepdims=True)

    def query_back(h, acc):
        row = block_of(h, HD)
        return acc + norm_column(row, gqT[row, :], gain_q)

    gain_grad_q = lax.fori_loop(0, hq, query_back, jnp.zeros((HD, 1), F32))
    gain_grad_k = jnp.zeros((HD, 1), F32)
    for i in range(hk):
        gain_grad_k = gain_grad_k + norm_column(pl.ds(qw + i * HD, HD), jnp.transpose(gk[i]), gain_k)
        gprojT[qw + kw + i * HD : qw + kw + (i + 1) * HD, :] = jnp.transpose(gv[i]).astype(BF16)

    def ni_copy(j):
        return remote(nisend.at[j - 1], nirecv.at[j - 1], nis.at[j], nir.at[j], at.seq_to(j))

    for i in range(ns):
        rows = pl.ds(i * T, T)
        gproj[rows, :] = jnp.transpose(gprojT[:, rows])
    for j in list(range(1, ns)) + [0]:
        part = mm_nt(gproj[block_of(at.seq_to(j)[1], T), :], wqkv[...])
        if j:
            nisend[j - 1] = part.astype(BF16)
            ni_copy(j).start()
        else:
            niown[...] = part
    for k in range(nd):
        part = mm(gprojT[...], normed[:, k * R : (k + 1) * R])
        qk2[k % 2, (k // 2) * R : (k // 2 + 1) * R, :] = jnp.transpose(part).astype(BF16)
    qk_copy = remote(qk2.at[1 - core], qkr, ss.at[1], sr.at[1], at.sib)
    qk_copy.start()
    for j in range(1, ns):
        gout_copy(j).wait_recv()
    acc = gosend[s].astype(F32)
    for j in range(1, ns):
        acc = acc + gorecv[j - 1].astype(F32)
    goown[...] = acc.astype(BF16)
    out_sum.start()
    qk_copy.wait_recv()
    qkown[...] = (qk2[core].astype(F32) + qkr[...].astype(F32)).astype(BF16)
    qkv_sum.start()
    dn_sum.total()

    for j in range(1, ns):
        ni_copy(j).wait_recv()
    gni = niown[...]
    for j in range(1, ns):
        gni = gni + nirecv[j - 1].astype(F32)
    stream = x[...].astype(F32)
    scale = lax.rsqrt(jnp.mean(stream * stream, axis=-1, keepdims=True) + EPSILON)
    unit = stream * scale
    weighted = gni * gsum[0:1, :]
    gstream[...] = gres[...] + scale * (weighted - unit * jnp.mean(weighted * unit, axis=-1, keepdims=True))
    first = jnp.sum(gni * unit, axis=0, keepdims=True)
    qk = jnp.broadcast_to(jnp.concatenate([gain_grad_q, gain_grad_k], axis=0), (2 * HD, 128))
    sm0[0:1, :] = first
    sm0[1:2, :] = gsecond[0:1, :]
    sm0[2:8, :] = jnp.zeros((6, width), F32)
    sm0[2:3, : 2 * HD] = jnp.transpose(qk)[0:1, :]

    def small_seq(j):
        return remote(sm0, sm1.at[j - 1], s1.at[j], r1.at[j], at.seq_to(j))

    def small_dp(j):
        return remote(sm2, sm3.at[j - 1], s2.at[j], r2.at[j], at.dp_to(j))

    for j in range(1, ns):
        small_seq(j).start()
    for j in range(1, ns):
        out_copy(j).wait_recv()
    acc = oown[...]
    for j in range(1, ns):
        acc = acc + orecv[j - 1].astype(F32)
    outputs[...] = acc.astype(BF16)
    for j in range(1, ns):
        small_seq(j).wait_recv()
    acc = sm0[...]
    for j in range(1, ns):
        acc = acc + sm1[j - 1]
    sm2[...] = acc
    for j in range(1, nd):
        small_dp(j).start()
    out_sum.total()
    qkv_sum.total()
    gu_sum.total()
    for j in range(1, nd):
        small_dp(j).wait_recv()
    for j in range(1, nd):
        acc = acc + sm3[j - 1]
    small[...] = acc

    for p in range(ns):
        pl.when(s != p)(mixed_back(p).wait_send)
    go_copy.wait_send()
    qk_copy.wait_send()
    for j in range(1, ns):
        gout_copy(j).wait_send()
        out_copy(j).wait_send()
        ni_copy(j).wait_send()
        small_seq(j).wait_send()
    for j in range(1, nd):
        small_dp(j).wait_send()
    for t in (dn_sum, out_sum, qkv_sum, gu_sum):
        t.drain()


def backward(ns, nd, piece, x, normed, projT, qT, kT, krows, vrows, inv, mixT, mrowsT, wout, wqkv, gsum, gres, osend,
             oown, guown, dnown, gsecond):
    T, width = x.shape
    L = ns * T
    nz = nd // 2
    n2 = guown.shape[1]
    R = guown.shape[0] // nz
    hq, hk = H // ns, KV // ns
    qw, kw = hq * HD, hk * HD
    pw = qw + 2 * kw
    cw = width // ns
    cos, sin = rope_columns(L)
    sh, vm = jax.ShapeDtypeStruct, pltpu.VMEM
    outs = (
        sh((T, width), BF16), sh((T, width), F32), sh((ns, R, n2), BF16), sh((ns, piece, width), BF16),
        sh((ns, R, pw), BF16), sh((ns, R, cw), BF16), sh((8, width), F32),
    )
    hbm = pl.BlockSpec(memory_space=pl.ANY)
    scratch = [
        vm((nz - 1, R, n2), BF16), vm((R, n2), BF16), vm((nz - 1, piece, width), BF16), vm((piece, width), BF16),
        vm((ns - 1, T, width), BF16), vm((ns, T, qw), BF16), vm((L, qw), BF16), vm((qw, L), BF16),
        vm((hk, L, qw // hk), BF16), vm((hk, L, HD), F32), vm((hk, L, HD), F32), vm((qw, L), F32), vm((pw, L), BF16),
        vm((L, pw), BF16), vm((ns - 1, T, width), BF16), vm((ns - 1, T, width), BF16), vm((T, width), F32),
        vm((2, nz * R, pw), BF16), vm((nz * R, pw), BF16), vm((nz * R, pw), BF16), vm((nz - 1, R, pw), BF16),
        vm((R, pw), BF16), vm((2, nz * R, width), BF16), vm((nz * R, width), BF16), vm((ns, nz * R, cw), BF16),
        vm((ns - 1, nz * R, cw), BF16), vm((nz * R, cw), BF16), vm((nz - 1, R, cw), BF16), vm((R, cw), BF16),
        vm((8, width), F32), vm((ns - 1, 8, width), F32), vm((8, width), F32), vm((nd - 1, 8, width), F32),
    ]
    sems = [DMA((ns,))] * 6 + [DMA((2,)), DMA((2,))] + [DMA((ns,))] * 4 + [DMA((nd,)), DMA((nd,))]
    return pl.pallas_call(
        functools.partial(backward_kernel, ns, nd),
        out_shape=outs,
        in_specs=vmem(21),
        out_specs=vmem(2) + [hbm] * 4 + vmem(1),
        scratch_shapes=scratch + sems + scatter_sems(ns, nz) * 4,
        compiler_params=pltpu.CompilerParams(
            collective_id=1, has_side_effects=True, vmem_limit_bytes=60 << 20
        ),
        cost_estimate=pl.CostEstimate(flops=10_000_000_000, bytes_accessed=30_000_000, transcendentals=6_000_000),
    )(x, normed, projT, qT, kT, krows, vrows, inv, mixT, mrowsT, wout, wqkv, gsum, gres, osend, oown, guown, dnown,
      gsecond, cos, sin)


def finish_kernel(ns, nd, piece, guall, qkvall, outall, gate, up, qkv, out):
    hq, hk = H // ns, KV // ns
    qw, kw = hq * HD, hk * HD
    pad = guall.shape[2] // 2 // nd
    parts = [guall[i].astype(F32) for i in range(ns)]
    for ref, base in ((gate, 0), (up, nd * pad)):
        ref[...] = jnp.concatenate(
            [parts[i][:, base + k * pad : base + k * pad + piece] for k in range(nd) for i in range(ns)], axis=1
        )
    parts = [qkvall[i].astype(F32) for i in range(ns)]
    qkv[...] = jnp.concatenate(
        [p[:, :qw] for p in parts] + [p[:, qw : qw + kw] for p in parts] + [p[:, qw + kw :] for p in parts], axis=1
    )
    out[...] = jnp.concatenate([outall[i].astype(F32) for i in range(ns)], axis=1)


def finish(ns, nd, piece, guall, qkvall, outall):
    R = guall.shape[1]
    rows = R // 4
    ff = ns * nd * piece
    widths = (ff, ff, ns * qkvall.shape[2], ns * outall.shape[2])
    return pl.pallas_call(
        functools.partial(finish_kernel, ns, nd, piece),
        grid=(4,),
        out_shape=[jax.ShapeDtypeStruct((R, w), F32) for w in widths],
        in_specs=[pl.BlockSpec((ns, rows, a.shape[2]), lambda i: (0, i, 0)) for a in (guall, qkvall, outall)],
        out_specs=[pl.BlockSpec((rows, w), lambda i: (i, 0)) for w in widths],
        compiler_params=pltpu.CompilerParams(vmem_limit_bytes=40 << 20),
    )(guall, qkvall, outall)


def shards(inputs, cotangent, first_gain, w_qkv, qk_gain, w_out, second_gain, w_gate, w_up, w_down):
    width = inputs.shape[2]
    ns, nd = lax.axis_size("seq"), lax.axis_size("dp")
    s, d = lax.axis_index("seq"), lax.axis_index("dp")
    qw, kw = H // ns * HD, KV // ns * HD
    piece = w_down.shape[0] // ns
    pad = -piece % 16

    qkv_mine = jnp.concatenate(
        [
            lax.dynamic_slice_in_dim(w_qkv, s * qw, qw, 1),
            lax.dynamic_slice_in_dim(w_qkv, H * HD + s * kw, kw, 1),
            lax.dynamic_slice_in_dim(w_qkv, (H + KV) * HD + s * kw, kw, 1),
        ],
        axis=1,
    )

    def slice_ff(w):
        w = w.reshape(w.shape[0], nd, ns, piece)[:, :, s, :]
        return jnp.pad(w, ((0, 0), (0, 0), (0, pad))).reshape(w.shape[0], nd * (piece + pad))

    gu_mine = jnp.concatenate([slice_ff(w_gate), slice_ff(w_up)], axis=1)
    dn_mine = jnp.pad(lax.dynamic_slice_in_dim(w_down, s * piece, piece, 0), ((0, pad), (0, 0)))
    gains = jnp.zeros((8, width), F32)
    gains = lax.dynamic_update_slice(gains, first_gain[None], (0, d * first_gain.shape[0]))
    gains = lax.dynamic_update_slice(gains, second_gain[None], (1, d * second_gain.shape[0]))
    gains = lax.dynamic_update_slice(gains, qk_gain[None], (2, d * qk_gain.shape[0]))
    x = inputs[0]
    kept = forward(ns, nd, x, gains, qkv_mine, w_out, cotangent[0], gu_mine, dn_mine)
    outputs, gstream, guall, dnall, qkvall, outall, small = backward(ns, nd, piece + pad, x, *kept)
    gate, up, qkv, out = finish(ns, nd, piece, guall, qkvall, outall)
    down = dnall[:, :piece].reshape(w_down.shape).astype(F32)
    gl, ql = first_gain.shape[0], qk_gain.shape[0]
    first = lax.dynamic_slice(small, (0, d * gl), (1, gl))[0]
    second = lax.dynamic_slice(small, (1, d * gl), (1, gl))[0]
    qk = lax.dynamic_slice(small, (2, d * ql), (1, ql))[0]
    return (outputs[None], gstream[None], first, qkv, qk, out, second, gate, up, down)


def solution(mesh):
    act = P("dp", "seq", None)
    vec, mat = P("dp"), P("dp", None)
    in_specs = (act, act, vec, mat, vec, mat, vec, mat, mat, mat)
    out_specs = (act, act, vec, mat, vec, mat, vec, mat, mat, mat)
    return jax.shard_map(shards, mesh=mesh, in_specs=in_specs, out_specs=out_specs, check_vma=False)
```

time: 694 us -> 328 us (0.47); the launches traced: 685 us -> 326 us
  waiting for transfers between devices: 315 us -> 0 us
  Pallas kernels: 75.6 us -> 305 us
  matrix products: 135 us -> 0 us
  local copies, waits for them, and re-layouts: 64.2 us -> 15.6 us
  blocking collectives: 40.8 us -> 0 us
  other arithmetic: 33.1 us -> 4.64 us
  between operations: 15.3 us -> 0.77 us
    pallas_call x1 -> x3, Pallas kernels: 75.6 us -> 305 us  [the longest x1 156 us: forward(): pl.pallas_call(functools.partial(forward_kernel, ns, nd), out_shape=outs,...]
    reduce_scatter x8 -> x0, waiting for transfers between devices: 197 us -> none  [the longest x1 54.7 us: shards(): gg = lax.psum_scatter(gg, 'dp', scatter_dimension=0, tiled=True)]
    dot_general x15 -> x0, matrix products: 135 us -> none  [the longest x1 26.8 us: attend_backward(): gk = jnp.einsum('kgrl,rkgd->lkd', gs, q, preferred_element_type=F32)]
    all_gather x4 -> x0, waiting for transfers between devices: 117 us -> none  [the longest x1 52.4 us: shards(): ffn = lax.all_gather(ffn, 'dp', axis=0, tiled=True)]
    psum x1 -> x0, blocking collectives: 40.8 us -> none  [shards(): small = lax.psum(small, ('dp', 'seq'))]
    slice x7 -> x0, local copies, waits for them, and re-layouts: 18.1 us -> none  [the longest x2 10.8 us: shards(): gg[1]]
    unnamed x76 -> x20, local copies, waits for them, and re-layouts: 17.4 us -> 4.83 us
    transpose x3 -> x0, local copies, waits for them, and re-layouts: 10.1 us -> none  [the longest x1 9.28 us: shards(): gg = gg.transpose(2, 1, 3, 0, 4).reshape(2, rows, ff)]
  transfers between devices with their start and end apart: 13 -> 0, of which waited for: 11 -> 0; matrix products, arithmetic and copies ran while one was open for 21% -> 0% of each run, Pallas kernels for 0% -> 0%
where the time goes in v3:
time: 328 us; the launch traced here: 326 us
  Pallas kernels  305 us (93%)
  local copies, waits for them, and re-layouts  15.6 us (5%)
  other arithmetic  4.64 us (1%)
    pallas_call x1, Pallas kernels, forward(): pl.pallas_call(functools.partial(forward_kernel, ns, nd), out_shape=outs,...  156 us
    pallas_call x1, Pallas kernels, backward(): pl.pallas_call(functools.partial(backward_kernel, ns, nd), out_shape=outs...  146 us

profile of v3, /device:TPU:30, one launch (start us, length us, event | category | flops | bytes accessed | tf_op | source)
XLA Modules:
  0.0 326.2 jit_solution(8786516473361833929)
XLA Ops:
  0.6 0.0 copy-start
  0.7 0.0 copy-start.4
  0.7 0.9 dynamic_update_slice.9
  1.6 0.8 dynamic_update_slice.10
  2.4 0.9 dynamic_update_slice.11.gains
  3.4 0.0 copy-start.7
  3.4 0.8 constant_dynamic-slice_fusion.5
  4.2 0.8 constant_dynamic-slice_fusion.6
  5.0 0.7 pad_maximum_fusion.1.wqkv_mine
  5.7 0.0 copy-done.7
  5.7 0.0 copy-done
  5.7 0.7 constant_dynamic-slice_fusion.1.dn_mine
  6.4 0.0 copy-done.4
  6.4 0.7 copy.26
  7.1 1.7 copy.27
  8.8 0.9 constant_dynamic-slice_fusion.2
  9.7 1.2 copy.29
  10.9 1.2 copy.28
  12.0 0.9 pad_maximum_fusion.gu_mine
  12.9 155.8 %shard_map.213 = (bf16[1024,1024]{1,0:T(8,128)(2,1)}, f32[384,1024]{1,0:T(8,128)}, bf16[256,1024]{1,0:T(8,128)(2,1)}, bf16[128,1024]{1,0:T(8,128)(2,1)}, bf16[2,...) custom-call(bf16[256,1024]{1,0:T(8,128)(2,1)} %bitcast.30, ...), custom_call_target="tpu_custom_call" | custom-call | flops 28000000000 | bytes 30000000 | tf_op jit(solution)/shard_map/pallas_call | solution.py:442
  168.7 145.9 %shard_map.214 = (bf16[256,1024]{1,0:T(8,128)(2,1)}, f32[256,1024]{1,0:T(8,128)}, bf16[4,128,2304]{2,1,0:T(8,128)(2,1)}, bf16[4,144,1024]{2,1,0:T(8,128)(2,1)}, ...) custom-call(bf16[256,1024]{1,0:T(8,128)(2,1)} %bitcast.31, ...), custom_call_target="tpu_custom_call" | custom-call | flops 10000000000 | bytes 30000000 | tf_op jit(solution)/shard_map/pallas_call | solution.py:756
  314.7 1.3 dynamic-slice_bitcast_fusion.1
  315.9 1.3 dynamic-slice_bitcast_fusion
  317.3 0.0 copy-start.1
  317.3 0.0 copy-start.2
  317.3 0.0 copy-start.3
  317.3 3.1 bitcast_convert_fusion
  320.4 0.0 copy-done.1
  320.4 0.0 copy-done.2
  320.4 0.0 copy-done.3
  320.4 0.0 copy-start.6
  320.4 3.4 %shard_map.215 = (f32[128,4608]{1,0:T(8,128)}, f32[128,4608]{1,0:T(8,128)}, f32[128,2048]{1,0:T(8,128)}, f32[128,1024]{1,0:T(8,128)}) custom-call(bf16[4,128,2304]{2,1,0:T(8,128)(2,1)S(1)} %copy-done.1, bf16[4,128,512]{2,1,0:T(8,128)(2,1)S(1)} %copy-done.2, bf16[4,128,256]{2,1,0:T(8,128)(2,1)S(1)} %copy-done.3), custom_call_target="tpu_custom_call" | custom-call | tf_op jit(solution)/shard_map/pallas_call | solution.py:791
  323.8 0.0 copy-start.5
  323.8 0.0 copy-done.6
  323.8 0.8 copy.35
  324.6 0.6 copy-done.5
  325.2 1.0 copy.36
  (1 shorter events, 0.0 us)
Async XLA Ops:
  0.6 5.0 %copy-start = (bf16[576,1024]{1,0:T(8,128)(2,1)S(1)}, bf16[576,1024]{1,0:T(8,128)(2,1)}, u32[]{:S(2)}) copy-start(bf16[576,1024]{1,0:T(8,128)(2,1)} %param.23) | copy-start | bytes 3538948
  0.7 5.8 %copy-start.4 = (bf16[128,4608]{1,0:T(8,128)(2,1)S(1)}, bf16[128,4608]{1,0:T(8,128)(2,1)}, u32[]{:S(2)}) copy-start(bf16[128,4608]{1,0:T(8,128)(2,1)} %param.21) | copy-start | bytes 3538948
  3.4 2.3 copy-start.7
  317.3 3.1 copy-start.1
  317.3 3.1 copy-start.2
  317.3 3.1 copy-start.3
  320.4 3.4 %copy-start.6 = (bf16[256,1024]{1,0:T(8,128)(2,1)S(1)}, bf16[256,1024]{1,0:T(8,128)(2,1)}, u32[]{:S(2)}) copy-start(bf16[256,1024]{1,0:T(8,128)(2,1)} %get-tuple-element.57) | copy-start | bytes 1572868
  323.8 1.4 copy-start.5

commit v4 on v3

v4 whole, which is shorter than its diff:
```python
import functools

import jax
import jax.numpy as jnp
import numpy as np
from jax import lax
from jax.experimental import pallas as pl
from jax.experimental.pallas import tpu as pltpu
from jax.sharding import PartitionSpec as P

H = 16
KV = 8
HD = 64
EPSILON = 1e-06
THETA_BASE = 1000000.0
F32 = jnp.float32
BF16 = jnp.bfloat16
VMEM_LIMIT = 61 << 20


def rope_columns(length):
    inverse = np.float32(THETA_BASE) ** (-np.arange(0, HD, 2).astype(np.float32) / np.float32(HD))
    angles = (np.arange(length, dtype=np.float32)[None, :] * inverse.astype(np.float32)[:, None]).astype(np.float32)
    angles = angles.astype(np.float64)
    return jnp.asarray(np.cos(angles), F32), jnp.asarray(np.sin(angles), F32)


MESH = pl.DeviceIdType.MESH
DMA = pltpu.SemaphoreType.DMA


def mm(a, b):
    return jnp.dot(a, b, preferred_element_type=F32)


def mm_nt(a, b):
    return lax.dot_general(a, b, (((1,), (1,)), ((), ())), preferred_element_type=F32)


def remote(src, dst, send, recv, device):
    return pltpu.make_async_remote_copy(
        src_ref=src, dst_ref=dst, send_sem=send, recv_sem=recv, device_id=device, device_id_type=MESH
    )


def block_of(index, size):
    return pl.ds(pl.multiple_of(index * size, size), size)


class Place:
    def __init__(self, ns, nd):
        self.ns, self.nd, self.nz = ns, nd, nd // 2
        self.d, self.s = lax.axis_index("dp"), lax.axis_index("seq")
        self.zz, self.core = self.d // 2, lax.rem(self.d, 2)
        self.sib = (self.d + 1 - 2 * self.core, self.s)

    def seq_to(self, j):
        return (self.d, lax.rem(self.s + j, self.ns))

    def seq_from(self, j):
        return lax.rem(self.s + self.ns - j, self.ns)

    def dp_to(self, j):
        return (lax.rem(self.d + j, self.nd), self.s)

    def z_index(self, j):
        return lax.rem(self.zz + j, self.nz)

    def z_from(self, j):
        return lax.rem(self.zz + self.nz - j, self.nz)

    def z_device(self, z):
        return (2 * z + self.core, self.s)

    def greet(self):
        bar = pltpu.get_barrier_semaphore()
        for j in range(1, self.nd):
            pl.semaphore_signal(bar, inc=1, device_id=self.dp_to(j), device_id_type=MESH)
        for j in range(1, self.ns):
            pl.semaphore_signal(bar, inc=1, device_id=self.seq_to(j), device_id_type=MESH)
        pl.semaphore_wait(bar, self.nd + self.ns - 2)


class Gather:
    def __init__(self, at, src, dst, sems, relayed=True):
        self.at, self.src, self.dst, self.relayed = at, src, dst, relayed
        self.send, self.recv, self.fsend, self.frecv, self.rsend, self.local = sems
        self.rows = src.shape[0]

    def piece(self, z):
        return self.dst.at[block_of(2 * z + self.at.core, self.rows)]

    def direct(self, j):
        at = self.at
        return remote(self.src, self.piece(at.zz), self.send.at[j], self.recv.at[j], at.z_device(at.z_index(j)))

    def near(self, j):
        at = self.at
        away = at.z_index(j) - at.zz
        return (away < at.nz - 1) & (away > 1 - at.nz) if self.relayed else away != 0

    def across(self, j):
        piece = self.src if j == 0 else self.piece(self.at.z_from(j))
        return remote(piece, self.piece(self.at.z_from(j)), self.fsend.at[j], self.frecv.at[j], self.at.sib)

    def relay(self, j):
        nz = self.at.nz
        legs = []
        if not self.relayed:
            return legs
        if j == nz - 2:
            legs.append((nz - 2, 0, nz - 1, nz - 1, 0))
        if j == 2:
            legs.append((1, nz - 1, 0, 1, 1))
        out = []
        for here, origin, target, index, k in legs:
            piece = self.piece(origin)
            copy = remote(piece, piece, self.rsend.at[k], self.recv.at[index], self.at.z_device(target))
            out.append((self.at.zz == here, copy))
        return out

    def order(self):
        nz = self.at.nz
        return list(range(2, nz - 1)) + [1, nz - 1]

    def start(self):
        at = self.at
        for j in range(1, at.nz):

            @pl.when(self.near(j))
            def _():
                self.direct(j).start()

        self.across(0).start()
        self.mine().start()

    def mine(self):
        return pltpu.make_async_copy(self.src, self.dst.at[block_of(self.at.d, self.rows)], self.local.at[0])

    def arrive(self):
        for j in self.order():
            self.direct(j).wait_recv()
            for here, copy in self.relay(j):
                pl.when(here)(copy.start)
            self.across(j).start()

    def finish(self):
        for j in range(self.at.nz):
            self.across(j).wait_recv()
        self.mine().wait()

    def drain(self):
        for j in range(self.at.nz):
            self.across(j).wait_send()
            if j:
                pl.when(self.near(j))(self.direct(j).wait_send)
                for here, copy in self.relay(j):
                    pl.when(here)(copy.wait_send)


def gather_sems(nz):
    return [DMA((nz,)), DMA((nz,)), DMA((nz,)), DMA((nz,)), DMA((2,)), DMA((1,))]


class Scatter:
    def __init__(self, at, pieces, inbox, final, out, sems):
        self.at, self.pieces, self.inbox, self.final, self.out = at, pieces, inbox, final, out
        self.send, self.recv, self.osend, self.orecv, self.local = sems
        self.rows = final.shape[0]

    def copy(self, j):
        at = self.at
        piece = self.pieces.at[block_of(at.z_index(j), self.rows)]
        return remote(piece, self.inbox.at[j - 1], self.send.at[j], self.recv.at[j], at.z_device(at.z_index(j)))

    def spread(self, j):
        at = self.at
        return remote(self.final, self.out.at[at.s], self.osend.at[j], self.orecv.at[j], at.seq_to(j))

    def keep(self):
        return pltpu.make_async_copy(self.final, self.out.at[self.at.s], self.local.at[0])

    def start(self):
        for j in range(1, self.at.nz):
            self.copy(j).start()

    def total(self):
        for j in range(1, self.at.nz):
            self.copy(j).wait_recv()
        acc = self.pieces[block_of(self.at.zz, self.rows), :].astype(F32)
        for j in range(1, self.at.nz):
            acc = acc + self.inbox[j - 1].astype(F32)
        self.final[...] = acc.astype(BF16)
        self.keep().start()
        for j in range(1, self.at.ns):
            self.spread(j).start()

    def drain(self):
        self.keep().wait()
        for j in range(1, self.at.ns):
            self.spread(j).wait()
        for j in range(1, self.at.nz):
            self.copy(j).wait_send()


def scatter_sems(ns, nz):
    return [DMA((nz,)), DMA((nz,)), DMA((ns,)), DMA((ns,)), DMA((1,))]


def block_kernel(
    ns, nd, x, gain1, gain2, gainqk, wqkv_rows, wout_mine, cot, wgate, wup, wdown, cos, sin,
    outputs, gstream, gateall, upall, dnall, qkvall, outall, small,
    normed, projT, qT, kT, krows, vrows, inv, mixT, mrowsT, wout, wqkv, gsum, osend, oown, gsecond,
    vT, resid, cotall, xall, gains, gbuf, wqkv_mine, gu_mine, gu, dn, hrow, hT, gb, gsend, grecv, gown, nmT,
    gur, uur, dnr,
    gaz, gaf, upz, upf, dnz, dnf, gmr, grows, qrows, gk, gv, gqT, qkr, qkown, qkz, qkf,
    gor, gorecv, goown, goz, gof, sm0, sm1, sm2, sm3,
    xs, xr, gs, gr, cs, cr, ms, mr, ns_, nr, ps, pr, ss, sr, loc, wl,
    os_, or_, bs, br, nis, nir, ss2, sr2, gos, gorc, s1, r1, s2, r2, *sems,
):
    at = Place(ns, nd)
    s, d, nz, core = at.s, at.d, at.nz, at.core
    T, width = x.shape
    L = ns * T
    R = wqkv_mine.shape[0]
    cw = width // ns
    n = dn.shape[0]
    piece = n // nd
    gl, ql = gain1.shape[1], gainqk.shape[1]
    dn_mine = wdown.at[block_of(s, piece)] if wdown.shape[0] == ns * piece else wdown
    hq, hk = H // ns, KV // ns
    group = hq // hk
    qw, kw = hq * HD, hk * HD
    own = block_of(s, T)
    pw = qw + 2 * kw
    gains[...] = jnp.zeros_like(gains)
    gains[0:1, :gl] = gain1[...]
    gains[1:2, :gl] = gain2[...]
    gains[2:3, :ql] = gainqk[...]
    for i in range(ns):

        @pl.when(s == i)
        def _():
            cuts = ((i * qw, qw), (H * HD + i * kw, kw), ((H + KV) * HD + i * kw, kw))
            wqkv_mine[...] = jnp.concatenate([wqkv_rows[:, a : a + b] for a, b in cuts], axis=1)

    at.greet()

    x_copies = [remote(x, xall.at[own], xs.at[j], xr.at[j], at.seq_to(j)) for j in range(1, ns)]
    g_copies = [remote(gains, gbuf.at[d], gs.at[j], gr.at[j], at.dp_to(j)) for j in range(1, nd)]
    c_copies = [remote(cot, cotall.at[own], cs.at[j], cr.at[j], at.seq_to(j)) for j in range(1, ns)]
    take_qkv = Gather(at, wqkv_mine, wqkv, sems[0:6], relayed=False)
    take_out = Gather(at, wout_mine, wout, sems[6:12], relayed=False)
    take_gu = Gather(at, gu_mine, gu, sems[12:18])
    take_dn = Gather(at, dn_mine, dn, sems[18:24])
    for c in g_copies + x_copies:
        c.start()
    take_qkv.start()
    take_out.start()
    xall[own, :] = x[...]
    gbuf[d] = gains[...]
    cot_local = pltpu.make_async_copy(cot, cotall.at[own], loc.at[0])
    cot_local.start()
    ff = wgate.shape[1]
    parts = max(1, -(-ff // (2 * n)))
    while nd % parts:
        parts += 1
    span = ff // parts
    stage = []
    for i, w in enumerate((wgate, wup)):
        for k in range(parts):
            row = pl.ds((i * parts + k) * R, R)
            stage.append(
                pltpu.make_async_copy(w.at[:, pl.ds(k * span, span)], gb.at[row, pl.ds(0, span)], wl.at[i, k])
            )
    for c in stage:
        c.start()
    for c in stage:
        c.wait()
    real = wgate.shape[1] // nd // ns
    gap = [jnp.zeros((R, piece - real), BF16)] if piece > real else []
    for i in range(ns):

        @pl.when(s == i)
        def _():
            cuts = []
            for w in range(2):
                for k in range(nd):
                    a = (k * ns + i) * real
                    row = (w * parts + a // span) * R
                    cuts += [gb[row : row + R, a % span : a % span + real]] + gap
            gu_mine[...] = jnp.concatenate(cuts, axis=1)

    for c in g_copies:
        c.wait_recv()
    gain_in = jnp.concatenate([gbuf[k][0:1, :gl] for k in range(nd)], axis=1)
    gain_mid = jnp.concatenate([gbuf[k][1:2, :gl] for k in range(nd)], axis=1)
    gain_qk = jnp.concatenate([gbuf[k][2:3, :ql] for k in range(nd)], axis=1)
    gsum[...] = jnp.zeros_like(gsum)
    gsum[0:1, :] = gain_in
    gsum[1:2, :] = gain_mid
    gsum[2:3, : 2 * HD] = gain_qk
    columns = jnp.transpose(jnp.broadcast_to(gain_qk, (8, 2 * HD)))
    gain_q, gain_k = columns[:HD, 0:1], columns[HD:, 0:1]
    for j in range(ns):
        rows = block_of(at.seq_from(j), T)
        if j:
            x_copies[j - 1].wait_recv()
        xc = xall[rows, :].astype(F32)
        scale = lax.rsqrt(jnp.mean(xc * xc, axis=-1, keepdims=True) + EPSILON)
        normed[rows, :] = (xc * scale * gain_in).astype(BF16)
    for c in c_copies:
        c.start()
    take_qkv.arrive()
    take_qkv.finish()
    for j in range(ns):
        rows = pl.ds(j * T, T)
        proj = mm(normed[rows, :], wqkv[...])
        projT[:, rows] = jnp.transpose(proj[:, : qw + kw])
        val = proj[:, qw + kw :]
        vT[:, rows] = jnp.transpose(val).astype(BF16)
        for i in range(hk):
            vrows[i, rows, :] = val[:, i * HD : (i + 1) * HD].astype(BF16)

    half = HD // 2

    def rope(row, gain, factor):
        u = projT[row, :]
        scale = lax.rsqrt(jnp.mean(u * u, axis=0, keepdims=True) + EPSILON)
        u = u * scale * gain
        a, b = u[:half], u[half:]
        return jnp.concatenate([a * cos[...] - b * sin[...], b * cos[...] + a * sin[...]], axis=0) * factor

    def rope_query(h, carry):
        row = block_of(h, HD)
        qT[row, :] = rope(row, gain_q, HD**-0.5).astype(BF16)
        return carry

    lax.fori_loop(0, hq, rope_query, 0)
    for i in range(hk):
        r = rope(pl.ds(qw + i * HD, HD), gain_k, 1.0)
        kT[i * HD : (i + 1) * HD, :] = r.astype(BF16)
        krows[i, :, :] = jnp.transpose(r).astype(BF16)

    keep = lax.broadcasted_iota(jnp.int32, (T, T), 0) <= lax.broadcasted_iota(jnp.int32, (T, T), 1)
    block = block_of(s, qw)

    def mixed_out(rb):
        return remote(mixT.at[rb], mrowsT.at[block], ms.at[rb], mr.at[s], (d, rb))

    for rb in range(ns):
        cols = pl.ds(rb * T, T)
        span = rb * T

        def head(h, carry):
            kv = h // group
            row, vrow = block_of(h, HD), block_of(kv, HD)
            q = qT[row, cols]
            p = jnp.where(keep, jnp.exp(mm(krows[kv, cols, :], q)), 0.0)
            tot = jnp.sum(p, axis=0, keepdims=True)
            m = mm(vT[vrow, cols], p.astype(BF16))
            if span:
                p = jnp.exp(mm(krows[kv, 0:span, :], q))
                tot = tot + jnp.sum(p, axis=0, keepdims=True)
                m = m + mm(vT[vrow, 0:span], p.astype(BF16))
            one = 1.0 / tot
            inv[h, :, cols] = one
            mixT[rb, row, :] = (m * one).astype(BF16)
            return carry

        lax.fori_loop(0, hq, head, 0)
        pl.when(s != rb)(mixed_out(rb).start)
        if rb == 0:
            take_gu.start()
        if rb == ns - 1:
            take_out.arrive()

    mrowsT[block, :] = mixT[s]
    for j in range(1, ns):
        src = at.seq_from(j)
        remote(mixT.at[0], mrowsT.at[block_of(src, qw)], ms.at[0], mr.at[src], (d, src)).wait_recv()
    take_out.finish()
    residual = x[...].astype(F32) + mm(jnp.transpose(mrowsT[...]), wout[...])
    resid[...] = residual
    scale_mid = lax.rsqrt(jnp.mean(residual * residual, axis=-1, keepdims=True) + EPSILON)
    xall[own, :] = (residual * scale_mid * gain_mid).astype(BF16)
    n_copies = [
        remote(xall.at[own], xall.at[own], ns_.at[j], nr.at[j], at.seq_to(j)) for j in range(1, ns)
    ]
    for c in n_copies:
        c.start()
    take_dn.start()
    take_gu.arrive()
    take_gu.finish()

    ft = 384 if n % 384 == 0 else 128
    nt = n // ft
    wt = 256
    for j in range(ns):
        rows = block_of(at.seq_from(j), T)
        if j:
            n_copies[j - 1].wait_recv()

        def pre_tile(i, carry):
            f = block_of(i, ft)
            gb[rows, f] = mm(xall[rows, :], gu[:, f]).astype(BF16)
            return carry

        lax.fori_loop(0, 2 * nt, pre_tile, 0)
    for c in c_copies:
        c.wait_recv()
    cot_local.wait()
    take_dn.arrive()
    take_dn.finish()
    p_copies = []
    for j in range(ns):
        rows = block_of(at.seq_from(j), T)

        def hidden_tile(i, carry):
            f, f2 = block_of(i, ft), block_of(i + nt, ft)
            gate, up = gb[rows, f].astype(F32), gb[rows, f2].astype(F32)
            sig = 1.0 / (1.0 + jnp.exp(-gate))
            act = gate * sig
            back = mm_nt(cotall[rows, :], dn[f, :])
            hid = act * up
            hrow[:, f] = hid.astype(BF16)
            hT[f, rows] = jnp.transpose(hid).astype(BF16)
            gb[rows, f] = (back * up * sig * (1.0 + gate * (1.0 - sig))).astype(BF16)
            gb[rows, f2] = (back * act).astype(BF16)
            return carry

        lax.fori_loop(0, nt, hidden_tile, 0)

        def back_tile(i, carry):
            w = block_of(i, wt)
            part = mm_nt(gb[rows, :], gu[w, :])
            if j:
                gsend[j - 1, :, w] = part.astype(BF16)
            else:
                gown[:, w] = part
            return carry

        lax.fori_loop(0, width // wt, back_tile, 0)
        if j:
            c = remote(gsend.at[j - 1], grecv.at[ns - j - 1], ps.at[j], pr.at[ns - j], at.seq_to(ns - j))
            c.start()
            p_copies.append(c)

        def out_tile(i, carry):
            w = block_of(i, wt)
            part = mm(hrow[...], dn[:, w])
            if j:
                osend[j - 1, :, w] = part.astype(BF16)
            else:
                oown[:, w] = part + resid[:, w]
            return carry

        lax.fori_loop(0, width // wt, out_tile, 0)

    for c in n_copies:
        c.wait_send()
    take_gu.drain()
    take_dn.drain()
    for k in range(nd):
        nmT[k % 2, (k // 2) * R : (k // 2 + 1) * R, :] = jnp.transpose(xall[:, k * R : (k + 1) * R])

    half_gu, half_dn = nz * R, nz * piece
    dns, dnown = dn.at[pl.ds(0, half_dn)], dn.at[pl.ds(half_dn, half_dn)]
    gus, gateown = (gu.at[pl.ds(i * half_gu, half_gu), pl.ds(0, n)] for i in range(2))
    uus, upown = (gu.at[pl.ds(i * half_gu, half_gu), pl.ds(n, n)] for i in range(2))

    def dn_rows(c, i):
        return hT[block_of(2 * i + c, piece), :]

    tiles = nt
    tw = n // tiles

    def other(buf, base):
        def tile(i, carry):
            f = block_of(i, tw)
            buf[:, f] = mm(nmT[1 - core], gb[:, pl.ds(pl.multiple_of(base + i * tw, 128), tw)]).astype(BF16)
            return carry

        lax.fori_loop(0, tiles, tile, 0)

    def summed(buf, got, base):
        def tile(i, carry):
            f = block_of(i, tw)
            part = mm(nmT[core], gb[:, pl.ds(pl.multiple_of(base + i * tw, 128), tw)])
            buf[:, f] = (part + got[:, f].astype(F32)).astype(BF16)
            return carry

        lax.fori_loop(0, tiles, tile, 0)

    dn_copy = remote(dns, dnr, ss.at[0], sr.at[0], at.sib)
    gate_copy = remote(gus, gur, ss.at[1], sr.at[1], at.sib)
    up_copy = remote(uus, uur, ss.at[2], sr.at[2], at.sib)

    def dn_other(i, carry):
        dns[block_of(i, piece), :] = mm(dn_rows(1 - core, i), cotall[...]).astype(BF16)
        return carry

    lax.fori_loop(0, nz, dn_other, 0)
    dn_copy.start()
    other(gus, 0)
    gate_copy.start()
    other(uus, n)
    up_copy.start()
    dn_copy.wait_recv()

    def dn_mine_sum(i, carry):
        r = block_of(i, piece)
        dnown[r, :] = (mm(dn_rows(core, i), cotall[...]) + dnr[r, :].astype(F32)).astype(BF16)
        return carry

    lax.fori_loop(0, nz, dn_mine_sum, 0)
    gate_copy.wait_recv()
    summed(gateown, gur, 0)
    up_copy.wait_recv()
    summed(upown, uur, n)

    for c in p_copies:
        c.wait()
    gnm = gown[...]
    for j in range(1, ns):
        gnm = gnm + grecv[j - 1].astype(F32)
    residual = resid[...]
    scale_mid = lax.rsqrt(jnp.mean(residual * residual, axis=-1, keepdims=True) + EPSILON)
    gsecond[...] = jnp.broadcast_to(jnp.sum(gnm * residual * scale_mid, axis=0, keepdims=True), (8, width))
    weighted = gnm * gain_mid
    gown[...] = (
        cotall[own, :].astype(F32)
        + scale_mid * weighted
        - residual * (scale_mid * scale_mid * scale_mid) * jnp.mean(weighted * residual, axis=-1, keepdims=True)
    )
    dn_sum = Scatter(at, dnown, dnz, dnf, dnall, sems[24:29])
    gate_sum = Scatter(at, gateown, gaz, gaf, gateall, sems[29:34])
    up_sum = Scatter(at, upown, upz, upf, upall, sems[44:49])
    qkv_sum = Scatter(at, qkown, qkz, qkf, qkvall, sems[34:39])
    out_sum = Scatter(at, goown, goz, gof, outall, sems[39:44])
    dn_sum.start()
    gate_sum.start()

    rback = gown[...].astype(BF16)

    def mixed_back(p):
        return remote(gmr.at[p], grows.at[own], bs.at[p], br.at[s], (d, p))

    for p in range(ns):
        gmr[p] = mm_nt(rback, wout[p * qw : (p + 1) * qw, :]).astype(BF16)
        pl.when(s != p)(mixed_back(p).start)
    grows[own, :] = gmr[s]

    for k in range(nd):
        nmT[k % 2, (k // 2) * R : (k // 2 + 1) * R, :] = mm(mrowsT[k * R : (k + 1) * R, :], rback).astype(BF16)
    go_copy = remote(nmT.at[1 - core], gor, ss2.at[0], sr2.at[0], at.sib)
    go_copy.start()
    for i in range(hk):
        qrows[i, :, :] = jnp.transpose(qT[i * group * HD : (i + 1) * group * HD, :])
    go_copy.wait_recv()
    gate_copy.wait_send()
    up_copy.wait_send()
    for p in range(ns):
        c = pl.ds(p * cw, cw)
        gu[0:half_gu, c] = (nmT[core, :, c].astype(F32) + gor[:, c].astype(F32)).astype(BF16)

    for j in range(1, ns):
        src = at.seq_from(j)
        remote(gmr.at[0], grows.at[block_of(src, T)], bs.at[0], br.at[src], (d, src)).wait_recv()
    for i in range(ns):
        rows = pl.ds(i * T, T)
        hT[pw : pw + qw, rows] = jnp.transpose(grows[rows, :])

    def gout_copy(j):
        return remote(gu.at[pl.ds(0, half_gu), block_of(at.seq_to(j)[1], cw)], gorecv.at[j - 1], gos.at[j], gorc.at[j], at.seq_to(j))

    def out_copy(j):
        return remote(osend.at[j - 1], xall.at[pl.ds((ns - j - 1) * T, T)], os_.at[j], or_.at[ns - j], at.seq_to(ns - j))

    for j in range(1, ns):
        gout_copy(j).start()

    causal = lax.broadcasted_iota(jnp.int32, (T, T), 0) <= lax.broadcasted_iota(jnp.int32, (T, T), 1)
    causal = jnp.concatenate([causal] * group, axis=1)
    gk[...] = jnp.zeros_like(gk)
    gv[...] = jnp.zeros_like(gv)

    def key_head(kv, carry):
        krow = block_of(kv, HD)
        lanes = block_of(kv, group * HD)
        for rb in range(ns):
            cols = pl.ds(rb * T, T)

            def side(ref, base):
                return jnp.concatenate(
                    [ref[pl.ds(pl.multiple_of(base + (kv * group + u) * HD, HD), HD), cols] for u in range(group)],
                    axis=1,
                )

            q, g = side(qT, 0), side(hT, pw)
            one = jnp.concatenate([inv[kv * group + u, :, cols] for u in range(group)], axis=1)
            m = jnp.concatenate(
                [mixT[rb, block_of(kv * group + u, HD), :] for u in range(group)], axis=1
            )
            delta = jnp.sum(g.astype(F32) * m.astype(F32), axis=0, keepdims=True)
            gr, qr = grows[cols, lanes], qrows[kv, cols, :]
            gr = jnp.concatenate([gr[:, u * HD : (u + 1) * HD] for u in range(group)], axis=0)
            qr = jnp.concatenate([qr[:, u * HD : (u + 1) * HD] for u in range(group)], axis=0)
            gq = jnp.zeros((HD, group * T), F32)
            for part, masked in ((pl.ds(0, rb * T), False), (cols, True)):
                if rb == 0 and not masked:
                    continue
                p = jnp.exp(mm(krows[kv, part, :], q)) * one
                if masked:
                    p = jnp.where(causal, p, 0.0)
                gp = mm(vrows[kv, part, :], g)
                ds = (p * (gp - delta)).astype(BF16)
                gv[kv, part, :] += mm(p.astype(BF16), gr)
                gk[kv, part, :] += mm(ds, qr)
                gq = gq + mm(kT[krow, part], ds)
            gq = gq * HD**-0.5
            for u in range(group):
                gqT[block_of(kv * group + u, HD), cols] = gq[:, u * T : (u + 1) * T]
        return carry

    lax.fori_loop(0, hk, key_head, 0)

    columns = jnp.transpose(gsum[:, : 2 * HD])
    gain_q, gain_k = columns[:HD, 2:3], columns[HD:, 2:3]

    def norm_column(row, g, gain):
        a, b = g[:half], g[half:]
        g = jnp.concatenate([a * cos[...] + b * sin[...], b * cos[...] - a * sin[...]], axis=0)
        u = projT[row, :]
        scale = lax.rsqrt(jnp.mean(u * u, axis=0, keepdims=True) + EPSILON)
        us = u * scale
        weighted = g * gain
        inner = jnp.mean(weighted * us, axis=0, keepdims=True)
        hT[row, :] = (scale * (weighted - us * inner)).astype(BF16)
        return jnp.sum(g * us, axis=1, keepdims=True)

    def query_back(h, acc):
        row = block_of(h, HD)
        return acc + norm_column(row, gqT[row, :], gain_q)

    gain_grad_q = lax.fori_loop(0, hq, query_back, jnp.zeros((HD, 1), F32))
    gain_grad_k = jnp.zeros((HD, 1), F32)
    for i in range(hk):
        gain_grad_k = gain_grad_k + norm_column(pl.ds(qw + i * HD, HD), jnp.transpose(gk[i]), gain_k)
        hT[qw + kw + i * HD : qw + kw + (i + 1) * HD, :] = jnp.transpose(gv[i]).astype(BF16)

    up_sum.start()

    def ni_copy(j):
        return remote(gsend.at[j - 1], grecv.at[j - 1], nis.at[j], nir.at[j], at.seq_to(j))

    for i in range(ns):
        rows = pl.ds(i * T, T)
        cotall[rows, 0:pw] = jnp.transpose(hT[0:pw, rows])
    for j in list(range(1, ns)) + [0]:
        part = mm_nt(cotall[block_of(at.seq_to(j)[1], T), 0:pw], wqkv[...])
        if j:
            gsend[j - 1] = part.astype(BF16)
            ni_copy(j).start()
        else:
            resid[...] = part
    for j in range(1, ns):
        out_copy(j).start()
    for k in range(nd):
        part = mm(hT[0:pw, :], normed[:, k * R : (k + 1) * R])
        gb[((k % 2) * nz + k // 2) * R : ((k % 2) * nz + k // 2 + 1) * R, 0:pw] = jnp.transpose(part).astype(BF16)
    qk_copy = remote(gb.at[block_of(1 - core, nz * R), pl.ds(0, pw)], qkr, ss2.at[1], sr2.at[1], at.sib)
    qk_copy.start()
    for j in range(1, ns):
        gout_copy(j).wait_recv()
    acc = gu[0:half_gu, block_of(s, cw)].astype(F32)
    for j in range(1, ns):
        acc = acc + gorecv[j - 1].astype(F32)
    goown[...] = acc.astype(BF16)
    out_sum.start()
    qk_copy.wait_recv()
    qkown[...] = (gb[block_of(core, nz * R), pl.ds(0, pw)].astype(F32) + qkr[...].astype(F32)).astype(BF16)
    qkv_sum.start()
    dn_sum.total()
    gate_sum.total()

    for j in range(1, ns):
        ni_copy(j).wait_recv()
    gni = resid[...]
    for j in range(1, ns):
        gni = gni + grecv[j - 1].astype(F32)
    stream = x[...].astype(F32)
    scale = lax.rsqrt(jnp.mean(stream * stream, axis=-1, keepdims=True) + EPSILON)
    unit = stream * scale
    weighted = gni * gsum[0:1, :]
    gown[...] = gown[...] + scale * (weighted - unit * jnp.mean(weighted * unit, axis=-1, keepdims=True))
    stream_store = pltpu.make_async_copy(gown, gstream, loc.at[2])
    stream_store.start()
    first = jnp.sum(gni * unit, axis=0, keepdims=True)
    qk = jnp.broadcast_to(jnp.concatenate([gain_grad_q, gain_grad_k], axis=0), (2 * HD, 128))
    sm0[0:1, :] = first
    sm0[1:2, :] = gsecond[0:1, :]
    sm0[2:8, :] = jnp.zeros((6, width), F32)
    sm0[2:3, : 2 * HD] = jnp.transpose(qk)[0:1, :]

    def small_seq(j):
        return remote(sm0, sm1.at[j - 1], s1.at[j], r1.at[j], at.seq_to(j))

    def small_dp(j):
        return remote(sm2, sm3.at[j - 1], s2.at[j], r2.at[j], at.dp_to(j))

    for j in range(1, ns):
        small_seq(j).start()
    up_sum.total()
    for j in range(1, ns):
        out_copy(j).wait_recv()
    acc = oown[...]
    for j in range(1, ns):
        acc = acc + xall[pl.ds((j - 1) * T, T), :].astype(F32)
    last = pl.ds((ns - 1) * T, T)
    xall[last, :] = acc.astype(BF16)
    out_store = pltpu.make_async_copy(xall.at[last], outputs, loc.at[1])
    out_store.start()
    for j in range(1, ns):
        small_seq(j).wait_recv()
    acc = sm0[...]
    for j in range(1, ns):
        acc = acc + sm1[j - 1]
    sm2[...] = acc
    for j in range(1, nd):
        small_dp(j).start()
    out_sum.total()
    qkv_sum.total()
    for j in range(1, nd):
        small_dp(j).wait_recv()
    for j in range(1, nd):
        acc = acc + sm3[j - 1]
    small[...] = acc

    for p in range(ns):
        pl.when(s != p)(mixed_back(p).wait_send)
    go_copy.wait_send()
    qk_copy.wait_send()
    for j in range(1, ns):
        gout_copy(j).wait_send()
        out_copy(j).wait_send()
        ni_copy(j).wait_send()
        small_seq(j).wait_send()
    for j in range(1, nd):
        small_dp(j).wait_send()
    for rb in range(ns):
        pl.when(s != rb)(mixed_out(rb).wait_send)
    for c in x_copies + g_copies + c_copies + [dn_copy]:
        c.wait_send()
    for t in (take_qkv, take_out):
        t.drain()
    for t in (dn_sum, out_sum, qkv_sum, gate_sum, up_sum):
        t.drain()
    out_store.wait()
    stream_store.wait()


def vmem(n):
    return [pl.BlockSpec(memory_space=pltpu.VMEM)] * n


def block(ns, nd, piece, x, gain1, gain2, gainqk, w_qkv, w_out, cot, w_gate, w_up, w_down):
    T, width = x.shape
    L = ns * T
    R = w_qkv.shape[0]
    n = nd * piece
    n2 = 2 * n
    nz = nd // 2
    hq, hk = H // ns, KV // ns
    qw, kw = hq * HD, hk * HD
    pw = qw + 2 * kw
    cw = width // ns
    cos, sin = rope_columns(L)
    sh, vm = jax.ShapeDtypeStruct, pltpu.VMEM
    outs = (
        sh((T, width), BF16), sh((T, width), F32), sh((ns, R, n), BF16), sh((ns, R, n), BF16),
        sh((ns, piece, width), BF16), sh((ns, R, pw), BF16), sh((ns, R, cw), BF16), sh((8, width), F32),
    )
    hbm = pl.BlockSpec(memory_space=pl.ANY)
    scratch = [
        vm((L, width), BF16), vm((qw + kw, L), F32), vm((qw, L), BF16), vm((kw, L), BF16),
        vm((hk, L, HD), BF16), vm((hk, L, HD), BF16), vm((hq, 1, L), F32), vm((ns, qw, T), BF16),
        vm((H * HD, T), BF16), vm((H * HD, width), BF16), vm((width, pw), BF16), vm((8, width), F32),
        vm((ns - 1, T, width), BF16), vm((T, width), F32), vm((8, width), F32),
        vm((kw, L), BF16), vm((T, width), F32), vm((L, width), BF16), vm((L, width), BF16), vm((8, 128), F32),
        vm((nd, 8, 128), F32), vm((R, pw), BF16), vm((R, n2), BF16), vm((nd * R, n2), BF16), vm((n, width), BF16),
        vm((T, n), BF16), vm((n, L), BF16), vm((L, n2), BF16), vm((ns - 1, T, width), BF16),
        vm((ns - 1, T, width), BF16), vm((T, width), F32), vm((2, nz * R, L), BF16),
        vm((nz * R, n), BF16), vm((nz * R, n), BF16), vm((nz * piece, width), BF16),
        vm((nz - 1, R, n), BF16), vm((R, n), BF16), vm((nz - 1, R, n), BF16), vm((R, n), BF16),
        vm((nz - 1, piece, width), BF16), vm((piece, width), BF16), vm((ns, T, qw), BF16), vm((L, qw), BF16),
        vm((hk, L, qw // hk), BF16), vm((hk, L, HD), F32), vm((hk, L, HD), F32), vm((qw, L), F32),
        vm((nz * R, pw), BF16), vm((nz * R, pw), BF16), vm((nz - 1, R, pw), BF16), vm((R, pw), BF16),
        vm((nz * R, width), BF16), vm((ns - 1, nz * R, cw), BF16), vm((nz * R, cw), BF16),
        vm((nz - 1, R, cw), BF16), vm((R, cw), BF16),
        vm((8, width), F32), vm((ns - 1, 8, width), F32), vm((8, width), F32), vm((nd - 1, 8, width), F32),
    ]
    sems = [DMA((ns,)), DMA((ns,)), DMA((nd,)), DMA((nd,))] + [DMA((ns,))] * 8 + [DMA((3,)), DMA((3,))]
    sems += [DMA((3,)), DMA((2, 8))]
    sems += [DMA((ns,))] * 6 + [DMA((2,)), DMA((2,))] + [DMA((ns,))] * 4 + [DMA((nd,)), DMA((nd,))]
    return pl.pallas_call(
        functools.partial(block_kernel, ns, nd),
        out_shape=outs,
        in_specs=vmem(5) + [hbm] * 5 + vmem(2),
        out_specs=[hbm] * 7 + vmem(1),
        scratch_shapes=scratch + sems + gather_sems(nz) * 4 + scatter_sems(ns, nz) * 5,
        compiler_params=pltpu.CompilerParams(
            collective_id=0, has_side_effects=True, vmem_limit_bytes=VMEM_LIMIT
        ),
        cost_estimate=pl.CostEstimate(flops=38_000_000_000, bytes_accessed=40_000_000, transcendentals=12_000_000),
    )(x, gain1, gain2, gainqk, w_qkv, w_out, cot, w_gate, w_up, w_down, cos, sin)


def finish_kernel(ns, nd, piece, gateall, upall, qkvall, outall, dnall, gate, up, qkv, out, down):
    hq, hk = H // ns, KV // ns
    qw, kw = hq * HD, hk * HD
    pad = gateall.shape[2] // nd
    for ref, got in ((gate, gateall), (up, upall)):
        parts = [got[i].astype(F32) for i in range(ns)]
        ref[...] = jnp.concatenate(
            [parts[i][:, k * pad : k * pad + piece] for k in range(nd) for i in range(ns)], axis=1
        )
    parts = [qkvall[i].astype(F32) for i in range(ns)]
    qkv[...] = jnp.concatenate(
        [p[:, :qw] for p in parts] + [p[:, qw : qw + kw] for p in parts] + [p[:, qw + kw :] for p in parts], axis=1
    )
    out[...] = jnp.concatenate([outall[i].astype(F32) for i in range(ns)], axis=1)
    down[...] = jnp.concatenate([dnall[i].astype(F32)[:piece] for i in range(dnall.shape[0])], axis=0)


def finish(ns, nd, piece, gateall, upall, qkvall, outall, dnall):
    R = gateall.shape[1]
    steps = 4
    rows = R // steps
    ff = ns * nd * piece
    width = dnall.shape[2]
    widths = (ff, ff, ns * qkvall.shape[2], ns * outall.shape[2])
    many = ns // steps
    ins = [pl.BlockSpec((ns, rows, a.shape[2]), lambda i: (0, i, 0)) for a in (gateall, upall, qkvall, outall)]
    ins.append(pl.BlockSpec((many,) + dnall.shape[1:], lambda i: (i, 0, 0)))
    outs = [pl.BlockSpec((rows, w), lambda i: (i, 0)) for w in widths]
    outs.append(pl.BlockSpec((many * piece, width), lambda i: (i, 0)))
    return pl.pallas_call(
        functools.partial(finish_kernel, ns, nd, piece),
        grid=(steps,),
        out_shape=[jax.ShapeDtypeStruct((R, w), F32) for w in widths]
        + [jax.ShapeDtypeStruct((ns * piece, width), F32)],
        in_specs=ins,
        out_specs=outs,
        compiler_params=pltpu.CompilerParams(vmem_limit_bytes=40 << 20),
    )(gateall, upall, qkvall, outall, dnall)


def shards(inputs, cotangent, first_gain, w_qkv, qk_gain, w_out, second_gain, w_gate, w_up, w_down):
    ns, nd = lax.axis_size("seq"), lax.axis_size("dp")
    s, d = lax.axis_index("seq"), lax.axis_index("dp")
    piece = w_down.shape[0] // ns
    pad = -piece % 16
    down_rows = w_down
    if pad:
        down_rows = jnp.pad(lax.dynamic_slice_in_dim(w_down, s * piece, piece, 0), ((0, pad), (0, 0)))
    x = inputs[0]
    outputs, gstream, gateall, upall, dnall, qkvall, outall, small = block(
        ns, nd, piece + pad, x, first_gain[None], second_gain[None], qk_gain[None], w_qkv, w_out, cotangent[0],
        w_gate, w_up, down_rows,
    )
    gate, up, qkv, out, down = finish(ns, nd, piece, gateall, upall, qkvall, outall, dnall)
    gl, ql = first_gain.shape[0], qk_gain.shape[0]
    first = lax.dynamic_slice(small, (0, d * gl), (1, gl))[0]
    second = lax.dynamic_slice(small, (1, d * gl), (1, gl))[0]
    qk = lax.dynamic_slice(small, (2, d * ql), (1, ql))[0]
    return (outputs[None], gstream[None], first, qkv, qk, out, second, gate, up, down)


def solution(mesh):
    act = P("dp", "seq", None)
    vec, mat = P("dp"), P("dp", None)
    in_specs = (act, act, vec, mat, vec, mat, vec, mat, mat, mat)
    out_specs = (act, act, vec, mat, vec, mat, vec, mat, mat, mat)
    return jax.shard_map(shards, mesh=mesh, in_specs=in_specs, out_specs=out_specs, check_vma=False)
```

time: 328 us -> 287 us (0.88)
  Pallas kernels: 305 us -> 275 us
  local copies, waits for them, and re-layouts: 15.6 us -> 10.8 us
  other arithmetic: 4.64 us -> 0 us
    pallas_call x3 -> x2, Pallas kernels: 305 us -> 275 us  [the longest x1 271 us: block(): pl.pallas_call(functools.partial(block_kernel, ns, nd), out_shape=outs, i...]
    unnamed x20 -> x16, local copies, waits for them, and re-layouts: 4.83 us -> 8.18 us
where the time goes in v4:
time: 287 us; the launch traced here: 286 us
  Pallas kernels  275 us (96%)
  local copies, waits for them, and re-layouts  10.8 us (4%)
    pallas_call x1, Pallas kernels, block(): pl.pallas_call(functools.partial(block_kernel, ns, nd), out_shape=outs, i...  271 us
    unnamed x16, local copies, waits for them, and re-layouts  8.18 us

profile of v4, /device:TPU:30, one launch (start us, length us, event | category | flops | bytes accessed | tf_op | source)
XLA Modules:
  0.0 286.1 jit_solution(14448138226566073303)
XLA Ops:
  0.7 270.7 %shard_map.195 = (bf16[256,1024]{1,0:T(8,128)(2,1)}, f32[256,1024]{1,0:T(8,128)}, bf16[4,128,1152]{2,1,0:T(8,128)(2,1)}, bf16[4,128,1152]{2,1,0:T(8,128)(2,1)}, ...) custom-call(bf16[256,1024]{1,0:T(8,128)(2,1)} %bitcast.15, ...), custom_call_target="tpu_custom_call" | custom-call | flops 38000001024 | bytes 40000000 | tf_op jit(solution)/shard_map/pallas_call | solution.py:806
  271.3 1.3 dynamic-slice_bitcast_fusion.1
  272.6 1.3 dynamic-slice_bitcast_fusion
  273.9 0.0 copy-start
  273.9 1.3 copy-done
  275.2 0.0 copy-start.1
  275.2 1.3 copy-done.1
  276.5 0.0 copy-start.2
  276.5 1.3 copy-done.2
  277.7 0.0 copy-start.3
  277.7 1.0 copy-done.3
  278.8 0.0 copy-start.4
  278.8 0.9 copy-done.4
  279.7 0.0 copy-start.6
  279.7 4.0 %shard_map.196 = (f32[128,4608]{1,0:T(8,128)}, f32[128,4608]{1,0:T(8,128)}, f32[128,2048]{1,0:T(8,128)}, f32[128,1024]{1,0:T(8,128)}, f32[576,1024]{1,0:T(8,128)}) custom-call(bf16[4,128,1152]{2,1,0:T(8,128)(2,1)S(1)} %copy-done, bf16[4,128,1152]{2,1,0:T(8,128)(2,1)S(1)} %copy-done.1, bf16[4,128,512]{2,1,0:T(8,128)(2,1)S(1)} %copy-done.3, ...), custom_call_target="tpu_custom_call" | custom-call | tf_op jit(solution)/shard_map/pallas_call | solution.py:848
  283.7 0.0 copy-start.5
  283.7 0.0 copy-done.6
  283.8 0.8 copy.24
  284.6 0.6 copy-done.5
  285.2 1.0 copy.25
Async XLA Ops:
  273.9 1.3 copy-start
  275.2 1.3 copy-start.1
  276.5 1.3 copy-start.2
  277.7 1.0 copy-start.3
  278.8 0.9 copy-start.4
  279.7 4.0 %copy-start.6 = (bf16[256,1024]{1,0:T(8,128)(2,1)S(1)}, bf16[256,1024]{1,0:T(8,128)(2,1)}, u32[]{:S(2)}) copy-start(bf16[256,1024]{1,0:T(8,128)(2,1)} %get-tuple-element.23) | copy-start | bytes 1572868
  283.7 1.4 copy-start.5

commit v5 on v4

--- a/solution.py
+++ b/solution.py
@@ -60,6 +60,20 @@
     def seq_from(self, j):
         return lax.rem(self.s + self.ns - j, self.ns)
 
+    def across(self):
+        return (self.s + 1 - 2 * lax.rem(self.s, 2), lax.rem(self.s + 2, 4), 3 - self.s)
+
+    def gather_rank(self, j):
+        if j == 0:
+            return self.s
+        return self.across()[j - 1] if self.ns == 4 else self.seq_from(j)
+
+    def reduce_rank(self, j):
+        if j == 0:
+            return self.s
+        x, y, o = self.across()
+        return (o, x, y)[j - 1] if self.ns == 4 else lax.rem(self.s + j, self.ns)
+
     def dp_to(self, j):
         return (lax.rem(self.d + j, self.nd), self.s)
 
@@ -79,6 +93,105 @@
         for j in range(1, self.ns):
             pl.semaphore_signal(bar, inc=1, device_id=self.seq_to(j), device_id_type=MESH)
         pl.semaphore_wait(bar, self.nd + self.ns - 2)
+
+
+class SeqGather:
+    def __init__(self, at, src, dst, sems):
+        self.at, self.src, self.dst = at, src, dst
+        self.send, self.recv = sems
+        self.half = src.shape[0] // 2
+
+    def direct(self, j):
+        at = self.at
+        to = at.across()[j - 1] if at.ns == 4 else at.seq_to(j)[1]
+        return remote(self.src, self.dst(at.s), self.send.at[j], self.recv.at[j], (at.d, to))
+
+    def forward(self, i):
+        at = self.at
+        part = self.dst(at.across()[i]).at[pl.ds(i * self.half, self.half)]
+        return remote(part, part, self.send.at[3 + i], self.recv.at[3 + i], (at.d, at.across()[1 - i]))
+
+    def near(self):
+        return range(1, 3 if self.at.ns == 4 else self.at.ns)
+
+    def start(self):
+        for j in self.near():
+            self.direct(j).start()
+
+    def hop(self):
+        if self.at.ns == 4:
+            for i in range(2):
+                self.direct(i + 1).wait_recv()
+                self.forward(i).start()
+
+    def wait(self, j):
+        if self.at.ns != 4:
+            self.direct(j).wait_recv()
+        elif j == 3:
+            for i in range(2):
+                self.forward(i).wait_recv()
+
+    def finish(self):
+        for j in range(1, self.at.ns):
+            self.wait(j)
+
+    def drain(self):
+        for j in self.near():
+            self.direct(j).wait_send()
+        if self.at.ns == 4:
+            for i in range(2):
+                self.forward(i).wait_send()
+
+
+def seq_sems(ns):
+    return [DMA((max(ns, 6),)), DMA((max(ns, 6),))]
+
+
+class SeqReduce:
+    def __init__(self, at, rows, stage, inbox, sems):
+        self.at, self.rows, self.stage, self.inbox = at, rows, stage, inbox
+        self.send, self.recv = sems
+
+    def part(self, ref, block, half=None):
+        if half is None:
+            return ref.at[pl.ds(block * self.rows, self.rows)]
+        h = self.rows // 2
+        return ref.at[pl.ds(block * self.rows + half * h, h)]
+
+    def leg(self, k):
+        at = self.at
+        if at.ns != 4:
+            src, dst, to = self.part(self.stage, k - 1), self.part(self.inbox, k - 1), at.seq_to(k)[1]
+        else:
+            b, h, i, n = ((0, 0, 2, 0), (0, 1, 2, 1), (1, 0, 0, 0), (2, 1, 1, 1), (2, 0, 1, 1), (1, 1, 0, 0))[k]
+            src, dst, to = self.part(self.stage, b, h), self.part(self.inbox, i, h), at.across()[n]
+        return remote(src, dst, self.send.at[k], self.recv.at[k], (at.d, to))
+
+    def push(self, j):
+        for k in (j,) if self.at.ns != 4 else ((), (0, 1), (2,), (3,))[j]:
+            self.leg(k).start()
+
+    def hop(self):
+        if self.at.ns != 4:
+            return
+        h = self.rows // 2
+        for k, b in ((0, 2), (1, 1)):
+            self.leg(k).wait_recv()
+            mine, came = pl.ds(b * self.rows + k * h, h), pl.ds(2 * self.rows + k * h, h)
+            self.stage[mine, :] = (self.stage[mine, :].astype(F32) + self.inbox[came, :].astype(F32)).astype(BF16)
+            self.leg(4 + k).start()
+
+    def total(self, acc):
+        four = self.at.ns == 4
+        for k in range(2, 6) if four else range(1, self.at.ns):
+            self.leg(k).wait_recv()
+        for b in range(2 if four else self.at.ns - 1):
+            acc = acc + self.inbox[b * self.rows : (b + 1) * self.rows, :].astype(F32)
+        return acc
+
+    def drain(self):
+        for k in range(6) if self.at.ns == 4 else range(1, self.at.ns):
+            self.leg(k).wait_send()
 
 
 class Gather:
@@ -121,27 +234,28 @@
 
     def order(self):
         nz = self.at.nz
-        return list(range(2, nz - 1)) + [1, nz - 1]
+        return sorted({2, nz - 2}), list(range(3, nz - 2)) + [1, nz - 1]
 
     def start(self):
-        at = self.at
-        for j in range(1, at.nz):
-
-            @pl.when(self.near(j))
-            def _():
-                self.direct(j).start()
-
+        first, rest = self.order()
+        for j in first + rest:
+            pl.when(self.near(j))(self.direct(j).start)
         self.across(0).start()
         self.mine().start()
 
     def mine(self):
         return pltpu.make_async_copy(self.src, self.dst.at[block_of(self.at.d, self.rows)], self.local.at[0])
 
-    def arrive(self):
-        for j in self.order():
+    def hop(self):
+        for j in self.order()[0]:
             self.direct(j).wait_recv()
             for here, copy in self.relay(j):
                 pl.when(here)(copy.start)
+            self.across(j).start()
+
+    def arrive(self):
+        for j in self.order()[1]:
+            self.direct(j).wait_recv()
             self.across(j).start()
 
     def finish(self):
@@ -165,46 +279,87 @@
 class Scatter:
     def __init__(self, at, pieces, inbox, final, out, sems):
         self.at, self.pieces, self.inbox, self.final, self.out = at, pieces, inbox, final, out
-        self.send, self.recv, self.osend, self.orecv, self.local = sems
+        self.send, self.recv, osend, orecv, self.local, self.rsend, self.rrecv = sems
         self.rows = final.shape[0]
+        self.share = SeqGather(at, final, lambda r: out.at[r], (osend, orecv))
+
+    def piece(self, z):
+        return self.pieces.at[block_of(z, self.rows)]
 
     def copy(self, j):
         at = self.at
-        piece = self.pieces.at[block_of(at.z_index(j), self.rows)]
-        return remote(piece, self.inbox.at[j - 1], self.send.at[j], self.recv.at[j], at.z_device(at.z_index(j)))
-
-    def spread(self, j):
+        z = at.z_index(j)
+        return remote(self.piece(z), self.inbox.at[j - 1], self.send.at[j], self.recv.at[j], at.z_device(z))
+
+    def far_copy(self, target, via):
+        slot = self.inbox.at[self.at.nz - 1]
+        return remote(self.piece(target), slot, self.rsend.at[0], self.rrecv.at[0], self.at.z_device(via))
+
+    def far(self):
+        nz = self.at.nz
+        return ((0, nz - 1, 1, nz - 2), (nz - 1, 0, nz - 2, 2))
+
+    def near(self, away):
+        return (away < self.at.nz - 1) & (away > 1 - self.at.nz)
+
+    def free(self, j):
+        go = self.near(self.at.z_index(j) - self.at.zz)
+        for _, _, via, k in self.far():
+            if k == j:
+                go = go & (self.at.zz != via)
+        return go
+
+    def start(self):
         at = self.at
-        return remote(self.final, self.out.at[at.s], self.osend.at[j], self.orecv.at[j], at.seq_to(j))
+        for origin, target, via, _ in self.far():
+            pl.when(at.zz == origin)(self.far_copy(target, via).start)
+        for j in range(1, at.nz):
+            pl.when(self.free(j))(self.copy(j).start)
+            away = at.z_from(j) - at.zz
+
+            @pl.when((away >= at.nz - 1) | (away <= 1 - at.nz))
+            def _():
+                self.inbox[j - 1] = jnp.zeros_like(self.inbox[j - 1])
+
+    def relay(self):
+        at = self.at
+        for _, target, via, j in self.far():
+
+            @pl.when(at.zz == via)
+            def _():
+                self.far_copy(target, via).wait_recv()
+                rows = block_of(target, self.rows)
+                both = self.pieces[rows, :].astype(F32) + self.inbox[at.nz - 1].astype(F32)
+                self.pieces[rows, :] = both.astype(BF16)
+                self.copy(j).start()
 
     def keep(self):
         return pltpu.make_async_copy(self.final, self.out.at[self.at.s], self.local.at[0])
 
-    def start(self):
-        for j in range(1, self.at.nz):
-            self.copy(j).start()
-
     def total(self):
-        for j in range(1, self.at.nz):
-            self.copy(j).wait_recv()
+        at = self.at
+        for j in range(1, at.nz):
+            pl.when(self.near(at.z_from(j) - at.zz))(self.copy(j).wait_recv)
         acc = self.pieces[block_of(self.at.zz, self.rows), :].astype(F32)
         for j in range(1, self.at.nz):
             acc = acc + self.inbox[j - 1].astype(F32)
         self.final[...] = acc.astype(BF16)
         self.keep().start()
-        for j in range(1, self.at.ns):
-            self.spread(j).start()
+        self.share.start()
 
     def drain(self):
         self.keep().wait()
-        for j in range(1, self.at.ns):
-            self.spread(j).wait()
-        for j in range(1, self.at.nz):
-            self.copy(j).wait_send()
+        self.share.finish()
+        self.share.drain()
+        at = self.at
+        for j in range(1, at.nz):
+            pl.when(self.near(at.z_index(j) - at.zz))(self.copy(j).wait_send)
+        for origin, target, via, _ in self.far():
+            pl.when(at.zz == origin)(self.far_copy(target, via).wait_send)
 
 
 def scatter_sems(ns, nz):
-    return [DMA((nz,)), DMA((nz,)), DMA((ns,)), DMA((ns,)), DMA((1,))]
+    return [DMA((nz,)), DMA((nz,))] + seq_sems(ns) + [DMA((1,)), DMA((1,)), DMA((1,))]
 
 
 def block_kernel(
@@ -246,15 +401,18 @@
 
     at.greet()
 
-    x_copies = [remote(x, xall.at[own], xs.at[j], xr.at[j], at.seq_to(j)) for j in range(1, ns)]
+    share_x = SeqGather(at, x, lambda r: xall.at[block_of(r, T)], (xs, xr))
     g_copies = [remote(gains, gbuf.at[d], gs.at[j], gr.at[j], at.dp_to(j)) for j in range(1, nd)]
-    c_copies = [remote(cot, cotall.at[own], cs.at[j], cr.at[j], at.seq_to(j)) for j in range(1, ns)]
+    share_cot = SeqGather(at, cot, lambda r: cotall.at[block_of(r, T)], (cs, cr))
+    share_nm = SeqGather(at, xall.at[own], lambda r: xall.at[block_of(r, T)], (ns_, nr))
     take_qkv = Gather(at, wqkv_mine, wqkv, sems[0:6], relayed=False)
     take_out = Gather(at, wout_mine, wout, sems[6:12], relayed=False)
-    take_gu = Gather(at, gu_mine, gu, sems[12:18])
+    take_gate = Gather(at, gu_mine.at[:, pl.ds(0, n)], gu.at[:, pl.ds(0, n)], sems[12:18])
+    take_up = Gather(at, gu_mine.at[:, pl.ds(n, n)], gu.at[:, pl.ds(n, n)], sems[59:65])
     take_dn = Gather(at, dn_mine, dn, sems[18:24])
-    for c in g_copies + x_copies:
+    for c in g_copies:
         c.start()
+    share_x.start()
     take_qkv.start()
     take_out.start()
     xall[own, :] = x[...]
@@ -303,14 +461,16 @@
     columns = jnp.transpose(jnp.broadcast_to(gain_qk, (8, 2 * HD)))
     gain_q, gain_k = columns[:HD, 0:1], columns[HD:, 0:1]
     for j in range(ns):
-        rows = block_of(at.seq_from(j), T)
+        rows = block_of(at.gather_rank(j), T)
+        if j == 1:
+            share_x.hop()
         if j:
-            x_copies[j - 1].wait_recv()
+            share_x.wait(j)
         xc = xall[rows, :].astype(F32)
         scale = lax.rsqrt(jnp.mean(xc * xc, axis=-1, keepdims=True) + EPSILON)
         normed[rows, :] = (xc * scale * gain_in).astype(BF16)
-    for c in c_copies:
-        c.start()
+    share_cot.start()
+    take_qkv.hop()
     take_qkv.arrive()
     take_qkv.finish()
     for j in range(ns):
@@ -342,6 +502,7 @@
         kT[i * HD : (i + 1) * HD, :] = r.astype(BF16)
         krows[i, :, :] = jnp.transpose(r).astype(BF16)
 
+    share_x.drain()
     keep = lax.broadcasted_iota(jnp.int32, (T, T), 0) <= lax.broadcasted_iota(jnp.int32, (T, T), 1)
     block = block_of(s, qw)
 
@@ -371,8 +532,9 @@
         lax.fori_loop(0, hq, head, 0)
         pl.when(s != rb)(mixed_out(rb).start)
         if rb == 0:
-            take_gu.start()
+            take_gate.start()
         if rb == ns - 1:
+            take_out.hop()
             take_out.arrive()
 
     mrowsT[block, :] = mixT[s]
@@ -384,37 +546,43 @@
     resid[...] = residual
     scale_mid = lax.rsqrt(jnp.mean(residual * residual, axis=-1, keepdims=True) + EPSILON)
     xall[own, :] = (residual * scale_mid * gain_mid).astype(BF16)
-    n_copies = [
-        remote(xall.at[own], xall.at[own], ns_.at[j], nr.at[j], at.seq_to(j)) for j in range(1, ns)
-    ]
-    for c in n_copies:
-        c.start()
+    share_nm.start()
+    share_cot.hop()
+    take_gate.hop()
+    take_up.start()
+    take_gate.arrive()
+    share_nm.hop()
+    share_nm.finish()
+    take_up.hop()
     take_dn.start()
-    take_gu.arrive()
-    take_gu.finish()
-
+    take_up.arrive()
     ft = 384 if n % 384 == 0 else 128
     nt = n // ft
     wt = 256
-    for j in range(ns):
-        rows = block_of(at.seq_from(j), T)
-        if j:
-            n_copies[j - 1].wait_recv()
-
-        def pre_tile(i, carry):
-            f = block_of(i, ft)
-            gb[rows, f] = mm(xall[rows, :], gu[:, f]).astype(BF16)
+
+    def pre_part(base):
+        def pre_block(j, carry):
+            rows = block_of(j, T)
+            for i in range(nt):
+                f = pl.ds(base + i * ft, ft)
+                gb[rows, f] = mm(xall[rows, :], gu[:, f]).astype(BF16)
             return carry
 
-        lax.fori_loop(0, 2 * nt, pre_tile, 0)
-    for c in c_copies:
-        c.wait_recv()
+        lax.fori_loop(0, ns, pre_block, 0)
+
+    take_gate.finish()
+    pre_part(0)
+    take_up.finish()
+    pre_part(n)
+    share_cot.finish()
     cot_local.wait()
+    take_dn.hop()
     take_dn.arrive()
     take_dn.finish()
-    p_copies = []
+    sum_nm = SeqReduce(at, T, gsend, grecv, (ps, pr))
     for j in range(ns):
-        rows = block_of(at.seq_from(j), T)
+        rows = block_of(at.reduce_rank(j), T)
+        stage = pl.ds((j - 1) * T, T)
 
         def hidden_tile(i, carry):
             f, f2 = block_of(i, ft), block_of(i + nt, ft)
@@ -435,39 +603,43 @@
             w = block_of(i, wt)
             part = mm_nt(gb[rows, :], gu[w, :])
             if j:
-                gsend[j - 1, :, w] = part.astype(BF16)
+                gsend[stage, w] = part.astype(BF16)
             else:
                 gown[:, w] = part
             return carry
 
         lax.fori_loop(0, width // wt, back_tile, 0)
         if j:
-            c = remote(gsend.at[j - 1], grecv.at[ns - j - 1], ps.at[j], pr.at[ns - j], at.seq_to(ns - j))
-            c.start()
-            p_copies.append(c)
+            sum_nm.push(j)
 
         def out_tile(i, carry):
             w = block_of(i, wt)
             part = mm(hrow[...], dn[:, w])
             if j:
-                osend[j - 1, :, w] = part.astype(BF16)
+                osend[stage, w] = part.astype(BF16)
             else:
                 oown[:, w] = part + resid[:, w]
             return carry
 
         lax.fori_loop(0, width // wt, out_tile, 0)
 
-    for c in n_copies:
-        c.wait_send()
-    take_gu.drain()
+    sum_nm.hop()
+    share_nm.drain()
+    share_cot.drain()
+    take_gate.drain()
+    take_up.drain()
     take_dn.drain()
-    for k in range(nd):
-        nmT[k % 2, (k // 2) * R : (k // 2 + 1) * R, :] = jnp.transpose(xall[:, k * R : (k + 1) * R])
-
     half_gu, half_dn = nz * R, nz * piece
     dns, dnown = dn.at[pl.ds(0, half_dn)], dn.at[pl.ds(half_dn, half_dn)]
     gus, gateown = (gu.at[pl.ds(i * half_gu, half_gu), pl.ds(0, n)] for i in range(2))
     uus, upown = (gu.at[pl.ds(i * half_gu, half_gu), pl.ds(n, n)] for i in range(2))
+    dn_sum = Scatter(at, dnown, dnz, dnf, dnall, sems[24:31])
+    gate_sum = Scatter(at, gateown, gaz, gaf, gateall, sems[31:38])
+    up_sum = Scatter(at, upown, upz, upf, upall, sems[38:45])
+    qkv_sum = Scatter(at, qkown, qkz, qkf, qkvall, sems[45:52])
+    out_sum = Scatter(at, goown, goz, gof, outall, sems[52:59])
+    for k in range(nd):
+        nmT[k % 2, (k // 2) * R : (k // 2 + 1) * R, :] = jnp.transpose(xall[:, k * R : (k + 1) * R])
 
     def dn_rows(c, i):
         return hT[block_of(2 * i + c, piece), :]
@@ -514,16 +686,15 @@
         return carry
 
     lax.fori_loop(0, nz, dn_mine_sum, 0)
+    dn_sum.start()
     gate_copy.wait_recv()
     summed(gateown, gur, 0)
     up_copy.wait_recv()
     summed(upown, uur, n)
-
-    for c in p_copies:
-        c.wait()
-    gnm = gown[...]
-    for j in range(1, ns):
-        gnm = gnm + grecv[j - 1].astype(F32)
+    gate_sum.start()
+
+    gnm = sum_nm.total(gown[...])
+    sum_nm.drain()
     residual = resid[...]
     scale_mid = lax.rsqrt(jnp.mean(residual * residual, axis=-1, keepdims=True) + EPSILON)
     gsecond[...] = jnp.broadcast_to(jnp.sum(gnm * residual * scale_mid, axis=0, keepdims=True), (8, width))
@@ -533,14 +704,6 @@
         + scale_mid * weighted
         - residual * (scale_mid * scale_mid * scale_mid) * jnp.mean(weighted * residual, axis=-1, keepdims=True)
     )
-    dn_sum = Scatter(at, dnown, dnz, dnf, dnall, sems[24:29])
-    gate_sum = Scatter(at, gateown, gaz, gaf, gateall, sems[29:34])
-    up_sum = Scatter(at, upown, upz, upf, upall, sems[44:49])
-    qkv_sum = Scatter(at, qkown, qkz, qkf, qkvall, sems[34:39])
-    out_sum = Scatter(at, goown, goz, gof, outall, sems[39:44])
-    dn_sum.start()
-    gate_sum.start()
-
     rback = gown[...].astype(BF16)
 
     def mixed_back(p):
@@ -551,6 +714,7 @@
         pl.when(s != p)(mixed_back(p).start)
     grows[own, :] = gmr[s]
 
+    dn_sum.relay()
     for k in range(nd):
         nmT[k % 2, (k // 2) * R : (k // 2 + 1) * R, :] = mm(mrowsT[k * R : (k + 1) * R, :], rback).astype(BF16)
     go_copy = remote(nmT.at[1 - core], gor, ss2.at[0], sr2.at[0], at.sib)
@@ -574,9 +738,9 @@
     def gout_copy(j):
         return remote(gu.at[pl.ds(0, half_gu), block_of(at.seq_to(j)[1], cw)], gorecv.at[j - 1], gos.at[j], gorc.at[j], at.seq_to(j))
 
-    def out_copy(j):
-        return remote(osend.at[j - 1], xall.at[pl.ds((ns - j - 1) * T, T)], os_.at[j], or_.at[ns - j], at.seq_to(ns - j))
-
+    sum_outputs = SeqReduce(at, T, osend, xall, (os_, or_))
+    for j in range(1, ns):
+        sum_outputs.push(j)
     for j in range(1, ns):
         gout_copy(j).start()
 
@@ -625,6 +789,7 @@
 
     lax.fori_loop(0, hk, key_head, 0)
 
+    sum_outputs.hop()
     columns = jnp.transpose(gsum[:, : 2 * HD])
     gain_q, gain_k = columns[:HD, 2:3], columns[HD:, 2:3]
 
@@ -649,28 +814,27 @@
         gain_grad_k = gain_grad_k + norm_column(pl.ds(qw + i * HD, HD), jnp.transpose(gk[i]), gain_k)
         hT[qw + kw + i * HD : qw + kw + (i + 1) * HD, :] = jnp.transpose(gv[i]).astype(BF16)
 
+    gate_sum.relay()
     up_sum.start()
 
-    def ni_copy(j):
-        return remote(gsend.at[j - 1], grecv.at[j - 1], nis.at[j], nir.at[j], at.seq_to(j))
-
+    sum_ni = SeqReduce(at, T, gsend, grecv, (nis, nir))
     for i in range(ns):
         rows = pl.ds(i * T, T)
         cotall[rows, 0:pw] = jnp.transpose(hT[0:pw, rows])
     for j in list(range(1, ns)) + [0]:
-        part = mm_nt(cotall[block_of(at.seq_to(j)[1], T), 0:pw], wqkv[...])
+        part = mm_nt(cotall[block_of(at.reduce_rank(j), T), 0:pw], wqkv[...])
         if j:
-            gsend[j - 1] = part.astype(BF16)
-            ni_copy(j).start()
+            gsend[pl.ds((j - 1) * T, T), :] = part.astype(BF16)
+            sum_ni.push(j)
         else:
             resid[...] = part
-    for j in range(1, ns):
-        out_copy(j).start()
     for k in range(nd):
         part = mm(hT[0:pw, :], normed[:, k * R : (k + 1) * R])
         gb[((k % 2) * nz + k // 2) * R : ((k % 2) * nz + k // 2 + 1) * R, 0:pw] = jnp.transpose(part).astype(BF16)
     qk_copy = remote(gb.at[block_of(1 - core, nz * R), pl.ds(0, pw)], qkr, ss2.at[1], sr2.at[1], at.sib)
     qk_copy.start()
+    sum_ni.hop()
+    dn_sum.total()
     for j in range(1, ns):
         gout_copy(j).wait_recv()
     acc = gu[0:half_gu, block_of(s, cw)].astype(F32)
@@ -681,14 +845,13 @@
     qk_copy.wait_recv()
     qkown[...] = (gb[block_of(core, nz * R), pl.ds(0, pw)].astype(F32) + qkr[...].astype(F32)).astype(BF16)
     qkv_sum.start()
-    dn_sum.total()
+    up_sum.relay()
+    out_sum.relay()
     gate_sum.total()
-
-    for j in range(1, ns):
-        ni_copy(j).wait_recv()
-    gni = resid[...]
-    for j in range(1, ns):
-        gni = gni + grecv[j - 1].astype(F32)
+    qkv_sum.relay()
+
+    gni = sum_ni.total(resid[...])
+    dn_sum.share.hop()
     stream = x[...].astype(F32)
     scale = lax.rsqrt(jnp.mean(stream * stream, axis=-1, keepdims=True) + EPSILON)
     unit = stream * scale
@@ -711,12 +874,9 @@
 
     for j in range(1, ns):
         small_seq(j).start()
+    gate_sum.share.hop()
     up_sum.total()
-    for j in range(1, ns):
-        out_copy(j).wait_recv()
-    acc = oown[...]
-    for j in range(1, ns):
-        acc = acc + xall[pl.ds((j - 1) * T, T), :].astype(F32)
+    acc = sum_outputs.total(oown[...])
     last = pl.ds((ns - 1) * T, T)
     xall[last, :] = acc.astype(BF16)
     out_store = pltpu.make_async_copy(xall.at[last], outputs, loc.at[1])
@@ -731,6 +891,9 @@
         small_dp(j).start()
     out_sum.total()
     qkv_sum.total()
+    up_sum.share.hop()
+    out_sum.share.hop()
+    qkv_sum.share.hop()
     for j in range(1, nd):
         small_dp(j).wait_recv()
     for j in range(1, nd):
@@ -743,14 +906,14 @@
     qk_copy.wait_send()
     for j in range(1, ns):
         gout_copy(j).wait_send()
-        out_copy(j).wait_send()
-        ni_copy(j).wait_send()
         small_seq(j).wait_send()
     for j in range(1, nd):
         small_dp(j).wait_send()
     for rb in range(ns):
         pl.when(s != rb)(mixed_out(rb).wait_send)
-    for c in x_copies + g_copies + c_copies + [dn_copy]:
+    for t in (sum_outputs, sum_ni):
+        t.drain()
+    for c in g_copies + [dn_copy]:
         c.wait_send()
     for t in (take_qkv, take_out):
         t.drain()
@@ -786,29 +949,30 @@
         vm((L, width), BF16), vm((qw + kw, L), F32), vm((qw, L), BF16), vm((kw, L), BF16),
         vm((hk, L, HD), BF16), vm((hk, L, HD), BF16), vm((hq, 1, L), F32), vm((ns, qw, T), BF16),
         vm((H * HD, T), BF16), vm((H * HD, width), BF16), vm((width, pw), BF16), vm((8, width), F32),
-        vm((ns - 1, T, width), BF16), vm((T, width), F32), vm((8, width), F32),
+        vm(((ns - 1) * T, width), BF16), vm((T, width), F32), vm((8, width), F32),
         vm((kw, L), BF16), vm((T, width), F32), vm((L, width), BF16), vm((L, width), BF16), vm((8, 128), F32),
         vm((nd, 8, 128), F32), vm((R, pw), BF16), vm((R, n2), BF16), vm((nd * R, n2), BF16), vm((n, width), BF16),
-        vm((T, n), BF16), vm((n, L), BF16), vm((L, n2), BF16), vm((ns - 1, T, width), BF16),
-        vm((ns - 1, T, width), BF16), vm((T, width), F32), vm((2, nz * R, L), BF16),
+        vm((T, n), BF16), vm((n, L), BF16), vm((L, n2), BF16), vm(((ns - 1) * T, width), BF16),
+        vm(((ns - 1) * T, width), BF16), vm((T, width), F32), vm((2, nz * R, L), BF16),
         vm((nz * R, n), BF16), vm((nz * R, n), BF16), vm((nz * piece, width), BF16),
-        vm((nz - 1, R, n), BF16), vm((R, n), BF16), vm((nz - 1, R, n), BF16), vm((R, n), BF16),
-        vm((nz - 1, piece, width), BF16), vm((piece, width), BF16), vm((ns, T, qw), BF16), vm((L, qw), BF16),
+        vm((nz, R, n), BF16), vm((R, n), BF16), vm((nz, R, n), BF16), vm((R, n), BF16),
+        vm((nz, piece, width), BF16), vm((piece, width), BF16), vm((ns, T, qw), BF16), vm((L, qw), BF16),
         vm((hk, L, qw // hk), BF16), vm((hk, L, HD), F32), vm((hk, L, HD), F32), vm((qw, L), F32),
-        vm((nz * R, pw), BF16), vm((nz * R, pw), BF16), vm((nz - 1, R, pw), BF16), vm((R, pw), BF16),
+        vm((nz * R, pw), BF16), vm((nz * R, pw), BF16), vm((nz, R, pw), BF16), vm((R, pw), BF16),
         vm((nz * R, width), BF16), vm((ns - 1, nz * R, cw), BF16), vm((nz * R, cw), BF16),
-        vm((nz - 1, R, cw), BF16), vm((R, cw), BF16),
+        vm((nz, R, cw), BF16), vm((R, cw), BF16),
         vm((8, width), F32), vm((ns - 1, 8, width), F32), vm((8, width), F32), vm((nd - 1, 8, width), F32),
     ]
-    sems = [DMA((ns,)), DMA((ns,)), DMA((nd,)), DMA((nd,))] + [DMA((ns,))] * 8 + [DMA((3,)), DMA((3,))]
+    sems = seq_sems(ns) + [DMA((nd,)), DMA((nd,))] + seq_sems(ns) + [DMA((ns,))] * 2 + seq_sems(ns) * 2
+    sems += [DMA((3,)), DMA((3,))]
     sems += [DMA((3,)), DMA((2, 8))]
-    sems += [DMA((ns,))] * 6 + [DMA((2,)), DMA((2,))] + [DMA((ns,))] * 4 + [DMA((nd,)), DMA((nd,))]
+    sems += seq_sems(ns) + [DMA((ns,))] * 2 + seq_sems(ns) + [DMA((2,)), DMA((2,))] + [DMA((ns,))] * 4 + [DMA((nd,)), DMA((nd,))]
     return pl.pallas_call(
         functools.partial(block_kernel, ns, nd),
         out_shape=outs,
         in_specs=vmem(5) + [hbm] * 5 + vmem(2),
         out_specs=[hbm] * 7 + vmem(1),
-        scratch_shapes=scratch + sems + gather_sems(nz) * 4 + scatter_sems(ns, nz) * 5,
+        scratch_shapes=scratch + sems + gather_sems(nz) * 4 + scatter_sems(ns, nz) * 5 + gather_sems(nz),
         compiler_params=pltpu.CompilerParams(
             collective_id=0, has_side_effects=True, vmem_limit_bytes=VMEM_LIMIT
         ),
@@ -816,7 +980,21 @@
     )(x, gain1, gain2, gainqk, w_qkv, w_out, cot, w_gate, w_up, w_down, cos, sin)
 
 
-def finish_kernel(ns, nd, piece, gateall, upall, qkvall, outall, dnall, gate, up, qkv, out, down):
+def finish_kernel(
+    ns, nd, piece, gateall, upall, qkvall, outall, dnall, got, stream, sums,
+    gate, up, qkv, out, down, outputs, gstream, first, second, qk,
+):
+    outputs[...] = got[...]
+    gstream[...] = stream[...]
+    d = lax.axis_index("dp")
+    for k in range(nd):
+
+        @pl.when(d == k)
+        def _():
+            for i, ref in enumerate((first, second, qk)):
+                w = ref.shape[1]
+                ref[...] = sums[i : i + 1, k * w : (k + 1) * w]
+
     hq, hk = H // ns, KV // ns
     qw, kw = hq * HD, hk * HD
     pad = gateall.shape[2] // nd
@@ -833,27 +1011,33 @@
     down[...] = jnp.concatenate([dnall[i].astype(F32)[:piece] for i in range(dnall.shape[0])], axis=0)
 
 
-def finish(ns, nd, piece, gateall, upall, qkvall, outall, dnall):
+def finish(ns, nd, piece, gateall, upall, qkvall, outall, dnall, got, stream, sums):
     R = gateall.shape[1]
+    T, width = got.shape
     steps = 4
     rows = R // steps
     ff = ns * nd * piece
-    width = dnall.shape[2]
     widths = (ff, ff, ns * qkvall.shape[2], ns * outall.shape[2])
     many = ns // steps
+    lines = (R, R, 2 * HD // nd)
     ins = [pl.BlockSpec((ns, rows, a.shape[2]), lambda i: (0, i, 0)) for a in (gateall, upall, qkvall, outall)]
     ins.append(pl.BlockSpec((many,) + dnall.shape[1:], lambda i: (i, 0, 0)))
+    tokens = pl.BlockSpec((T // steps, width), lambda i: (i, 0))
+    ins += [tokens, tokens, pl.BlockSpec((8, width), lambda i: (0, 0))]
     outs = [pl.BlockSpec((rows, w), lambda i: (i, 0)) for w in widths]
-    outs.append(pl.BlockSpec((many * piece, width), lambda i: (i, 0)))
+    outs += [pl.BlockSpec((many * piece, width), lambda i: (i, 0)), tokens, tokens]
+    outs += [pl.BlockSpec((1, w), lambda i: (0, 0)) for w in lines]
+    sh = jax.ShapeDtypeStruct
     return pl.pallas_call(
         functools.partial(finish_kernel, ns, nd, piece),
         grid=(steps,),
-        out_shape=[jax.ShapeDtypeStruct((R, w), F32) for w in widths]
-        + [jax.ShapeDtypeStruct((ns * piece, width), F32)],
+        out_shape=[sh((R, w), F32) for w in widths]
+        + [sh((ns * piece, width), F32), sh((T, width), BF16), sh((T, width), F32)]
+        + [sh((1, w), F32) for w in lines],
         in_specs=ins,
         out_specs=outs,
-        compiler_params=pltpu.CompilerParams(vmem_limit_bytes=40 << 20),
-    )(gateall, upall, qkvall, outall, dnall)
+        compiler_params=pltpu.CompilerParams(vmem_limit_bytes=VMEM_LIMIT),
+    )(gateall, upall, qkvall, outall, dnall, got, stream, sums)
 
 
 def shards(inputs, cotangent, first_gain, w_qkv, qk_gain, w_out, second_gain, w_gate, w_up, w_down):
@@ -869,12 +1053,10 @@
         ns, nd, piece + pad, x, first_gain[None], second_gain[None], qk_gain[None], w_qkv, w_out, cotangent[0],
         w_gate, w_up, down_rows,
     )
-    gate, up, qkv, out, down = finish(ns, nd, piece, gateall, upall, qkvall, outall, dnall)
-    gl, ql = first_gain.shape[0], qk_gain.shape[0]
-    first = lax.dynamic_slice(small, (0, d * gl), (1, gl))[0]
-    second = lax.dynamic_slice(small, (1, d * gl), (1, gl))[0]
-    qk = lax.dynamic_slice(small, (2, d * ql), (1, ql))[0]
-    return (outputs[None], gstream[None], first, qkv, qk, out, second, gate, up, down)
+    gate, up, qkv, out, down, outputs, gstream, first, second, qk = finish(
+        ns, nd, piece, gateall, upall, qkvall, outall, dnall, outputs, gstream, small
+    )
+    return (outputs[None], gstream[None], first[0], qkv, qk[0], out, second[0], gate, up, down)
 
 
 def solution(mesh):

time: 287 us -> 243 us (0.85); the launches traced: 286 us -> 238 us
  Pallas kernels: 275 us -> 237 us
  local copies, waits for them, and re-layouts: 10.8 us -> 0 us
    pallas_call x1, Pallas kernels: 271 us -> 230 us  [block(): pl.pallas_call(functools.partial(block_kernel, ns, nd), out_shape=outs, i...]
    unnamed x16 -> x0, local copies, waits for them, and re-layouts: 8.18 us -> none
    pallas_call x1, Pallas kernels: 4 us -> 7.19 us  [finish(): pl.pallas_call(functools.partial(finish_kernel, ns, nd, piece), grid=(ste...]
where the time goes in v5:
time: 243 us; the launch traced here: 238 us
  Pallas kernels  237 us (98%)
    pallas_call x1, Pallas kernels, block(): pl.pallas_call(functools.partial(block_kernel, ns, nd), out_shape=outs, i...  230 us
    pallas_call x1, Pallas kernels, finish(): pl.pallas_call(functools.partial(finish_kernel, ns, nd, piece), grid=(ste...  7.19 us

profile of v5, /device:TPU:30, one launch (start us, length us, event | category | flops | bytes accessed | tf_op | source)
XLA Modules:
  0.0 238.1 jit_solution(16535242316562477991)
XLA Ops:
  0.6 230.0 %shard_map.195 = (bf16[256,1024]{1,0:T(8,128)(2,1)}, f32[256,1024]{1,0:T(8,128)}, bf16[4,128,1152]{2,1,0:T(8,128)(2,1)}, bf16[4,128,1152]{2,1,0:T(8,128)(2,1)}, ...) custom-call(bf16[256,1024]{1,0:T(8,128)(2,1)} %bitcast.11, ...), custom_call_target="tpu_custom_call" | custom-call | flops 38000001024 | bytes 40000000 | tf_op jit(solution)/shard_map/pallas_call | solution.py:970
  230.7 7.2 %shard_map.196 = (f32[128,4608]{1,0:T(8,128)}, f32[128,4608]{1,0:T(8,128)}, f32[128,2048]{1,0:T(8,128)}, f32[128,1024]{1,0:T(8,128)}, f32[576,1024]{1,0:T(8,128)...) custom-call(bf16[4,128,1152]{2,1,0:T(8,128)(2,1)} %get-tuple-element, ...), custom_call_target="tpu_custom_call" | custom-call | tf_op jit(solution)/shard_map/pallas_call | solution.py:1031
